TPU v7x, 512 devices: a whole 4x8x8 slice. The times are simulated.
512 devices in a mesh: tests: 16 (over z, y_hi), grid: 32 (over x, y_lo, core).
Axes of the slice: x: 4, y: 8 (y_hi: 2, y_lo: 4; y = y_hi * 4 + y_lo), z: 8, core: 2. Of those that a mesh axis runs over, the one named last changes fastest.
Arguments:
- log_cond: float32 [64, 128, 128], P('grid'), may hold values from -0.7 to 0.7
- opening_increase: float32 [16, 64, 128, 128], P('tests', 'grid'), may hold values from -6 to 6
- heat_load: float32 [16, 64, 128, 128], P('tests', 'grid'), may hold values from -6 to 6
- measured: float32 [16, 128], P('tests', 'grid'), may hold values from -12 to 12
- duct_cells: int32 [8192, 8], P('grid'), may hold values from 0 to 32767
- duct_segment: int32 [8192, 1], P('grid'), may hold values from 0 to 127; in each aligned block of 256 rows (0 to 255, 256 to 511, ...) at most 4 rows name the same one
Outputs:
- theta_grad: float32 [64, 128, 128], P('grid', 'tests')
- seg_residual: float32 [16, 128], P('tests', 'grid')
Inputs may be any that keep to these rules, and one draw needn't show every extreme that they name: `duct_cells`: row r is a flat index (first dimension slowest) into the 2 x 128 x 128 cells of slab r // 256. `duct_segment`: in each aligned block of 256 rows (the ducts of one slab) no segment is named more than 4 times, a bound that some block reaches.
All inputs are finite; a program needn't handle non-finite values.
Results may differ from a plain program's by a relative error of at most 0.000022.
Values sent between devices are 32-bit elements; how exact they have to be, the bound alone decides.
No kernel may reach another device: no remote copies, remote signals or barrier semaphores. Data moves between devices by JAX's collectives and lax.ppermute only.
A program may use at most 64 MiB of HBM per device.

v0:
```python
import jax
import jax.numpy as jnp
from jax import lax
from jax.sharding import PartitionSpec as P

STEPS = 4


timelapse_width = 0.08
boundary_factor = 0.5
axis_weights = (1.0, 1.0, 1.0, 1.0, 0.5, 0.5)


def padded(shard, sides, width):
    for axis, dim in sides:
        size, length = (lax.axis_size(axis), shard.shape[dim])
        up = [(i, (i + 1) % size) for i in range(size - 1)]
        down = [(j, i) for i, j in up]
        last = lax.slice_in_dim(shard, length - width, length, axis=dim)
        leading = lax.slice_in_dim(shard, 0, width, axis=dim)
        before = lax.ppermute(last, axis, up)
        after = lax.ppermute(leading, axis, down)
        shard = jnp.concatenate([before, shard, after], axis=dim)
    return shard


def ahead(values, mesh_axis):
    length = values.shape[mesh_axis]
    zero_shape = list(values.shape)
    zero_shape[mesh_axis] = 1
    return jnp.concatenate(
        [lax.slice_in_dim(values, 1, length, axis=mesh_axis), jnp.zeros(zero_shape, values.dtype)],
        mesh_axis,
    )


def behind(values, mesh_axis):
    length = values.shape[mesh_axis]
    zero_shape = list(values.shape)
    zero_shape[mesh_axis] = 1
    return jnp.concatenate(
        [
            jnp.zeros(zero_shape, values.dtype),
            lax.slice_in_dim(values, 0, length - 1, axis=mesh_axis),
        ],
        mesh_axis,
    )


def adjacent_entries(extended_profile):
    middle_entry = extended_profile[1:-1]
    remaining_entries = [
        extended_profile[2:],
        extended_profile[:-2],
        ahead(middle_entry, 1),
        behind(middle_entry, 1),
        ahead(middle_entry, 2),
        behind(middle_entry, 2),
    ]
    return (middle_entry, remaining_entries)


def framed_profile(values):
    return padded(values, (("grid", 0),), 1)


def apply_operator(extended_profile, cond_others, thermal_permeance):
    middle_entry, remaining_entries = adjacent_entries(extended_profile)
    accumulated_amount = jnp.zeros_like(middle_entry)
    for weight, other, other_cond in zip(axis_weights, remaining_entries, cond_others):
        accumulated_amount = accumulated_amount + weight * 0.5 * (
            thermal_permeance + other_cond
        ) * (other - middle_entry)
    return accumulated_amount


def local(log_cond, opening_increase, heat_load, measured, duct_cells, duct_segment):
    thermal_permeance = jnp.exp(log_cond)
    thermal_profile = opening_increase[0]
    power_injection = heat_load[0]
    slabs = lax.axis_size("grid")
    stored = []
    unused, cond_others = adjacent_entries(framed_profile(thermal_permeance))
    for sweep in range(STEPS):
        extended_profile = framed_profile(thermal_profile)
        stored.append(extended_profile)
        thermal_profile = thermal_profile + timelapse_width * (
            apply_operator(extended_profile, cond_others, thermal_permeance) + power_injection
        )
    linear_entries = thermal_profile.reshape(-1)
    segment_ids = duct_segment[:, 0]
    interim_outcome = boundary_factor * jnp.sum(linear_entries[duct_cells], axis=1)
    seg_local = measured.shape[1]
    seg_count = slabs * seg_local
    duct_count = duct_cells.shape[0]
    capacity = 2 * duct_count // seg_count
    ident = jnp.arange(duct_count, dtype=jnp.int32)
    matches = (segment_ids[:, None] == segment_ids[None, :]) & (ident[None, :] < ident[:, None])
    position = jnp.sum(matches.astype(jnp.int32), axis=1)
    buffer = (
        jnp.zeros((seg_count * capacity,), jnp.float32)
        .at[segment_ids * capacity + position]
        .add(interim_outcome)
    )
    buffer = buffer.reshape(slabs, seg_local * capacity)
    received = lax.all_to_all(buffer, "grid", split_axis=0, concat_axis=0, tiled=True)
    totals = jnp.sum(received.reshape(slabs, seg_local, capacity), axis=(0, 2))
    resid = totals - measured[0]
    all_resid = lax.all_gather(resid, "grid", axis=0, tiled=True)
    sources = jnp.repeat(boundary_factor * all_resid[segment_ids], duct_cells.shape[1])
    costate_profile = (
        jnp.zeros(linear_entries.shape, jnp.float32).at[duct_cells.reshape(-1)].add(sources)
    )
    costate_profile = costate_profile.reshape(thermal_profile.shape)
    permeance_sensitivity = jnp.zeros_like(thermal_profile)
    for sweep in range(STEPS - 1, -1, -1):
        middle_entry, temp_others = adjacent_entries(stored[sweep])
        adjoint_pad = framed_profile(costate_profile)
        unused_center, adjoint_others = adjacent_entries(adjoint_pad)
        for weight, temp_other, adjoint_other in zip(axis_weights, temp_others, adjoint_others):
            permeance_sensitivity = permeance_sensitivity + weight * 0.5 * (
                costate_profile - adjoint_other
            ) * (middle_entry - temp_other)
        costate_profile = costate_profile + timelapse_width * apply_operator(
            adjoint_pad, cond_others, thermal_permeance
        )
    grad_theta = -timelapse_width * thermal_permeance * permeance_sensitivity
    accumulated_amount = lax.psum(grad_theta, "tests")
    share_rows = accumulated_amount.shape[1] // lax.axis_size("tests")
    result = lax.dynamic_slice_in_dim(
        accumulated_amount, lax.axis_index("tests") * share_rows, share_rows, 1
    )
    return (result, resid[None])


def solution(mesh):
    in_specs = (
        P("grid", None, None),
        P("tests", "grid", None, None),
        P("tests", "grid", None, None),
        P("tests", "grid"),
        P("grid", None),
        P("grid", None),
    )
    out_specs = (P("grid", "tests", None), P("tests", "grid"))
    return jax.shard_map(local, mesh=mesh, in_specs=in_specs, out_specs=out_specs, check_vma=False)
```

profile of v0, /device:TPU:2, one launch (start us, length us, event | category | flops | bytes accessed | tf_op | source)
XLA Modules:
  0.0 414.4 jit_solution(10981032482643247199)
XLA Ops:
  10.2 6.3 %collective-permute-start = (f32[1,128,128]{2,1,0:T(8,128)S(1)}, f32[1,128,128]{2,1,0:T(8,128)S(1)}, u32[]{:S(2)}, u32[]{:S(2)}) collective-permute-start(f32[1,128,128]{2,1,0:T(8,128)S(1)} %get-tuple-element.52), channel_id=1, source_target_pairs={{1,0},{2,1},{3,2},{4,3},{5,4},{6,5},{7,6},{8,7},{9,8},{10,9},{11,1... | collective-permute-start | bytes 196616 | tf_op jit(solution)/shard_map/ppermute | solution.py:22
  18.5 2.4 collective-permute-start.3
  23.2 3.6 collective-permute-done.3
  27.5 2.3 collective-permute-start.4
  31.9 6.6 %collective-permute-done.5 = f32[1,128,128]{2,1,0:T(8,128)S(1)} collective-permute-done((f32[1,128,128]{2,1,0:T(8,128)S(1)}, f32[1,128,128]{2,1,0:T(8,128)S(1)}, u32[]{:S(2)}, u32[]{:S(2)}) %collective-permute-start.5) | collective-permute-done | bytes 65568 | tf_op jit(solution)/shard_map/ppermute | solution.py:21
  41.2 2.4 collective-permute-start.7
  43.6 5.8 %collective-permute-done.7 = f32[1,128,128]{2,1,0:T(8,128)S(1)} collective-permute-done((f32[1,128,128]{2,1,0:T(8,128)S(1)}, f32[1,128,128]{2,1,0:T(8,128)S(1)}, u32[]{:S(2)}, u32[]{:S(2)}) %collective-permute-start.7) | collective-permute-done | bytes 65568 | tf_op jit(solution)/shard_map/ppermute | solution.py:21
  52.1 2.4 collective-permute-start.9
  54.6 5.8 %collective-permute-done.9 = f32[1,128,128]{2,1,0:T(8,128)S(1)} collective-permute-done((f32[1,128,128]{2,1,0:T(8,128)S(1)}, f32[1,128,128]{2,1,0:T(8,128)S(1)}, u32[]{:S(2)}, u32[]{:S(2)}) %collective-permute-start.9) | collective-permute-done | bytes 65568 | tf_op jit(solution)/shard_map/ppermute | solution.py:21
  61.0 11.8 %gather_fusion = f32[2048]{0:T(1024)S(1)} fusion(f32[32768]{0:T(1024)S(1)} %bitcast.29, s32[2048]{0:T(1024)S(1)} %broadcast_clamp_fusion), kind=kCustom, calls=%fused_computation | custom fusion | bytes 24576 | tf_op jit(solution)/shard_map/gather | solution.py:92
  73.0 2.5 scatter_custom_fusion
  76.2 5.0 %all-to-all-start = ((f32[32,1,16]{2,1,0:T(1,128)}), f32[32,1,16]{2,1,0:T(1,128)S(1)}, u32[]{:S(2)}, u32[]{:S(2)}) async-start(f32[32,1,16]{2,1,0:T(1,128)} %bitcast.9), calls=%async_computation | async-start | bytes 32768 | tf_op jit(solution)/shard_map/all_to_all | solution.py:106
  83.8 3.9 all-to-all-done
  88.7 58.5 %all-reduce.36 = f32[128]{0:T(128)S(1)} all-reduce(f32[128]{0:T(128)S(1)} %fusion.146), channel_id=1, replica_groups=mesh['tests'=16,'grid'=32] {'grid'}, use_global_device_ids=true, to_apply=%add.36 | all-reduce | flops 128 | bytes 1024
  149.3 11.3 %scatter_custom_fusion.1 = f32[32768]{0:T(1024)S(1)} fusion(s32[2048]{0:T(1024)S(1)} %bitcast.39, f32[2048]{0:T(1024)S(1)} %reshape.105, f32[]{:T(128)} %constant.14.clone.1), kind=kCustom, calls=%fused_computation.174 | custom fusion | flops 2048 | bytes 131076 | tf_op jit(solution)/shard_map/scatter-add | solution.py:112
  162.6 2.4 collective-permute-start.11
  165.1 5.8 %collective-permute-done.11 = f32[1,128,128]{2,1,0:T(8,128)S(1)} collective-permute-done((f32[1,128,128]{2,1,0:T(8,128)S(1)}, f32[1,128,128]{2,1,0:T(8,128)S(1)}, u32[]{:S(2)}, u32[]{:S(2)}) %collective-permute-start.11) | collective-permute-done | bytes 65568 | tf_op jit(solution)/shard_map/ppermute | solution.py:21
  173.1 2.4 collective-permute-start.13
  175.5 5.8 %collective-permute-done.13 = f32[1,128,128]{2,1,0:T(8,128)S(1)} collective-permute-done((f32[1,128,128]{2,1,0:T(8,128)S(1)}, f32[1,128,128]{2,1,0:T(8,128)S(1)}, u32[]{:S(2)}, u32[]{:S(2)}) %collective-permute-start.13) | collective-permute-done | bytes 65568 | tf_op jit(solution)/shard_map/ppermute | solution.py:21
  183.5 2.4 collective-permute-start.15
  186.0 6.0 %collective-permute-done.15 = f32[1,128,128]{2,1,0:T(8,128)S(1)} collective-permute-done((f32[1,128,128]{2,1,0:T(8,128)S(1)}, f32[1,128,128]{2,1,0:T(8,128)S(1)}, u32[]{:S(2)}, u32[]{:S(2)}) %collective-permute-start.15) | collective-permute-done | bytes 65568 | tf_op jit(solution)/shard_map/ppermute | solution.py:21
  194.2 2.5 collective-permute-start.17
  196.8 5.8 %collective-permute-done.17 = f32[1,128,128]{2,1,0:T(8,128)S(1)} collective-permute-done((f32[1,128,128]{2,1,0:T(8,128)S(1)}, f32[1,128,128]{2,1,0:T(8,128)S(1)}, u32[]{:S(2)}, u32[]{:S(2)}) %collective-permute-start.17) | collective-permute-done | bytes 65568 | tf_op jit(solution)/shard_map/ppermute | solution.py:21
  204.8 201.5 %all-reduce.39.cloned.1.call-done = f32[2,128,128]{2,1,0:T(8,128)} async-done(((f32[2,128,128]{2,1,0:T(8,128)}), f32[2,128,128]{2,1,0:T(8,128)}) %all-reduce.39.cloned.1.call-update) | async-done | bytes 131088 | tf_op jit(solution)/shard_map/psum | solution.py:128
  (135 shorter events, 33.7 us)
Async XLA Ops:
  8.1 15.0 %collective-permute-start.2 = (f32[1,128,128]{2,1,0:T(8,128)S(1)}, f32[1,128,128]{2,1,0:T(8,128)S(1)}, u32[]{:S(2)}, u32[]{:S(2)}) collective-permute-start(f32[1,128,128]{2,1,0:T(8,128)S(1)} %get-tuple-element.51), channel_id=1, source_target_pairs={{0,1},{1,2},{2,3},{3,4},{4,5},{5,6},{6,7},{7,8},{8,9},{9,10},{10,1... | collective-permute-start | bytes 196616 | tf_op jit(solution)/shard_map/ppermute | solution.py:21
  10.2 13.0 %collective-permute-start = (f32[1,128,128]{2,1,0:T(8,128)S(1)}, f32[1,128,128]{2,1,0:T(8,128)S(1)}, u32[]{:S(2)}, u32[]{:S(2)}) collective-permute-start(f32[1,128,128]{2,1,0:T(8,128)S(1)} %get-tuple-element.52), channel_id=1, source_target_pairs={{1,0},{2,1},{3,2},{4,3},{5,4},{6,5},{7,6},{8,7},{9,8},{10,9},{11,1... | collective-permute-start | bytes 196616 | tf_op jit(solution)/shard_map/ppermute | solution.py:22
  16.6 6.6 %collective-permute-start.1 = (f32[1,128,128]{2,1,0:T(8,128)S(1)}, f32[1,128,128]{2,1,0:T(8,128)S(1)}, u32[]{:S(2)}, u32[]{:S(2)}) collective-permute-start(f32[1,128,128]{2,1,0:T(8,128)S(1)} %get-tuple-element.61), channel_id=1, source_target_pairs={{1,0},{2,1},{3,2},{4,3},{5,4},{6,5},{7,6},{8,7},{9,8},{10,9},{11,1... | collective-permute-start | bytes 196616 | tf_op jit(solution)/shard_map/ppermute | solution.py:22
  18.5 8.3 %collective-permute-start.3 = (f32[1,128,128]{2,1,0:T(8,128)S(1)}, f32[1,128,128]{2,1,0:T(8,128)S(1)}, u32[]{:S(2)}, u32[]{:S(2)}) collective-permute-start(f32[1,128,128]{2,1,0:T(8,128)S(1)} %get-tuple-element.62), channel_id=1, source_target_pairs={{0,1},{1,2},{2,3},{3,4},{4,5},{5,6},{6,7},{7,8},{8,9},{9,10},{10,1... | collective-permute-start | bytes 196616 | tf_op jit(solution)/shard_map/ppermute | solution.py:21
  27.5 4.4 %collective-permute-start.4 = (f32[1,128,128]{2,1,0:T(8,128)S(1)}, f32[1,128,128]{2,1,0:T(8,128)S(1)}, u32[]{:S(2)}, u32[]{:S(2)}) collective-permute-start(f32[1,128,128]{2,1,0:T(8,128)S(1)} %get-tuple-element.49), channel_id=1, source_target_pairs={{1,0},{2,1},{3,2},{4,3},{5,4},{6,5},{7,6},{8,7},{9,8},{10,9},{11,1... | collective-permute-start | bytes 196616 | tf_op jit(solution)/shard_map/ppermute | solution.py:22
  29.8 8.7 %collective-permute-start.5 = (f32[1,128,128]{2,1,0:T(8,128)S(1)}, f32[1,128,128]{2,1,0:T(8,128)S(1)}, u32[]{:S(2)}, u32[]{:S(2)}) collective-permute-start(f32[1,128,128]{2,1,0:T(8,128)S(1)} %get-tuple-element.50), channel_id=1, source_target_pairs={{0,1},{1,2},{2,3},{3,4},{4,5},{5,6},{6,7},{7,8},{8,9},{9,10},{10,1... | collective-permute-start | bytes 196616 | tf_op jit(solution)/shard_map/ppermute | solution.py:21
  39.2 4.4 %collective-permute-start.6 = (f32[1,128,128]{2,1,0:T(8,128)S(1)}, f32[1,128,128]{2,1,0:T(8,128)S(1)}, u32[]{:S(2)}, u32[]{:S(2)}) collective-permute-start(f32[1,128,128]{2,1,0:T(8,128)S(1)} %get-tuple-element.43), channel_id=1, source_target_pairs={{1,0},{2,1},{3,2},{4,3},{5,4},{6,5},{7,6},{8,7},{9,8},{10,9},{11,1... | collective-permute-start | bytes 196616 | tf_op jit(solution)/shard_map/ppermute | solution.py:22
  41.2 8.3 %collective-permute-start.7 = (f32[1,128,128]{2,1,0:T(8,128)S(1)}, f32[1,128,128]{2,1,0:T(8,128)S(1)}, u32[]{:S(2)}, u32[]{:S(2)}) collective-permute-start(f32[1,128,128]{2,1,0:T(8,128)S(1)} %get-tuple-element.44), channel_id=1, source_target_pairs={{0,1},{1,2},{2,3},{3,4},{4,5},{5,6},{6,7},{7,8},{8,9},{9,10},{10,1... | collective-permute-start | bytes 196616 | tf_op jit(solution)/shard_map/ppermute | solution.py:21
  50.2 4.4 %collective-permute-start.8 = (f32[1,128,128]{2,1,0:T(8,128)S(1)}, f32[1,128,128]{2,1,0:T(8,128)S(1)}, u32[]{:S(2)}, u32[]{:S(2)}) collective-permute-start(f32[1,128,128]{2,1,0:T(8,128)S(1)} %get-tuple-element.37), channel_id=1, source_target_pairs={{1,0},{2,1},{3,2},{4,3},{5,4},{6,5},{7,6},{8,7},{9,8},{10,9},{11,1... | collective-permute-start | bytes 196616 | tf_op jit(solution)/shard_map/ppermute | solution.py:22
  52.1 8.3 %collective-permute-start.9 = (f32[1,128,128]{2,1,0:T(8,128)S(1)}, f32[1,128,128]{2,1,0:T(8,128)S(1)}, u32[]{:S(2)}, u32[]{:S(2)}) collective-permute-start(f32[1,128,128]{2,1,0:T(8,128)S(1)} %get-tuple-element.38), channel_id=1, source_target_pairs={{0,1},{1,2},{2,3},{3,4},{4,5},{5,6},{6,7},{7,8},{8,9},{9,10},{10,1... | collective-permute-start | bytes 196616 | tf_op jit(solution)/shard_map/ppermute | solution.py:21
  76.2 11.5 %all-to-all-start = ((f32[32,1,16]{2,1,0:T(1,128)}), f32[32,1,16]{2,1,0:T(1,128)S(1)}, u32[]{:S(2)}, u32[]{:S(2)}) async-start(f32[32,1,16]{2,1,0:T(1,128)} %bitcast.9), calls=%async_computation | async-start | bytes 32768 | tf_op jit(solution)/shard_map/all_to_all | solution.py:106
  81.2 325.1 %all-reduce.39.cloned.1.call-start = ((), (), s32[]{:S(2)}) async-start(), calls=%async_computation.1 | async-start | bytes 262144 | tf_op jit(solution)/shard_map/psum | solution.py:128
  160.7 4.5 %collective-permute-start.10 = (f32[1,128,128]{2,1,0:T(8,128)S(1)}, f32[1,128,128]{2,1,0:T(8,128)S(1)}, u32[]{:S(2)}, u32[]{:S(2)}) collective-permute-start(f32[1,128,128]{2,1,0:T(8,128)S(1)} %get-tuple-element.31), channel_id=1, source_target_pairs={{1,0},{2,1},{3,2},{4,3},{5,4},{6,5},{7,6},{8,7},{9,8},{10,9},{11,1... | collective-permute-start | bytes 196616 | tf_op jit(solution)/shard_map/ppermute | solution.py:22
  162.6 8.3 %collective-permute-start.11 = (f32[1,128,128]{2,1,0:T(8,128)S(1)}, f32[1,128,128]{2,1,0:T(8,128)S(1)}, u32[]{:S(2)}, u32[]{:S(2)}) collective-permute-start(f32[1,128,128]{2,1,0:T(8,128)S(1)} %get-tuple-element.32), channel_id=1, source_target_pairs={{0,1},{1,2},{2,3},{3,4},{4,5},{5,6},{6,7},{7,8},{8,9},{9,10},{10,1... | collective-permute-start | bytes 196616 | tf_op jit(solution)/shard_map/ppermute | solution.py:21
  171.2 4.4 %collective-permute-start.12 = (f32[1,128,128]{2,1,0:T(8,128)S(1)}, f32[1,128,128]{2,1,0:T(8,128)S(1)}, u32[]{:S(2)}, u32[]{:S(2)}) collective-permute-start(f32[1,128,128]{2,1,0:T(8,128)S(1)} %get-tuple-element.25), channel_id=1, source_target_pairs={{1,0},{2,1},{3,2},{4,3},{5,4},{6,5},{7,6},{8,7},{9,8},{10,9},{11,1... | collective-permute-start | bytes 196616 | tf_op jit(solution)/shard_map/ppermute | solution.py:22
  173.1 8.3 %collective-permute-start.13 = (f32[1,128,128]{2,1,0:T(8,128)S(1)}, f32[1,128,128]{2,1,0:T(8,128)S(1)}, u32[]{:S(2)}, u32[]{:S(2)}) collective-permute-start(f32[1,128,128]{2,1,0:T(8,128)S(1)} %get-tuple-element.26), channel_id=1, source_target_pairs={{0,1},{1,2},{2,3},{3,4},{4,5},{5,6},{6,7},{7,8},{8,9},{9,10},{10,1... | collective-permute-start | bytes 196616 | tf_op jit(solution)/shard_map/ppermute | solution.py:21
  181.6 4.4 %collective-permute-start.14 = (f32[1,128,128]{2,1,0:T(8,128)S(1)}, f32[1,128,128]{2,1,0:T(8,128)S(1)}, u32[]{:S(2)}, u32[]{:S(2)}) collective-permute-start(f32[1,128,128]{2,1,0:T(8,128)S(1)} %get-tuple-element.19), channel_id=1, source_target_pairs={{1,0},{2,1},{3,2},{4,3},{5,4},{6,5},{7,6},{8,7},{9,8},{10,9},{11,1... | collective-permute-start | bytes 196616 | tf_op jit(solution)/shard_map/ppermute | solution.py:22
  183.5 8.4 %collective-permute-start.15 = (f32[1,128,128]{2,1,0:T(8,128)S(1)}, f32[1,128,128]{2,1,0:T(8,128)S(1)}, u32[]{:S(2)}, u32[]{:S(2)}) collective-permute-start(f32[1,128,128]{2,1,0:T(8,128)S(1)} %get-tuple-element.20), channel_id=1, source_target_pairs={{0,1},{1,2},{2,3},{3,4},{4,5},{5,6},{6,7},{7,8},{8,9},{9,10},{10,1... | collective-permute-start | bytes 196616 | tf_op jit(solution)/shard_map/ppermute | solution.py:21
  192.0 10.6 %copy-start.16 = (f32[1,128,128]{2,1,0:T(8,128)S(1)}, f32[1,128,128]{2,1,0:T(8,128)}, u32[]{:S(2)}) copy-start(f32[1,128,128]{2,1,0:T(8,128)} %copy-done.15) | copy-start | bytes 196612
  192.0 10.6 %copy-start.18 = (f32[1,128,128]{2,1,0:T(8,128)S(1)}, f32[1,128,128]{2,1,0:T(8,128)}, u32[]{:S(2)}) copy-start(f32[1,128,128]{2,1,0:T(8,128)} %copy-done.17) | copy-start | bytes 196612
  192.0 10.6 %copy-start.20 = (f32[1,128,128]{2,1,0:T(8,128)S(1)}, f32[1,128,128]{2,1,0:T(8,128)}, u32[]{:S(2)}) copy-start(f32[1,128,128]{2,1,0:T(8,128)} %copy-done.19) | copy-start | bytes 196612
  192.0 10.6 %copy-start.22 = (f32[1,128,128]{2,1,0:T(8,128)S(1)}, f32[1,128,128]{2,1,0:T(8,128)}, u32[]{:S(2)}) copy-start(f32[1,128,128]{2,1,0:T(8,128)} %copy-done.21) | copy-start | bytes 196612
  192.2 4.6 %collective-permute-start.16 = (f32[1,128,128]{2,1,0:T(8,128)S(1)}, f32[1,128,128]{2,1,0:T(8,128)S(1)}, u32[]{:S(2)}, u32[]{:S(2)}) collective-permute-start(f32[1,128,128]{2,1,0:T(8,128)S(1)} %get-tuple-element.13), channel_id=1, source_target_pairs={{1,0},{2,1},{3,2},{4,3},{5,4},{6,5},{7,6},{8,7},{9,8},{10,9},{11,1... | collective-permute-start | bytes 196616 | tf_op jit(solution)/shard_map/ppermute | solution.py:22
  194.2 8.4 %collective-permute-start.17 = (f32[1,128,128]{2,1,0:T(8,128)S(1)}, f32[1,128,128]{2,1,0:T(8,128)S(1)}, u32[]{:S(2)}, u32[]{:S(2)}) collective-permute-start(f32[1,128,128]{2,1,0:T(8,128)S(1)} %get-tuple-element.14), channel_id=1, source_target_pairs={{0,1},{1,2},{2,3},{3,4},{4,5},{5,6},{6,7},{7,8},{8,9},{9,10},{10,1... | collective-permute-start | bytes 196616 | tf_op jit(solution)/shard_map/ppermute | solution.py:21
  (23 other events, 110.8 us)
Sparse Core Ops, SparseCore 0:
  204.4 201.8 all-reduce.38
where the time goes:
time: 415 us; the launch traced here: 414 us
  waiting for transfers between devices  251 us (60%)
  blocking collectives  58.5 us (14%)
  starting transfers between devices  48.2 us (12%)
  local copies, waits for them, and re-layouts  23.7 us (6%)
  other arithmetic  17.9 us (4%)
  between operations  15.5 us (4%)
    psum x1, waiting for transfers between devices, local(): accumulated_amount = lax.psum(grad_theta, 'tests')  201 us
    unnamed x1, blocking collectives  58.5 us
    ppermute x9, waiting for transfers between devices, padded(): before = lax.ppermute(last, axis, up)  45.2 us
    ppermute x9, starting transfers between devices, padded(): after = lax.ppermute(leading, axis, down)  22.1 us
    ppermute x9, starting transfers between devices, padded(): before = lax.ppermute(last, axis, up)  21.1 us
    gather x2, local copies, waits for them, and re-layouts, local(): linear_entries[duct_cells]  11.9 us
    scatter-add x1, other arithmetic, local(): jnp.zeros(linear_entries.shape, jnp.float32).at[duct_cells.reshape(-1)]  11.3 us
  transfers between devices with their start and end apart: 20, of which 10 were waited for; matrix products, arithmetic and copies ran while one was open for 1% of the time, Pallas kernels for 0%

commit v1 on v0

v1 whole, which is shorter than its diff:
```python
import functools

import jax
import jax.numpy as jnp
from jax import lax
from jax.experimental import pallas as pl
from jax.experimental.pallas import tpu as pltpu
from jax.sharding import PartitionSpec as P

STEPS = 4
DT = 0.08
WX = 0.5 * DT
WZ = 0.25 * DT
NY = 128
NZ = 128
CELLS = 2 * NY
EXT = 10
PAD = 8
YP = NY + 2 * PAD
MID = slice(PAD, PAD + NY)
CH = 32
PACK = 3 * CELLS + 24
bf16 = jnp.bfloat16
f32 = jnp.float32


def position():
    g = lax.axis_index("grid")
    return g, lax.rem(g, 2), lax.div(g, 2), lax.axis_size("grid") // 2


def validity():
    _, core, chip, chips = position()
    low, high = (chip > 0).astype(f32), (chip < chips - 1).astype(f32)
    near = jnp.where(core == 0, low, high)
    far = jnp.where(core == 0, high, low)
    return near, far


def row_validity(i, near, far):
    return jnp.where(i < 4, near, jnp.where(i < 8, 1.0, far))


def lane_masks(rows):
    lane = lax.broadcasted_iota(jnp.int32, (rows, NZ), 1)
    return lane < NZ - 1, lane > 0


def ahead_z(values, keep):
    return jnp.where(keep, pltpu.roll(values, NZ - 1, 1), 0.0)


def behind_z(values, keep):
    return jnp.where(keep, pltpu.roll(values, 1, 1), 0.0)


def zero_pads(ref, lead):
    ref[lead, 0:PAD] = jnp.zeros((PAD, NZ), f32)
    ref[lead, PAD + NY : YP] = jnp.zeros((PAD, NZ), f32)


def coefficients(cond, kx, ky, kzp, kzm, keep):
    ahead_keep, behind_keep = lane_masks(CH)

    def row(i, carry):
        for y in range(0, NY, CH):
            here = pl.ds(PAD + y, CH)
            c = cond[i, here]
            cxp, cxm = cond[i + 1, here], cond[i - 1, here]
            cyp, cym = cond[i, pl.ds(PAD + y + 1, CH)], cond[i, pl.ds(PAD + y - 1, CH)]
            czp, czm = ahead_z(c, ahead_keep), behind_z(c, behind_keep)
            kx[i, pl.ds(y, CH)] = WX * (c + cxp)
            face_y = WX * (c + cyp)
            if y + CH == NY:
                edge = lax.broadcasted_iota(jnp.int32, (CH, NZ), 0) == CH - 1
                face_y = jnp.where(edge, 0.0, face_y)
            ky[i, here] = face_y
            kzp[i, pl.ds(y, CH)] = jnp.where(ahead_keep, WZ * (c + czp), 0.0)
            kzm[i, pl.ds(y, CH)] = jnp.where(behind_keep, WZ * (c + czm), 0.0)
            total = WX * (((cxp + cxm) + (cyp + cym)) + 4.0 * c) + WZ * ((czp + czm) + 2.0 * c)
            keep[i, pl.ds(y, CH)] = 1.0 - total
        ky[i, 0:PAD] = jnp.zeros((PAD, NZ), f32)
        return carry

    kx[0] = WX * (cond[0, MID] + cond[1, MID])
    lax.fori_loop(1, 9, row, 0)


def advance(src, dst, first, last, coefs, load, near, far):
    kx, ky, kzp, kzm, keep = coefs

    def row(i, carry):
        inside = row_validity(i, near, far)
        for y in range(0, NY, CH):
            here, flat = pl.ds(PAD + y, CH), pl.ds(y, CH)
            u = src[i, here]
            new = keep[i, flat] * u
            new += kx[i, flat] * src[i + 1, here]
            new += kx[i - 1, flat] * src[i - 1, here]
            new += ky[i, here] * src[i, pl.ds(PAD + y + 1, CH)]
            new += ky[i, pl.ds(PAD + y - 1, CH)] * src[i, pl.ds(PAD + y - 1, CH)]
            new += kzp[i, flat] * pltpu.roll(u, NZ - 1, 1)
            new += kzm[i, flat] * pltpu.roll(u, 1, 1)
            if load is not None:
                new += load[i, flat]
            dst[i, here] = new * inside
        return carry

    lax.fori_loop(first, last + 1, row, 0)


def parts_of(values, count):
    parts = []
    for _ in range(count):
        part = values.astype(bf16).astype(f32)
        parts.append(part)
        values = values - part
    return parts


def stacked_rows(parts):
    row = lax.broadcasted_iota(jnp.int32, (16, parts[0].shape[1]), 0)
    out = jnp.zeros(row.shape, f32)
    for number, part in enumerate(parts):
        out = jnp.where(row == number, part, out)
    return out.astype(bf16)


def hot(index, count):
    return lax.broadcasted_iota(jnp.int32, (count, index.shape[1]), 0) == index


def as_bf16(mask):
    return jnp.where(mask, 1.0, 0.0).astype(bf16)


def duct_lists(duct, base, core):
    cells = jnp.concatenate([duct[base : base + 8], duct[base + 8 : base + 16]], axis=1)
    cells = cells.astype(jnp.int32) ^ (core * CELLS // 2 * NZ)
    extra = duct[base + 16 : base + 24]
    segment = jnp.concatenate([extra[0:1], extra[1:2]], axis=1).astype(jnp.int32)
    return cells >> 7, cells & (NZ - 1), segment


def forward_kernel(
    near2, near1, own, far1, far2, measured, kept, sums, temp, load, cond, kx, ky, kzp, kzm, keep
):
    g, core, _, _ = position()
    near, far = validity()
    slabs = (near2, near1, own, far1, far2)
    for j, slab in enumerate(slabs):
        valid = (near, near, 1.0, 1.0, far)[j]
        for r in range(2):
            i = 2 * j + r
            start = pl.multiple_of((r ^ core) * NY, NY)
            temp[0, i, MID] = slab[pl.ds(start, NY)]
            load[i] = DT * slab[pl.ds(CELLS + start, NY)]
            cond[i, MID] = jnp.exp(slab[pl.ds(2 * CELLS + start, NY)]) * valid

    def pads(i, carry):
        zero_pads(cond, i)
        for k in range(STEPS):
            zero_pads(temp.at[k], i)
        return carry

    lax.fori_loop(0, EXT, pads, 0)
    coefficients(cond, kx, ky, kzp, kzm, keep)
    coefs = (kx, ky, kzp, kzm, keep)
    for k in range(STEPS):
        advance(temp.at[k], temp.at[k + 1], k + 1, 8 - k, coefs, load, near, far)

    def save(i, carry):
        for k in range(STEPS):
            kept[k, i] = temp[k, 3 + i]
        return carry

    lax.fori_loop(0, 4, save, 0)

    rows, lanes, segment = duct_lists(own, 3 * CELLS, core)
    across = jnp.concatenate([temp[STEPS, 4, MID].T, temp[STEPS, 5, MID].T], axis=1)
    stack = jnp.concatenate([part.astype(bf16) for part in parts_of(across, 3)], axis=0)
    picked = jnp.zeros((NZ, 256), f32)
    for c in range(8):
        at_row = as_bf16(hot(rows[c : c + 1], CELLS))
        found = jnp.dot(stack, at_row, preferred_element_type=f32)
        value = (found[2 * NZ :] + found[NZ : 2 * NZ]) + found[:NZ]
        picked = picked + jnp.where(hot(lanes[c : c + 1], NZ), value, 0.0)
    partial = 0.5 * jnp.sum(picked, axis=0, keepdims=True)
    by_segment = lax.dot_general(
        stacked_rows(parts_of(partial, 3)),
        as_bf16(hot(segment, 128)),
        (((1,), (1,)), ((), ())),
        preferred_element_type=f32,
    )
    total = jnp.sum(by_segment, axis=0, keepdims=True)
    lane = lax.broadcasted_iota(jnp.int32, (1, 128), 1)
    for n in range(measured.shape[1]):
        mine = lane == measured.shape[1] * g + n
        total = total - jnp.where(mine, measured[0:1, n : n + 1], 0.0)
    sums[...] = jnp.broadcast_to(total, sums.shape)


def backward_kernel(
    near2, near1, own, far1, far2, near2d, near1d, ownd, far1d, far2d, kept, sums,
    grad, seg, costate, cond, kx, ky, kzp, kzm, keep, acc,
):
    g, core, _, _ = position()
    near, far = validity()
    conds = (near2, near1, own, far1, far2)
    ducts = (near2d, near1d, ownd, far1d, far2d)
    resid = jnp.sum(sums[...], axis=0, keepdims=True)
    shift = lax.rem(128 - seg.shape[1] * g, 128)
    seg[...] = pltpu.roll(jnp.broadcast_to(resid, (8, 128)), shift, 1)[0:1, 0 : seg.shape[1]]
    stack = stacked_rows(parts_of(0.5 * resid, 3))
    for j in range(5):
        valid = (near, near, 1.0, 1.0, far)[j]
        for r in range(2):
            start = pl.multiple_of((r ^ core) * NY, NY)
            cond[2 * j + r, MID] = jnp.exp(conds[j][pl.ds(start, NY)]) * valid
        rows, lanes, segment = duct_lists(ducts[j], 0, core)
        source = jnp.dot(stack, as_bf16(hot(segment, 128)), preferred_element_type=f32)
        source = jnp.sum(source, axis=0, keepdims=True) * valid
        upper, lower = parts_of(source, 2)
        out = jnp.zeros((CELLS, 2 * NZ), f32)
        for c in range(8):
            at_row = as_bf16(hot(rows[c : c + 1], CELLS))
            at_lane = hot(lanes[c : c + 1], NZ)
            weight = jnp.concatenate(
                [jnp.where(at_lane, upper, 0.0).astype(bf16), jnp.where(at_lane, lower, 0.0).astype(bf16)],
                axis=0,
            )
            out = out + lax.dot_general(
                at_row, weight, (((1,), (1,)), ((), ())), preferred_element_type=f32
            )
        out = out[:, :NZ] + out[:, NZ:]
        costate[0, 2 * j, MID] = out[:NY]
        costate[0, 2 * j + 1, MID] = out[NY:]

    def pads(i, carry):
        zero_pads(cond, i)
        for k in range(STEPS):
            zero_pads(costate.at[k], i)
        return carry

    lax.fori_loop(0, EXT, pads, 0)
    coefficients(cond, kx, ky, kzp, kzm, keep)
    coefs = (kx, ky, kzp, kzm, keep)
    for k in range(STEPS - 1):
        advance(costate.at[k], costate.at[k + 1], k + 1, 8 - k, coefs, None, near, far)
    ahead_keep, behind_keep = lane_masks(CH)
    share = grad.shape[2]

    def sensitivity(i, carry):
        at = (i - 4) ^ core
        for y in range(0, NY, CH):
            here = pl.ds(PAD + y, CH)
            left, right = pl.ds(PAD + y - 1, CH), pl.ds(PAD + y + 1, CH)
            total = jnp.zeros((CH, NZ), f32)
            for k in range(STEPS):
                u, a = kept.at[k], costate.at[STEPS - 1 - k]
                p = i - 3
                uc, ac = u[p, here], a[i, here]
                total += (uc - u[p + 1, here]) * (ac - a[i + 1, here])
                total += (uc - u[p - 1, here]) * (ac - a[i - 1, here])
                total += (uc - u[p, right]) * (ac - a[i, right])
                total += (uc - u[p, left]) * (ac - a[i, left])
                side = (uc - ahead_z(uc, ahead_keep)) * (ac - ahead_z(ac, ahead_keep))
                side += (uc - behind_z(uc, behind_keep)) * (ac - behind_z(ac, behind_keep))
                total += 0.5 * side
            acc[pl.ds(y, CH)] = (-WX) * cond[i, here] * total
        for n in range(NY // share):
            grad[n, at] = acc[pl.ds(n * share, share)]
        return carry

    lax.fori_loop(4, 6, sensitivity, 0)


def field(*lead, pad=True):
    return pltpu.VMEM((*lead, YP if pad else NY, NZ), f32)


def local(log_cond, opening_increase, heat_load, measured, duct_cells, duct_segment):
    grid = lax.axis_size("grid")
    tests = lax.axis_size("tests")
    lists = duct_cells.reshape(2, 128, 8).transpose(0, 2, 1).reshape(16, 128).astype(f32)
    segment = duct_segment.reshape(2, 128).astype(f32)
    pack = jnp.concatenate(
        [
            opening_increase.reshape(CELLS, NZ),
            heat_load.reshape(CELLS, NZ),
            log_cond.reshape(CELLS, NZ),
            lists,
            segment,
            jnp.zeros((6, NZ), f32),
        ],
        axis=0,
    )
    to_far = [(s, s - 2) for s in range(2, grid, 2)] + [(s, s + 2) for s in range(1, grid - 2, 2)]
    to_near = [(s, s + 2) for s in range(0, grid - 2, 2)] + [(s, s - 2) for s in range(3, grid, 2)]
    swap = [(s, s ^ 1) for s in range(grid)]
    far2 = lax.ppermute(pack, "grid", to_far)
    far1 = lax.ppermute(pack, "grid", swap)
    near2 = lax.ppermute(pack, "grid", to_near)
    near1 = lax.ppermute(far2, "grid", swap)
    packs = (near2, near1, pack, far1, far2)
    vmem = pl.BlockSpec(memory_space=pltpu.VMEM)
    coefs = [field(EXT, pad=False), field(EXT), field(EXT, pad=False), field(EXT, pad=False), field(EXT, pad=False)]
    params = pltpu.CompilerParams(vmem_limit_bytes=40 * 1024 * 1024)
    kept, sums = pl.pallas_call(
        forward_kernel,
        out_shape=(
            jax.ShapeDtypeStruct((STEPS, 4, YP, NZ), f32),
            jax.ShapeDtypeStruct((grid, 128), f32),
        ),
        in_specs=[vmem] * 6,
        out_specs=(vmem, vmem),
        scratch_shapes=[field(STEPS + 1, EXT), field(EXT, pad=False), field(EXT), *coefs],
        compiler_params=params,
        name="forward",
    )(*packs, measured)
    sums = lax.all_to_all(sums, "grid", split_axis=0, concat_axis=0, tiled=True)
    cond_spec = pl.BlockSpec((CELLS, NZ), lambda i: (2, 0))
    duct_spec = pl.BlockSpec((24, NZ), lambda i: (3 * CELLS // 24, 0))
    whole4 = pl.BlockSpec((STEPS, 4, YP, NZ), lambda i: (0, 0, 0, 0))
    share = NY // tests
    grad, seg = pl.pallas_call(
        backward_kernel,
        grid=(1,),
        out_shape=(
            jax.ShapeDtypeStruct((tests, 2, share, NZ), f32),
            jax.ShapeDtypeStruct(measured.shape, f32),
        ),
        in_specs=[cond_spec] * 5 + [duct_spec] * 5 + [whole4, pl.BlockSpec((grid, 128), lambda i: (0, 0))],
        out_specs=(
            pl.BlockSpec((tests, 2, share, NZ), lambda i: (0, 0, 0, 0)),
            pl.BlockSpec(measured.shape, lambda i: (0, 0)),
        ),
        scratch_shapes=[field(STEPS, EXT), field(EXT), *coefs, pltpu.VMEM((NY, NZ), f32)],
        compiler_params=params,
        name="backward",
    )(*packs, *packs, kept, sums)
    grad = lax.all_to_all(grad, "tests", split_axis=0, concat_axis=0, tiled=True)
    return jnp.sum(grad, axis=0), seg


def solution(mesh):
    in_specs = (
        P("grid", None, None),
        P("tests", "grid", None, None),
        P("tests", "grid", None, None),
        P("tests", "grid"),
        P("grid", None),
        P("grid", None),
    )
    out_specs = (P("grid", "tests", None), P("tests", "grid"))
    return jax.shard_map(local, mesh=mesh, in_specs=in_specs, out_specs=out_specs, check_vma=False)
```

time: 415 us -> 81.1 us (0.20)
  the two profiles are of different devices: /device:TPU:2 before, /device:TPU:8 now
where the time goes in v1:
time: 81.1 us; the launch traced here: 80.7 us
  blocking collectives  38.7 us (48%)
  starting transfers between devices  13.5 us (17%)
  waiting for transfers between devices  11.3 us (14%)
  Pallas kernels  11.2 us (14%)
  local copies, waits for them, and re-layouts  3.41 us (4%)
  other arithmetic  2 us (2%)
    all_to_all x1, blocking collectives, local(): lax.all_to_all(grad, 'tests', split_axis=0, concat_axis=0, tiled=True)  26.6 us
    all_to_all x1, blocking collectives, local(): sums = lax.all_to_all(sums, 'grid', split_axis=0, concat_axis=0, tiled=True)  12.2 us
    ppermute x1, waiting for transfers between devices, local(): far2 = lax.ppermute(pack, 'grid', to_far)  9.57 us
    ppermute x1, starting transfers between devices, local(): far2 = lax.ppermute(pack, 'grid', to_far)  7.72 us
    pallas_call x1, Pallas kernels, local(): pl.pallas_call(backward_kernel, grid=(1,), out_shape=(jax.ShapeDtypeStruc...  6.74 us
    pallas_call x1, Pallas kernels, local(): pl.pallas_call(forward_kernel, out_shape=(jax.ShapeDtypeStruct((STEPS, 4,...  4.42 us
    concatenate x1, local copies, waits for them, and re-layouts, local(): jnp.concatenate([opening_increase.reshape(CELLS, NZ), heat_load.reshape(C...  2.76 us
    ppermute x1, starting transfers between devices, local(): far1 = lax.ppermute(pack, 'grid', swap)  1.92 us
  transfers between devices with their start and end apart: 4, of which 2 were waited for; matrix products, arithmetic and copies ran while one was open for 0% of the time, Pallas kernels for 0%

profile of v1, /device:TPU:8, one launch (start us, length us, event | category | flops | bytes accessed | tf_op | source)
XLA Modules:
  0.0 80.7 jit_solution(17973610687648761459)
XLA Ops:
  0.6 0.7 convert_element_type.22
  1.3 0.7 convert_bitcast_fusion
  2.0 2.8 %concatenate.3.own.ownd = f32[792,128]{1,0:T(8,128)S(1)} concatenate(f32[256,128]{1,0:T(8,128)} %bitcast.16, f32[256,128]{1,0:T(8,128)} %bitcast.17, f32[256,128]{1,0:T(8,128)} %bitcast.18, f32[16,128]{1,0:T(8,128)S(1)} %convert_bitcast_fusion, f32[2,128]{1,0:T(2,128)S(1)} %bitcast.19, f32[6,128]{1,0:T(8,128)S(1)} %broadcast_in_dim.3), dimensions={0} | concatenate | bytes 811008 | tf_op jit(solution)/shard_map/concatenate | solution.py:287
  4.8 7.7 %collective-permute-start.1 = (f32[792,128]{1,0:T(8,128)S(1)}, f32[792,128]{1,0:T(8,128)S(1)}, u32[]{:S(2)}, u32[]{:S(2)}) collective-permute-start(f32[792,128]{1,0:T(8,128)S(1)} %concatenate.3.own.ownd), channel_id=1, source_target_pairs={{2,0},{4,2},{6,4},{8,6},{10,8},{12,10},{14,12},{16,14},{18,16},{20... | collective-permute-start | bytes 1216520 | tf_op jit(solution)/shard_map/ppermute | solution.py:301
  12.5 1.9 %collective-permute-start.3 = (f32[792,128]{1,0:T(8,128)S(1)}, f32[792,128]{1,0:T(8,128)S(1)}, u32[]{:S(2)}, u32[]{:S(2)}) collective-permute-start(f32[792,128]{1,0:T(8,128)S(1)} %concatenate.3.own.ownd), channel_id=1, source_target_pairs={{0,1},{1,0},{2,3},{3,2},{4,5},{5,4},{6,7},{7,6},{8,9},{9,8},{10,11... | collective-permute-start | bytes 1216520 | tf_op jit(solution)/shard_map/ppermute | solution.py:302
  14.4 1.9 %collective-permute-start = (f32[792,128]{1,0:T(8,128)S(1)}, f32[792,128]{1,0:T(8,128)S(1)}, u32[]{:S(2)}, u32[]{:S(2)}) collective-permute-start(f32[792,128]{1,0:T(8,128)S(1)} %concatenate.3.own.ownd), channel_id=1, source_target_pairs={{0,2},{2,4},{4,6},{6,8},{8,10},{10,12},{12,14},{14,16},{16,18},{18... | collective-permute-start | bytes 1216520 | tf_op jit(solution)/shard_map/ppermute | solution.py:303
  16.4 9.6 %collective-permute-done.1.far2.far2d = f32[792,128]{1,0:T(8,128)S(1)} collective-permute-done((f32[792,128]{1,0:T(8,128)S(1)}, f32[792,128]{1,0:T(8,128)S(1)}, u32[]{:S(2)}, u32[]{:S(2)}) %collective-permute-start.1) | collective-permute-done | bytes 405536 | tf_op jit(solution)/shard_map/ppermute | solution.py:301
  25.9 1.9 %collective-permute-start.2 = (f32[792,128]{1,0:T(8,128)S(1)}, f32[792,128]{1,0:T(8,128)S(1)}, u32[]{:S(2)}, u32[]{:S(2)}) collective-permute-start(f32[792,128]{1,0:T(8,128)S(1)} %collective-permute-done.1.far2.far2d), channel_id=1, source_target_pairs={{0,1},{1,0},{2,3},{3,2},{4,5},{5,4},{6,7},{7,6},{8,9},{9,8},{10,11... | collective-permute-start | bytes 1216520 | tf_op jit(solution)/shard_map/ppermute | solution.py:304
  27.8 0.0 collective-permute-done.3.far1.far1d
  27.9 0.0 collective-permute-done.near2.near2d
  27.9 1.7 %collective-permute-done.2.near1.near1d = f32[792,128]{1,0:T(8,128)S(1)} collective-permute-done((f32[792,128]{1,0:T(8,128)S(1)}, f32[792,128]{1,0:T(8,128)S(1)}, u32[]{:S(2)}, u32[]{:S(2)}) %collective-permute-start.2) | collective-permute-done | bytes 405536 | tf_op jit(solution)/shard_map/ppermute | solution.py:304
  29.6 0.0 copy-start
  29.6 0.7 copy-done
  30.2 4.4 %forward.1 = (f32[4,4,144,128]{3,2,1,0:T(8,128)S(1)}, f32[32,128]{1,0:T(8,128)S(1)}) custom-call(f32[792,128]{1,0:T(8,128)S(1)} %collective-permute-done.near2.near2d, f32[792,128]{1,0:T(8,128)S(1)} %collective-permute-done.2.near1.near1d, f32[792,128]{1,0:T(8,128)S(1)} %concatenate.3.own.ownd, f32[792,128]{1,0:T(8,128)S(1)} %collective-permute-done.3.far1.far1d, ...), custom_call_target="tpu_custom_call" | custom-call | tf_op jit(solution)/shard_map/forward/pallas_call | solution.py:309
  34.6 12.2 %all_to_all.16 = f32[32,1,128]{2,1,0:T(1,128)S(1)} all-to-all(f32[32,1,128]{2,1,0:T(1,128)S(1)} %bitcast.15), channel_id=1, replica_groups=mesh['tests'=16,'grid'=32] {'grid'}, dimensions={0} | all-to-all | bytes 32768 | tf_op jit(solution)/shard_map/all_to_all | solution.py:321
  46.8 6.7 %backward.1 = (f32[16,2,8,128]{3,2,1,0:T(8,128)S(1)}, f32[1,4]{1,0:T(1,128)}) custom-call(f32[792,128]{1,0:T(8,128)S(1)} %collective-permute-done.near2.near2d, f32[792,128]{1,0:T(8,128)S(1)} %collective-permute-done.2.near1.near1d, f32[792,128]{1,0:T(8,128)S(1)} %concatenate.3.own.ownd, f32[792,128]{1,0:T(8,128)S(1)} %collective-permute-done.3.far1.far1d, ...), custom_call_target="tpu_custom_call" | custom-call | tf_op jit(solution)/shard_map/backward/pallas_call | solution.py:326
  53.5 26.6 %all_to_all.17 = f32[16,2,8,128]{3,2,1,0:T(8,128)S(1)} all-to-all(f32[16,2,8,128]{3,2,1,0:T(8,128)S(1)} %get-tuple-element.8), channel_id=1, replica_groups=mesh['tests'=16,'grid'=32] {'tests'}, dimensions={0} | all-to-all | bytes 262144 | tf_op jit(solution)/shard_map/all_to_all | solution.py:342
  80.1 0.6 reduce_sum.9
  (1 shorter events, 0.0 us)
Async XLA Ops:
  4.8 21.2 %collective-permute-start.1 = (f32[792,128]{1,0:T(8,128)S(1)}, f32[792,128]{1,0:T(8,128)S(1)}, u32[]{:S(2)}, u32[]{:S(2)}) collective-permute-start(f32[792,128]{1,0:T(8,128)S(1)} %concatenate.3.own.ownd), channel_id=1, source_target_pairs={{2,0},{4,2},{6,4},{8,6},{10,8},{12,10},{14,12},{16,14},{18,16},{20... | collective-permute-start | bytes 1216520 | tf_op jit(solution)/shard_map/ppermute | solution.py:301
  12.5 15.4 %collective-permute-start.3 = (f32[792,128]{1,0:T(8,128)S(1)}, f32[792,128]{1,0:T(8,128)S(1)}, u32[]{:S(2)}, u32[]{:S(2)}) collective-permute-start(f32[792,128]{1,0:T(8,128)S(1)} %concatenate.3.own.ownd), channel_id=1, source_target_pairs={{0,1},{1,0},{2,3},{3,2},{4,5},{5,4},{6,7},{7,6},{8,9},{9,8},{10,11... | collective-permute-start | bytes 1216520 | tf_op jit(solution)/shard_map/ppermute | solution.py:302
  14.4 13.4 %collective-permute-start = (f32[792,128]{1,0:T(8,128)S(1)}, f32[792,128]{1,0:T(8,128)S(1)}, u32[]{:S(2)}, u32[]{:S(2)}) collective-permute-start(f32[792,128]{1,0:T(8,128)S(1)} %concatenate.3.own.ownd), channel_id=1, source_target_pairs={{0,2},{2,4},{4,6},{6,8},{8,10},{10,12},{12,14},{14,16},{16,18},{18... | collective-permute-start | bytes 1216520 | tf_op jit(solution)/shard_map/ppermute | solution.py:303
  25.9 3.6 %collective-permute-start.2 = (f32[792,128]{1,0:T(8,128)S(1)}, f32[792,128]{1,0:T(8,128)S(1)}, u32[]{:S(2)}, u32[]{:S(2)}) collective-permute-start(f32[792,128]{1,0:T(8,128)S(1)} %collective-permute-done.1.far2.far2d), channel_id=1, source_target_pairs={{0,1},{1,0},{2,3},{3,2},{4,5},{5,4},{6,7},{7,6},{8,9},{9,8},{10,11... | collective-permute-start | bytes 1216520 | tf_op jit(solution)/shard_map/ppermute | solution.py:304
  29.6 0.7 copy-start

commit v2 on v1

--- a/solution.py
+++ b/solution.py
@@ -1,5 +1,3 @@
-import functools
-
 import jax
 import jax.numpy as jnp
 from jax import lax
@@ -19,7 +17,12 @@
 YP = NY + 2 * PAD
 MID = slice(PAD, PAD + NY)
 CH = 32
-PACK = 3 * CELLS + 24
+Q0 = 0
+U0 = NY
+C0 = U0 + CELLS
+D0 = C0 + CELLS
+Q1 = D0 + 24
+PACK = Q1 + NY
 bf16 = jnp.bfloat16
 f32 = jnp.float32
 
@@ -134,28 +137,65 @@
     return jnp.where(mask, 1.0, 0.0).astype(bf16)
 
 
-def duct_lists(duct, base, core):
+def duct_lists(duct, base, flip):
     cells = jnp.concatenate([duct[base : base + 8], duct[base + 8 : base + 16]], axis=1)
-    cells = cells.astype(jnp.int32) ^ (core * CELLS // 2 * NZ)
+    cells = cells.astype(jnp.int32)
+    if flip:
+        cells = cells ^ (NY * NZ)
     extra = duct[base + 16 : base + 24]
     segment = jnp.concatenate([extra[0:1], extra[1:2]], axis=1).astype(jnp.int32)
     return cells >> 7, cells & (NZ - 1), segment
 
 
+def pack_kernel(log_cond, opening, heat, cells, segment, measured, full, cells_v, segment_v, measured_v, sems):
+    g, core, _, _ = position()
+    copies = []
+
+    def copy(src, dst):
+        copies.append(pltpu.make_async_copy(src, dst, sems.at[len(copies)]))
+        copies[-1].start()
+
+    for r in range(2):
+        at = r ^ core
+        copy(opening.at[0, at], full.at[pl.ds(U0 + r * NY, NY)])
+        copy(log_cond.at[at], full.at[pl.ds(C0 + r * NY, NY)])
+        copy(heat.at[0, at], full.at[pl.ds(Q1 if r else Q0, NY)])
+    copy(cells, cells_v)
+    copy(segment, segment_v)
+    copy(measured, measured_v)
+    for each in copies:
+        each.wait()
+    flipped = (cells_v[...] ^ (core * NY * NZ)).astype(f32)
+    lane = lax.broadcasted_iota(jnp.int32, (8, 128), 1)
+    row = lax.broadcasted_iota(jnp.int32, (8, 128), 0)
+    seg = segment_v[...].astype(f32)
+    extra = jnp.where(row == 0, seg[:, :128], jnp.where(row == 1, seg[:, 128:], 0.0))
+    for n in range(measured.shape[1]):
+        mine = (row == 2) & (lane == measured.shape[1] * g + n)
+        extra = jnp.where(mine, measured_v[0:1, n : n + 1], extra)
+    full[D0 : D0 + 8] = flipped[:, :128]
+    full[D0 + 8 : D0 + 16] = flipped[:, 128:]
+    full[D0 + 16 : D0 + 24] = extra
+
+
+def slab_rows(near2, near1, own, far1, far2):
+    out = []
+    for j, slab in enumerate((near2, near1, own, far1, far2)):
+        for r in range(2):
+            out.append((slab, 1 - r if j in (1, 3) else r))
+    return out
+
+
 def forward_kernel(
-    near2, near1, own, far1, far2, measured, kept, sums, temp, load, cond, kx, ky, kzp, kzm, keep
+    near2, near1, own, far1, far2, temp, sums, cond, kx, ky, kzp, kzm, keep, load
 ):
-    g, core, _, _ = position()
     near, far = validity()
-    slabs = (near2, near1, own, far1, far2)
-    for j, slab in enumerate(slabs):
-        valid = (near, near, 1.0, 1.0, far)[j]
-        for r in range(2):
-            i = 2 * j + r
-            start = pl.multiple_of((r ^ core) * NY, NY)
-            temp[0, i, MID] = slab[pl.ds(start, NY)]
-            load[i] = DT * slab[pl.ds(CELLS + start, NY)]
-            cond[i, MID] = jnp.exp(slab[pl.ds(2 * CELLS + start, NY)]) * valid
+    for i, (slab, r) in enumerate(slab_rows(near2, near1, own, far1, far2)):
+        valid = near if i < 4 else (far if i > 7 else 1.0)
+        temp[0, i, MID] = slab[pl.ds(U0 + r * NY, NY)]
+        cond[i, MID] = jnp.exp(slab[pl.ds(C0 + r * NY, NY)]) * valid
+        if 1 <= i <= 8:
+            load[i] = DT * slab[pl.ds(Q1 if r else Q0, NY)]
 
     def pads(i, carry):
         zero_pads(cond, i)
@@ -169,14 +209,7 @@
     for k in range(STEPS):
         advance(temp.at[k], temp.at[k + 1], k + 1, 8 - k, coefs, load, near, far)
 
-    def save(i, carry):
-        for k in range(STEPS):
-            kept[k, i] = temp[k, 3 + i]
-        return carry
-
-    lax.fori_loop(0, 4, save, 0)
-
-    rows, lanes, segment = duct_lists(own, 3 * CELLS, core)
+    rows, lanes, segment = duct_lists(own, D0, False)
     across = jnp.concatenate([temp[STEPS, 4, MID].T, temp[STEPS, 5, MID].T], axis=1)
     stack = jnp.concatenate([part.astype(bf16) for part in parts_of(across, 3)], axis=0)
     picked = jnp.zeros((NZ, 256), f32)
@@ -192,58 +225,45 @@
         (((1,), (1,)), ((), ())),
         preferred_element_type=f32,
     )
-    total = jnp.sum(by_segment, axis=0, keepdims=True)
-    lane = lax.broadcasted_iota(jnp.int32, (1, 128), 1)
-    for n in range(measured.shape[1]):
-        mine = lane == measured.shape[1] * g + n
-        total = total - jnp.where(mine, measured[0:1, n : n + 1], 0.0)
+    total = jnp.sum(by_segment, axis=0, keepdims=True) - own[pl.ds(D0 + 16, 8)][2:3]
     sums[...] = jnp.broadcast_to(total, sums.shape)
 
 
 def backward_kernel(
-    near2, near1, own, far1, far2, near2d, near1d, ownd, far1d, far2d, kept, sums,
-    grad, seg, costate, cond, kx, ky, kzp, kzm, keep, acc,
+    near2, near1, own, far1, far2, temp, sums, cond, kx, ky, kzp, kzm, keep,
+    grad, seg, costate, acc, at_rows, weights,
 ):
     g, core, _, _ = position()
     near, far = validity()
-    conds = (near2, near1, own, far1, far2)
-    ducts = (near2d, near1d, ownd, far1d, far2d)
     resid = jnp.sum(sums[...], axis=0, keepdims=True)
     shift = lax.rem(128 - seg.shape[1] * g, 128)
     seg[...] = pltpu.roll(jnp.broadcast_to(resid, (8, 128)), shift, 1)[0:1, 0 : seg.shape[1]]
     stack = stacked_rows(parts_of(0.5 * resid, 3))
-    for j in range(5):
+    for j, slab in enumerate((near2, near1, own, far1, far2)):
         valid = (near, near, 1.0, 1.0, far)[j]
-        for r in range(2):
-            start = pl.multiple_of((r ^ core) * NY, NY)
-            cond[2 * j + r, MID] = jnp.exp(conds[j][pl.ds(start, NY)]) * valid
-        rows, lanes, segment = duct_lists(ducts[j], 0, core)
+        rows, lanes, segment = duct_lists(slab, D0, j in (1, 3))
         source = jnp.dot(stack, as_bf16(hot(segment, 128)), preferred_element_type=f32)
         source = jnp.sum(source, axis=0, keepdims=True) * valid
         upper, lower = parts_of(source, 2)
-        out = jnp.zeros((CELLS, 2 * NZ), f32)
         for c in range(8):
-            at_row = as_bf16(hot(rows[c : c + 1], CELLS))
+            at = pl.ds(256 * c, 256)
+            at_rows[j, :, at] = as_bf16(hot(rows[c : c + 1], CELLS))
             at_lane = hot(lanes[c : c + 1], NZ)
-            weight = jnp.concatenate(
-                [jnp.where(at_lane, upper, 0.0).astype(bf16), jnp.where(at_lane, lower, 0.0).astype(bf16)],
-                axis=0,
-            )
-            out = out + lax.dot_general(
-                at_row, weight, (((1,), (1,)), ((), ())), preferred_element_type=f32
-            )
+            weights[j, 0:NZ, at] = jnp.where(at_lane, upper, 0.0).astype(bf16)
+            weights[j, NZ : 2 * NZ, at] = jnp.where(at_lane, lower, 0.0).astype(bf16)
+        out = lax.dot_general(
+            at_rows[j], weights[j], (((1,), (1,)), ((), ())), preferred_element_type=f32
+        )
         out = out[:, :NZ] + out[:, NZ:]
         costate[0, 2 * j, MID] = out[:NY]
         costate[0, 2 * j + 1, MID] = out[NY:]
 
     def pads(i, carry):
-        zero_pads(cond, i)
         for k in range(STEPS):
             zero_pads(costate.at[k], i)
         return carry
 
     lax.fori_loop(0, EXT, pads, 0)
-    coefficients(cond, kx, ky, kzp, kzm, keep)
     coefs = (kx, ky, kzp, kzm, keep)
     for k in range(STEPS - 1):
         advance(costate.at[k], costate.at[k + 1], k + 1, 8 - k, coefs, None, near, far)
@@ -257,13 +277,12 @@
             left, right = pl.ds(PAD + y - 1, CH), pl.ds(PAD + y + 1, CH)
             total = jnp.zeros((CH, NZ), f32)
             for k in range(STEPS):
-                u, a = kept.at[k], costate.at[STEPS - 1 - k]
-                p = i - 3
-                uc, ac = u[p, here], a[i, here]
-                total += (uc - u[p + 1, here]) * (ac - a[i + 1, here])
-                total += (uc - u[p - 1, here]) * (ac - a[i - 1, here])
-                total += (uc - u[p, right]) * (ac - a[i, right])
-                total += (uc - u[p, left]) * (ac - a[i, left])
+                u, a = temp.at[k], costate.at[STEPS - 1 - k]
+                uc, ac = u[i, here], a[i, here]
+                total += (uc - u[i + 1, here]) * (ac - a[i + 1, here])
+                total += (uc - u[i - 1, here]) * (ac - a[i - 1, here])
+                total += (uc - u[i, right]) * (ac - a[i, right])
+                total += (uc - u[i, left]) * (ac - a[i, left])
                 side = (uc - ahead_z(uc, ahead_keep)) * (ac - ahead_z(ac, ahead_keep))
                 side += (uc - behind_z(uc, behind_keep)) * (ac - behind_z(ac, behind_keep))
                 total += 0.5 * side
@@ -276,25 +295,32 @@
 
 
 def field(*lead, pad=True):
-    return pltpu.VMEM((*lead, YP if pad else NY, NZ), f32)
+    return (*lead, YP if pad else NY, NZ)
+
+
+def in_hbm(values):
+    return pltpu.with_memory_space_constraint(values, pltpu.HBM)
 
 
 def local(log_cond, opening_increase, heat_load, measured, duct_cells, duct_segment):
     grid = lax.axis_size("grid")
     tests = lax.axis_size("tests")
-    lists = duct_cells.reshape(2, 128, 8).transpose(0, 2, 1).reshape(16, 128).astype(f32)
-    segment = duct_segment.reshape(2, 128).astype(f32)
-    pack = jnp.concatenate(
-        [
-            opening_increase.reshape(CELLS, NZ),
-            heat_load.reshape(CELLS, NZ),
-            log_cond.reshape(CELLS, NZ),
-            lists,
-            segment,
-            jnp.zeros((6, NZ), f32),
+    vmem = pl.BlockSpec(memory_space=pltpu.VMEM)
+    params = pltpu.CompilerParams(vmem_limit_bytes=24 * 1024 * 1024)
+    pack = pl.pallas_call(
+        pack_kernel,
+        out_shape=pltpu.VMEM((PACK, NZ), f32),
+        in_specs=[pl.BlockSpec(memory_space=pltpu.HBM)] * 6,
+        out_specs=vmem,
+        scratch_shapes=[
+            pltpu.VMEM((8, 256), jnp.int32),
+            pltpu.VMEM((1, 256), jnp.int32),
+            pltpu.VMEM(measured.shape, f32),
+            pltpu.SemaphoreType.DMA((9,)),
         ],
-        axis=0,
-    )
+        compiler_params=params,
+        name="pack",
+    )(*map(in_hbm, (log_cond, opening_increase, heat_load, duct_cells.T, duct_segment.T, measured)))
     to_far = [(s, s - 2) for s in range(2, grid, 2)] + [(s, s + 2) for s in range(1, grid - 2, 2)]
     to_near = [(s, s + 2) for s in range(0, grid - 2, 2)] + [(s, s - 2) for s in range(3, grid, 2)]
     swap = [(s, s ^ 1) for s in range(grid)]
@@ -303,42 +329,37 @@
     near2 = lax.ppermute(pack, "grid", to_near)
     near1 = lax.ppermute(far2, "grid", swap)
     packs = (near2, near1, pack, far1, far2)
-    vmem = pl.BlockSpec(memory_space=pltpu.VMEM)
-    coefs = [field(EXT, pad=False), field(EXT), field(EXT, pad=False), field(EXT, pad=False), field(EXT, pad=False)]
-    params = pltpu.CompilerParams(vmem_limit_bytes=40 * 1024 * 1024)
-    kept, sums = pl.pallas_call(
+    coefs = [field(EXT), field(EXT, pad=False), field(EXT), field(EXT, pad=False), field(EXT, pad=False), field(EXT, pad=False)]
+    temp, sums, *coefs = pl.pallas_call(
         forward_kernel,
-        out_shape=(
-            jax.ShapeDtypeStruct((STEPS, 4, YP, NZ), f32),
-            jax.ShapeDtypeStruct((grid, 128), f32),
+        out_shape=tuple(
+            jax.ShapeDtypeStruct(shape, f32) for shape in (field(STEPS + 1, EXT), (grid, 128), *coefs)
         ),
-        in_specs=[vmem] * 6,
-        out_specs=(vmem, vmem),
-        scratch_shapes=[field(STEPS + 1, EXT), field(EXT, pad=False), field(EXT), *coefs],
+        in_specs=[vmem] * 5,
+        out_specs=(vmem,) * 8,
+        scratch_shapes=[pltpu.VMEM(field(EXT, pad=False), f32)],
         compiler_params=params,
         name="forward",
-    )(*packs, measured)
+    )(*packs)
     sums = lax.all_to_all(sums, "grid", split_axis=0, concat_axis=0, tiled=True)
-    cond_spec = pl.BlockSpec((CELLS, NZ), lambda i: (2, 0))
-    duct_spec = pl.BlockSpec((24, NZ), lambda i: (3 * CELLS // 24, 0))
-    whole4 = pl.BlockSpec((STEPS, 4, YP, NZ), lambda i: (0, 0, 0, 0))
     share = NY // tests
     grad, seg = pl.pallas_call(
         backward_kernel,
-        grid=(1,),
         out_shape=(
             jax.ShapeDtypeStruct((tests, 2, share, NZ), f32),
             jax.ShapeDtypeStruct(measured.shape, f32),
         ),
-        in_specs=[cond_spec] * 5 + [duct_spec] * 5 + [whole4, pl.BlockSpec((grid, 128), lambda i: (0, 0))],
-        out_specs=(
-            pl.BlockSpec((tests, 2, share, NZ), lambda i: (0, 0, 0, 0)),
-            pl.BlockSpec(measured.shape, lambda i: (0, 0)),
-        ),
-        scratch_shapes=[field(STEPS, EXT), field(EXT), *coefs, pltpu.VMEM((NY, NZ), f32)],
+        in_specs=[vmem] * 13,
+        out_specs=(vmem, vmem),
+        scratch_shapes=[
+            pltpu.VMEM(field(STEPS, EXT), f32),
+            pltpu.VMEM((NY, NZ), f32),
+            pltpu.VMEM((5, CELLS, 2048), bf16),
+            pltpu.VMEM((5, CELLS, 2048), bf16),
+        ],
         compiler_params=params,
         name="backward",
-    )(*packs, *packs, kept, sums)
+    )(*packs, temp, sums, *coefs)
     grad = lax.all_to_all(grad, "tests", split_axis=0, concat_axis=0, tiled=True)
     return jnp.sum(grad, axis=0), seg
 

time: 81.1 us -> 76.7 us (0.946)
  local copies, waits for them, and re-layouts: 3.41 us -> 0 us
  other arithmetic: 2 us -> 0.62 us
    concatenate x1 -> x0, local copies, waits for them, and re-layouts: 2.76 us -> none  [local(): jnp.concatenate([opening_increase.reshape(CELLS, NZ), heat_load.reshape(C...]
    convert_element_type x2 -> x0, other arithmetic: 1.38 us -> none  [the longest x1 0.7 us: local(): duct_cells.reshape(2, 128, 8).transpose(0, 2, 1).reshape(16, 128)]
    pallas_call x2 -> x3, Pallas kernels: 11.2 us -> 11.6 us  [the longest x1 5.96 us: local(): pl.pallas_call(backward_kernel, out_shape=(jax.ShapeDtypeStruct((tests, 2...]
where the time goes in v2:
time: 76.7 us; the launch traced here: 76.4 us
  blocking collectives  38.7 us (50%)
  starting transfers between devices  13.5 us (18%)
  Pallas kernels  11.6 us (15%)
  waiting for transfers between devices  11.3 us (15%)
    all_to_all x1, blocking collectives, local(): lax.all_to_all(grad, 'tests', split_axis=0, concat_axis=0, tiled=True)  26.6 us
    all_to_all x1, blocking collectives, local(): sums = lax.all_to_all(sums, 'grid', split_axis=0, concat_axis=0, tiled=True)  12.2 us
    ppermute x1, waiting for transfers between devices, local(): far2 = lax.ppermute(pack, 'grid', to_far)  9.57 us
    ppermute x1, starting transfers between devices, local(): far2 = lax.ppermute(pack, 'grid', to_far)  7.73 us
    pallas_call x1, Pallas kernels, local(): pl.pallas_call(backward_kernel, out_shape=(jax.ShapeDtypeStruct((tests, 2...  5.96 us
    pallas_call x1, Pallas kernels, local(): pl.pallas_call(forward_kernel, out_shape=tuple((jax.ShapeDtypeStruct(shap...  4.45 us
    ppermute x1, starting transfers between devices, local(): far1 = lax.ppermute(pack, 'grid', swap)  1.92 us
    ppermute x1, starting transfers between devices, local(): near2 = lax.ppermute(pack, 'grid', to_near)  1.92 us
  transfers between devices with their start and end apart: 4, of which 2 were waited for; matrix products, arithmetic and copies ran while one was open for 0% of the time, Pallas kernels for 0%

profile of v2, /device:TPU:8, one launch (start us, length us, event | category | flops | bytes accessed | tf_op | source)
XLA Modules:
  0.0 76.4 jit_solution(496480739239006993)
XLA Ops:
  0.6 1.2 %pack.1.own = f32[792,128]{1,0:T(8,128)S(1)} custom-call(f32[2,128,128]{2,1,0:T(8,128)} %log_cond.1, f32[1,2,128,128]{3,2,1,0:T(8,128)} %opening.1, f32[1,2,128,128]{3,2,1,0:T(8,128)} %heat.1, s32[8,256]{1,0:T(8,128)} %bitcast.8, s32[1,256]{1,0:T(1,128)} %bitcast.9, f32[1,4]{1,0:T(1,128)} %measured.1), custom_call_target="tpu_custom_call" | custom-call | tf_op jit(solution)/shard_map/pack/pallas_call | solution.py:310
  1.8 7.7 %collective-permute-start.1 = (f32[792,128]{1,0:T(8,128)S(1)}, f32[792,128]{1,0:T(8,128)S(1)}, u32[]{:S(2)}, u32[]{:S(2)}) collective-permute-start(f32[792,128]{1,0:T(8,128)S(1)} %pack.1.own), channel_id=1, source_target_pairs={{2,0},{4,2},{6,4},{8,6},{10,8},{12,10},{14,12},{16,14},{18,16},{20... | collective-permute-start | bytes 1216520 | tf_op jit(solution)/shard_map/ppermute | solution.py:327
  9.5 1.9 %collective-permute-start.3 = (f32[792,128]{1,0:T(8,128)S(1)}, f32[792,128]{1,0:T(8,128)S(1)}, u32[]{:S(2)}, u32[]{:S(2)}) collective-permute-start(f32[792,128]{1,0:T(8,128)S(1)} %pack.1.own), channel_id=1, source_target_pairs={{0,1},{1,0},{2,3},{3,2},{4,5},{5,4},{6,7},{7,6},{8,9},{9,8},{10,11... | collective-permute-start | bytes 1216520 | tf_op jit(solution)/shard_map/ppermute | solution.py:328
  11.5 1.9 %collective-permute-start = (f32[792,128]{1,0:T(8,128)S(1)}, f32[792,128]{1,0:T(8,128)S(1)}, u32[]{:S(2)}, u32[]{:S(2)}) collective-permute-start(f32[792,128]{1,0:T(8,128)S(1)} %pack.1.own), channel_id=1, source_target_pairs={{0,2},{2,4},{4,6},{6,8},{8,10},{10,12},{12,14},{14,16},{16,18},{18... | collective-permute-start | bytes 1216520 | tf_op jit(solution)/shard_map/ppermute | solution.py:329
  13.4 9.6 %collective-permute-done.1.far2 = f32[792,128]{1,0:T(8,128)S(1)} collective-permute-done((f32[792,128]{1,0:T(8,128)S(1)}, f32[792,128]{1,0:T(8,128)S(1)}, u32[]{:S(2)}, u32[]{:S(2)}) %collective-permute-start.1) | collective-permute-done | bytes 405536 | tf_op jit(solution)/shard_map/ppermute | solution.py:327
  23.0 1.9 %collective-permute-start.2 = (f32[792,128]{1,0:T(8,128)S(1)}, f32[792,128]{1,0:T(8,128)S(1)}, u32[]{:S(2)}, u32[]{:S(2)}) collective-permute-start(f32[792,128]{1,0:T(8,128)S(1)} %collective-permute-done.1.far2), channel_id=1, source_target_pairs={{0,1},{1,0},{2,3},{3,2},{4,5},{5,4},{6,7},{7,6},{8,9},{9,8},{10,11... | collective-permute-start | bytes 1216520 | tf_op jit(solution)/shard_map/ppermute | solution.py:330
  24.9 0.0 collective-permute-done.3.far1
  24.9 0.0 collective-permute-done.near2
  24.9 1.7 %collective-permute-done.2.near1 = f32[792,128]{1,0:T(8,128)S(1)} collective-permute-done((f32[792,128]{1,0:T(8,128)S(1)}, f32[792,128]{1,0:T(8,128)S(1)}, u32[]{:S(2)}, u32[]{:S(2)}) %collective-permute-start.2) | collective-permute-done | bytes 405536 | tf_op jit(solution)/shard_map/ppermute | solution.py:330
  26.6 4.4 %forward.1 = (f32[5,10,144,128]{3,2,1,0:T(8,128)S(1)}, f32[32,128]{1,0:T(8,128)S(1)}, f32[10,144,128]{2,1,0:T(8,128)S(1)}, f32[10,128,128]{2,1,0:T(8,128)S(1)}, ...) custom-call(f32[792,128]{1,0:T(8,128)S(1)} %collective-permute-done., ...), custom_call_target="tpu_custom_call" | custom-call | tf_op jit(solution)/shard_map/forward/pallas_call | solution.py:333
  31.0 12.2 %all_to_all.16 = f32[32,1,128]{2,1,0:T(1,128)S(1)} all-to-all(f32[32,1,128]{2,1,0:T(1,128)S(1)} %bitcast.7), channel_id=1, replica_groups=mesh['tests'=16,'grid'=32] {'grid'}, dimensions={0} | all-to-all | bytes 32768 | tf_op jit(solution)/shard_map/all_to_all | solution.py:344
  43.2 6.0 %backward.1 = (f32[16,2,8,128]{3,2,1,0:T(8,128)S(1)}, f32[1,4]{1,0:T(1,128)}) custom-call(f32[792,128]{1,0:T(8,128)S(1)} %collective-permute-done.near2, f32[792,128]{1,0:T(8,128)S(1)} %collective-permute-done.2.near1, f32[792,128]{1,0:T(8,128)S(1)} %pack.1.own, f32[792,128]{1,0:T(8,128)S(1)} %collective-permute-done.3.far1, ...), custom_call_target="tpu_custom_call" | custom-call | tf_op jit(solution)/shard_map/backward/pallas_call | solution.py:346
  49.2 26.6 %all_to_all.17 = f32[16,2,8,128]{3,2,1,0:T(8,128)S(1)} all-to-all(f32[16,2,8,128]{3,2,1,0:T(8,128)S(1)} %get-tuple-element.20), channel_id=1, replica_groups=mesh['tests'=16,'grid'=32] {'tests'}, dimensions={0} | all-to-all | bytes 262144 | tf_op jit(solution)/shard_map/all_to_all | solution.py:363
  75.7 0.6 reduce_sum.9
Async XLA Ops:
  1.8 21.2 %collective-permute-start.1 = (f32[792,128]{1,0:T(8,128)S(1)}, f32[792,128]{1,0:T(8,128)S(1)}, u32[]{:S(2)}, u32[]{:S(2)}) collective-permute-start(f32[792,128]{1,0:T(8,128)S(1)} %pack.1.own), channel_id=1, source_target_pairs={{2,0},{4,2},{6,4},{8,6},{10,8},{12,10},{14,12},{16,14},{18,16},{20... | collective-permute-start | bytes 1216520 | tf_op jit(solution)/shard_map/ppermute | solution.py:327
  9.5 15.4 %collective-permute-start.3 = (f32[792,128]{1,0:T(8,128)S(1)}, f32[792,128]{1,0:T(8,128)S(1)}, u32[]{:S(2)}, u32[]{:S(2)}) collective-permute-start(f32[792,128]{1,0:T(8,128)S(1)} %pack.1.own), channel_id=1, source_target_pairs={{0,1},{1,0},{2,3},{3,2},{4,5},{5,4},{6,7},{7,6},{8,9},{9,8},{10,11... | collective-permute-start | bytes 1216520 | tf_op jit(solution)/shard_map/ppermute | solution.py:328
  11.5 13.4 %collective-permute-start = (f32[792,128]{1,0:T(8,128)S(1)}, f32[792,128]{1,0:T(8,128)S(1)}, u32[]{:S(2)}, u32[]{:S(2)}) collective-permute-start(f32[792,128]{1,0:T(8,128)S(1)} %pack.1.own), channel_id=1, source_target_pairs={{0,2},{2,4},{4,6},{6,8},{8,10},{10,12},{12,14},{14,16},{16,18},{18... | collective-permute-start | bytes 1216520 | tf_op jit(solution)/shard_map/ppermute | solution.py:329
  23.0 3.6 %collective-permute-start.2 = (f32[792,128]{1,0:T(8,128)S(1)}, f32[792,128]{1,0:T(8,128)S(1)}, u32[]{:S(2)}, u32[]{:S(2)}) collective-permute-start(f32[792,128]{1,0:T(8,128)S(1)} %collective-permute-done.1.far2), channel_id=1, source_target_pairs={{0,1},{1,0},{2,3},{3,2},{4,5},{5,4},{6,7},{7,6},{8,9},{9,8},{10,11... | collective-permute-start | bytes 1216520 | tf_op jit(solution)/shard_map/ppermute | solution.py:330

commit v3 on v2

--- a/solution.py
+++ b/solution.py
@@ -23,6 +23,7 @@
 D0 = C0 + CELLS
 Q1 = D0 + 24
 PACK = Q1 + NY
+COST_ESTIMATE = 2_000_000_000
 bf16 = jnp.bfloat16
 f32 = jnp.float32
 
@@ -147,7 +148,7 @@
     return cells >> 7, cells & (NZ - 1), segment
 
 
-def pack_kernel(log_cond, opening, heat, cells, segment, measured, full, cells_v, segment_v, measured_v, sems):
+def pack_kernel(log_cond, opening, heat, cells, segment, measured, full, near, cells_v, segment_v, measured_v, sems):
     g, core, _, _ = position()
     copies = []
 
@@ -157,9 +158,13 @@
 
     for r in range(2):
         at = r ^ core
-        copy(opening.at[0, at], full.at[pl.ds(U0 + r * NY, NY)])
-        copy(log_cond.at[at], full.at[pl.ds(C0 + r * NY, NY)])
-        copy(heat.at[0, at], full.at[pl.ds(Q1 if r else Q0, NY)])
+        for out, skip in ((full, 0), (near, NY)):
+            copy(opening.at[0, at], out.at[pl.ds(U0 - skip + r * NY, NY)])
+            copy(log_cond.at[at], out.at[pl.ds(C0 - skip + r * NY, NY)])
+            if r == 1:
+                copy(heat.at[0, at], out.at[pl.ds(Q1 - skip, NY)])
+            elif skip == 0:
+                copy(heat.at[0, at], out.at[pl.ds(Q0, NY)])
     copy(cells, cells_v)
     copy(segment, segment_v)
     copy(measured, measured_v)
@@ -173,29 +178,55 @@
     for n in range(measured.shape[1]):
         mine = (row == 2) & (lane == measured.shape[1] * g + n)
         extra = jnp.where(mine, measured_v[0:1, n : n + 1], extra)
-    full[D0 : D0 + 8] = flipped[:, :128]
-    full[D0 + 8 : D0 + 16] = flipped[:, 128:]
-    full[D0 + 16 : D0 + 24] = extra
+    for out, skip in ((full, 0), (near, NY)):
+        out[pl.ds(D0 - skip, 8)] = flipped[:, :128]
+        out[pl.ds(D0 - skip + 8, 8)] = flipped[:, 128:]
+        out[pl.ds(D0 - skip + 16, 8)] = extra
+
+
+def write_hots(duct, base, flip, j, at_rows, at_lanes, at_segments):
+    rows, lanes, segment = duct_lists(duct, base, flip)
+    for c in range(8):
+        at = pl.ds(256 * c, 256)
+        at_rows[j, :, at] = as_bf16(hot(rows[c : c + 1], CELLS))
+        at_lanes[j, :, at] = as_bf16(hot(lanes[c : c + 1], NZ))
+    if at_segments is not None:
+        at_segments[j] = as_bf16(hot(segment, 128))
+
+
+def prepare_own_kernel(own, at_rows, at_lanes, at_segments):
+    write_hots(own, D0, False, 0, at_rows, at_lanes, at_segments)
+
+
+def prepare_far_kernel(far1, far2, at_rows, at_lanes, at_segments):
+    write_hots(far1, D0, True, 0, at_rows, at_lanes, at_segments)
+    write_hots(far2, D0, False, 1, at_rows, at_lanes, at_segments)
+
+
+def prepare_near_kernel(near2, far_segments, at_segments):
+    _, _, segment = duct_lists(near2, D0 - NY, False)
+    at_segments[0] = as_bf16(hot(segment, 128))
 
 
 def slab_rows(near2, near1, own, far1, far2):
     out = []
     for j, slab in enumerate((near2, near1, own, far1, far2)):
         for r in range(2):
-            out.append((slab, 1 - r if j in (1, 3) else r))
+            out.append((slab, NY if j == 0 else 0, 1 - r if j in (1, 3) else r))
     return out
 
 
 def forward_kernel(
-    near2, near1, own, far1, far2, temp, sums, cond, kx, ky, kzp, kzm, keep, load
+    near2, near1, own, far1, far2, at_rows, at_lanes, at_segments,
+    temp, sums, cond, kx, ky, kzp, kzm, keep, load,
 ):
     near, far = validity()
-    for i, (slab, r) in enumerate(slab_rows(near2, near1, own, far1, far2)):
+    for i, (slab, skip, r) in enumerate(slab_rows(near2, near1, own, far1, far2)):
         valid = near if i < 4 else (far if i > 7 else 1.0)
-        temp[0, i, MID] = slab[pl.ds(U0 + r * NY, NY)]
-        cond[i, MID] = jnp.exp(slab[pl.ds(C0 + r * NY, NY)]) * valid
+        temp[0, i, MID] = slab[pl.ds(U0 - skip + r * NY, NY)]
+        cond[i, MID] = jnp.exp(slab[pl.ds(C0 - skip + r * NY, NY)]) * valid
         if 1 <= i <= 8:
-            load[i] = DT * slab[pl.ds(Q1 if r else Q0, NY)]
+            load[i] = DT * slab[pl.ds((Q1 - skip) if r else Q0, NY)]
 
     def pads(i, carry):
         zero_pads(cond, i)
@@ -209,19 +240,18 @@
     for k in range(STEPS):
         advance(temp.at[k], temp.at[k + 1], k + 1, 8 - k, coefs, load, near, far)
 
-    rows, lanes, segment = duct_lists(own, D0, False)
     across = jnp.concatenate([temp[STEPS, 4, MID].T, temp[STEPS, 5, MID].T], axis=1)
     stack = jnp.concatenate([part.astype(bf16) for part in parts_of(across, 3)], axis=0)
     picked = jnp.zeros((NZ, 256), f32)
     for c in range(8):
-        at_row = as_bf16(hot(rows[c : c + 1], CELLS))
-        found = jnp.dot(stack, at_row, preferred_element_type=f32)
+        at = pl.ds(256 * c, 256)
+        found = jnp.dot(stack, at_rows[0, :, at], preferred_element_type=f32)
         value = (found[2 * NZ :] + found[NZ : 2 * NZ]) + found[:NZ]
-        picked = picked + jnp.where(hot(lanes[c : c + 1], NZ), value, 0.0)
+        picked = picked + value * at_lanes[0, :, at].astype(f32)
     partial = 0.5 * jnp.sum(picked, axis=0, keepdims=True)
     by_segment = lax.dot_general(
         stacked_rows(parts_of(partial, 3)),
-        as_bf16(hot(segment, 128)),
+        at_segments[0],
         (((1,), (1,)), ((), ())),
         preferred_element_type=f32,
     )
@@ -230,8 +260,9 @@
 
 
 def backward_kernel(
-    near2, near1, own, far1, far2, temp, sums, cond, kx, ky, kzp, kzm, keep,
-    grad, seg, costate, acc, at_rows, weights,
+    near2, near1, own_rows, own_lanes, own_segments, far_rows, far_lanes, far_segments, near2_segments,
+    temp, sums, cond, kx, ky, kzp, kzm, keep, grad, seg,
+    costate, acc, weights, near_rows, near_lanes, near_segments,
 ):
     g, core, _, _ = position()
     near, far = validity()
@@ -239,20 +270,22 @@
     shift = lax.rem(128 - seg.shape[1] * g, 128)
     seg[...] = pltpu.roll(jnp.broadcast_to(resid, (8, 128)), shift, 1)[0:1, 0 : seg.shape[1]]
     stack = stacked_rows(parts_of(0.5 * resid, 3))
-    for j, slab in enumerate((near2, near1, own, far1, far2)):
-        valid = (near, near, 1.0, 1.0, far)[j]
-        rows, lanes, segment = duct_lists(slab, D0, j in (1, 3))
-        source = jnp.dot(stack, as_bf16(hot(segment, 128)), preferred_element_type=f32)
+    write_hots(near2, D0 - NY, False, 0, near_rows, near_lanes, None)
+    near_segments[0] = near2_segments[0]
+    write_hots(near1, D0, True, 1, near_rows, near_lanes, near_segments)
+    own, fars = (own_rows, own_lanes, own_segments), (far_rows, far_lanes, far_segments)
+    nears = (near_rows, near_lanes, near_segments)
+    places = ((nears, 0, near), (nears, 1, near), (own, 0, 1.0), (fars, 0, 1.0), (fars, 1, far))
+    for j, ((at_rows, at_lanes, at_segments), n, valid) in enumerate(places):
+        source = jnp.dot(stack, at_segments[n], preferred_element_type=f32)
         source = jnp.sum(source, axis=0, keepdims=True) * valid
-        upper, lower = parts_of(source, 2)
+        upper, lower = (part.astype(bf16) for part in parts_of(source, 2))
         for c in range(8):
             at = pl.ds(256 * c, 256)
-            at_rows[j, :, at] = as_bf16(hot(rows[c : c + 1], CELLS))
-            at_lane = hot(lanes[c : c + 1], NZ)
-            weights[j, 0:NZ, at] = jnp.where(at_lane, upper, 0.0).astype(bf16)
-            weights[j, NZ : 2 * NZ, at] = jnp.where(at_lane, lower, 0.0).astype(bf16)
+            weights[j, 0:NZ, at] = at_lanes[n, :, at] * upper
+            weights[j, NZ : 2 * NZ, at] = at_lanes[n, :, at] * lower
         out = lax.dot_general(
-            at_rows[j], weights[j], (((1,), (1,)), ((), ())), preferred_element_type=f32
+            at_rows[n], weights[j], (((1,), (1,)), ((), ())), preferred_element_type=f32
         )
         out = out[:, :NZ] + out[:, NZ:]
         costate[0, 2 * j, MID] = out[:NY]
@@ -307,16 +340,16 @@
     tests = lax.axis_size("tests")
     vmem = pl.BlockSpec(memory_space=pltpu.VMEM)
     params = pltpu.CompilerParams(vmem_limit_bytes=24 * 1024 * 1024)
-    pack = pl.pallas_call(
+    pack, pack_near = pl.pallas_call(
         pack_kernel,
-        out_shape=pltpu.VMEM((PACK, NZ), f32),
+        out_shape=(pltpu.VMEM((PACK, NZ), f32), pltpu.VMEM((PACK - NY, NZ), f32)),
         in_specs=[pl.BlockSpec(memory_space=pltpu.HBM)] * 6,
-        out_specs=vmem,
+        out_specs=(vmem, vmem),
         scratch_shapes=[
             pltpu.VMEM((8, 256), jnp.int32),
             pltpu.VMEM((1, 256), jnp.int32),
             pltpu.VMEM(measured.shape, f32),
-            pltpu.SemaphoreType.DMA((9,)),
+            pltpu.SemaphoreType.DMA((14,)),
         ],
         compiler_params=params,
         name="pack",
@@ -326,40 +359,62 @@
     swap = [(s, s ^ 1) for s in range(grid)]
     far2 = lax.ppermute(pack, "grid", to_far)
     far1 = lax.ppermute(pack, "grid", swap)
-    near2 = lax.ppermute(pack, "grid", to_near)
+    near2 = lax.ppermute(pack_near, "grid", to_near)
+
+    def hots(slabs):
+        return (
+            pltpu.VMEM((slabs, CELLS, 2048), bf16),
+            pltpu.VMEM((slabs, NZ, 2048), bf16),
+            pltpu.VMEM((slabs, 128, 256), bf16),
+        )
+
+    def prepare(kernel, out_shape, name, *slabs):
+        return pl.pallas_call(
+            kernel,
+            out_shape=out_shape,
+            in_specs=[vmem] * len(slabs),
+            out_specs=(vmem,) * len(out_shape),
+            compiler_params=params,
+            cost_estimate=pl.CostEstimate(flops=COST_ESTIMATE, bytes_accessed=4_000_000, transcendentals=0),
+            name=name,
+        )(*slabs)
+
+    own_hots = prepare(prepare_own_kernel, hots(1), "prepare_own", pack)
+    far2, *own_hots = lax.optimization_barrier((far2, *own_hots))
     near1 = lax.ppermute(far2, "grid", swap)
+    far_hots = prepare(prepare_far_kernel, hots(2), "prepare_far", far1, far2)
+    near_hots = prepare(prepare_near_kernel, hots(1)[2:], "prepare_near", near2, far_hots[2])
+    near2, near_hots, far_hots = lax.optimization_barrier((near2, near_hots, far_hots))
     packs = (near2, near1, pack, far1, far2)
     coefs = [field(EXT), field(EXT, pad=False), field(EXT), field(EXT, pad=False), field(EXT, pad=False), field(EXT, pad=False)]
     temp, sums, *coefs = pl.pallas_call(
         forward_kernel,
-        out_shape=tuple(
-            jax.ShapeDtypeStruct(shape, f32) for shape in (field(STEPS + 1, EXT), (grid, 128), *coefs)
-        ),
-        in_specs=[vmem] * 5,
+        out_shape=tuple(pltpu.VMEM(shape, f32) for shape in (field(STEPS + 1, EXT), (grid, 128), *coefs)),
+        in_specs=[vmem] * 8,
         out_specs=(vmem,) * 8,
         scratch_shapes=[pltpu.VMEM(field(EXT, pad=False), f32)],
         compiler_params=params,
         name="forward",
-    )(*packs)
+    )(*packs, *own_hots)
     sums = lax.all_to_all(sums, "grid", split_axis=0, concat_axis=0, tiled=True)
     share = NY // tests
     grad, seg = pl.pallas_call(
         backward_kernel,
         out_shape=(
-            jax.ShapeDtypeStruct((tests, 2, share, NZ), f32),
+            pltpu.VMEM((tests, 2, share, NZ), f32),
             jax.ShapeDtypeStruct(measured.shape, f32),
         ),
-        in_specs=[vmem] * 13,
+        in_specs=[vmem] * 17,
         out_specs=(vmem, vmem),
         scratch_shapes=[
             pltpu.VMEM(field(STEPS, EXT), f32),
             pltpu.VMEM((NY, NZ), f32),
             pltpu.VMEM((5, CELLS, 2048), bf16),
-            pltpu.VMEM((5, CELLS, 2048), bf16),
+            *hots(2),
         ],
         compiler_params=params,
         name="backward",
-    )(*packs, temp, sums, *coefs)
+    )(near2, near1, *own_hots, *far_hots, *near_hots, temp, sums, *coefs)
     grad = lax.all_to_all(grad, "tests", split_axis=0, concat_axis=0, tiled=True)
     return jnp.sum(grad, axis=0), seg
 

time: 76.7 us -> 75.5 us (0.984)
  blocking collectives: 38.7 us -> 37.2 us
  Pallas kernels: 11.6 us -> 12.6 us
    all_to_all x1, blocking collectives: 26.6 us -> 25.4 us  [local(): lax.all_to_all(grad, 'tests', split_axis=0, concat_axis=0, tiled=True)]
    pallas_call x3 -> x6, Pallas kernels: 11.6 us -> 12.6 us  [the longest x1 5.96 us: local(): pl.pallas_call(backward_kernel, out_shape=(pltpu.VMEM((tests, 2, share, N...]
  transfers between devices with their start and end apart: 4 -> 4, of which waited for: 2 -> 2; matrix products, arithmetic and copies ran while one was open for 0% -> 0% of each run, Pallas kernels for 0% -> 1%
where the time goes in v3:
time: 75.5 us; the launch traced here: 75.2 us
  blocking collectives  37.2 us (49%)
  starting transfers between devices  13.5 us (18%)
  Pallas kernels  12.6 us (17%)
  waiting for transfers between devices  10.6 us (14%)
    all_to_all x1, blocking collectives, local(): lax.all_to_all(grad, 'tests', split_axis=0, concat_axis=0, tiled=True)  25.4 us
    all_to_all x1, blocking collectives, local(): sums = lax.all_to_all(sums, 'grid', split_axis=0, concat_axis=0, tiled=True)  11.8 us
    ppermute x1, waiting for transfers between devices, local(): far2 = lax.ppermute(pack, 'grid', to_far)  9.48 us
    ppermute x1, starting transfers between devices, local(): far2 = lax.ppermute(pack, 'grid', to_far)  7.73 us
    pallas_call x1, Pallas kernels, local(): pl.pallas_call(backward_kernel, out_shape=(pltpu.VMEM((tests, 2, share, N...  5.96 us
    pallas_call x1, Pallas kernels, local(): pl.pallas_call(forward_kernel, out_shape=tuple((pltpu.VMEM(shape, f32) fo...  4.49 us
    ppermute x1, starting transfers between devices, local(): far1 = lax.ppermute(pack, 'grid', swap)  1.92 us
    ppermute x1, starting transfers between devices, local(): near2 = lax.ppermute(pack_near, 'grid', to_near)  1.92 us
  transfers between devices with their start and end apart: 4, of which 2 were waited for; matrix products, arithmetic and copies ran while one was open for 0% of the time, Pallas kernels for 1%

profile of v3, /device:TPU:8, one launch (start us, length us, event | category | flops | bytes accessed | tf_op | source)
XLA Modules:
  0.0 75.2 jit_solution(15603405545393135494)
XLA Ops:
  0.6 1.3 %pack.1 = (f32[792,128]{1,0:T(8,128)S(1)}, f32[664,128]{1,0:T(8,128)S(1)}) custom-call(f32[2,128,128]{2,1,0:T(8,128)} %log_cond.1, f32[1,2,128,128]{3,2,1,0:T(8,128)} %opening.1, f32[1,2,128,128]{3,2,1,0:T(8,128)} %heat.1, s32[8,256]{1,0:T(8,128)} %bitcast.8, s32[1,256]{1,0:T(1,128)} %bitcast.9, f32[1,4]{1,0:T(1,128)} %measured.1), custom_call_target="tpu_custom_call" | custom-call | tf_op jit(solution)/shard_map/pack/pallas_call | solution.py:343
  2.0 7.7 %collective-permute-start.2 = (f32[792,128]{1,0:T(8,128)S(1)}, f32[792,128]{1,0:T(8,128)S(1)}, u32[]{:S(2)}, u32[]{:S(2)}) collective-permute-start(f32[792,128]{1,0:T(8,128)S(1)} %get-tuple-element.30.own), channel_id=1, source_target_pairs={{2,0},{4,2},{6,4},{8,6},{10,8},{12,10},{14,12},{16,14},{18,16},{20... | collective-permute-start | bytes 1216520 | tf_op jit(solution)/shard_map/ppermute | solution.py:360
  9.7 1.9 %collective-permute-start.1 = (f32[792,128]{1,0:T(8,128)S(1)}, f32[792,128]{1,0:T(8,128)S(1)}, u32[]{:S(2)}, u32[]{:S(2)}) collective-permute-start(f32[792,128]{1,0:T(8,128)S(1)} %get-tuple-element.30.own), channel_id=1, source_target_pairs={{0,1},{1,0},{2,3},{3,2},{4,5},{5,4},{6,7},{7,6},{8,9},{9,8},{10,11... | collective-permute-start | bytes 1216520 | tf_op jit(solution)/shard_map/ppermute | solution.py:361
  11.7 1.9 %collective-permute-start = (f32[664,128]{1,0:T(8,128)S(1)}, f32[664,128]{1,0:T(8,128)S(1)}, u32[]{:S(2)}, u32[]{:S(2)}) collective-permute-start(f32[664,128]{1,0:T(8,128)S(1)} %get-tuple-element.29), channel_id=1, source_target_pairs={{0,2},{2,4},{4,6},{6,8},{8,10},{10,12},{12,14},{14,16},{16,18},{18... | collective-permute-start | bytes 1019912 | tf_op jit(solution)/shard_map/ppermute | solution.py:362
  13.6 0.3 prepare_own.1
  13.9 9.5 %collective-permute-done.2.far2 = f32[792,128]{1,0:T(8,128)S(1)} collective-permute-done((f32[792,128]{1,0:T(8,128)S(1)}, f32[792,128]{1,0:T(8,128)S(1)}, u32[]{:S(2)}, u32[]{:S(2)}) %collective-permute-start.2) | collective-permute-done | bytes 405536 | tf_op jit(solution)/shard_map/ppermute | solution.py:360
  23.4 1.9 %collective-permute-start.3 = (f32[792,128]{1,0:T(8,128)S(1)}, f32[792,128]{1,0:T(8,128)S(1)}, u32[]{:S(2)}, u32[]{:S(2)}) collective-permute-start(f32[792,128]{1,0:T(8,128)S(1)} %collective-permute-done.2.far2), channel_id=1, source_target_pairs={{0,1},{1,0},{2,3},{3,2},{4,5},{5,4},{6,7},{7,6},{8,9},{9,8},{10,11... | collective-permute-start | bytes 1216520 | tf_op jit(solution)/shard_map/ppermute | solution.py:384
  25.3 0.0 collective-permute-done.1.far1
  25.3 0.6 prepare_far.1
  25.8 0.0 collective-permute-done.near2
  25.9 1.1 %collective-permute-done.3.near1 = f32[792,128]{1,0:T(8,128)S(1)} collective-permute-done((f32[792,128]{1,0:T(8,128)S(1)}, f32[792,128]{1,0:T(8,128)S(1)}, u32[]{:S(2)}, u32[]{:S(2)}) %collective-permute-start.3) | collective-permute-done | bytes 405536 | tf_op jit(solution)/shard_map/ppermute | solution.py:384
  27.0 4.5 %forward.1 = (f32[5,10,144,128]{3,2,1,0:T(8,128)S(1)}, f32[32,128]{1,0:T(8,128)S(1)}, f32[10,144,128]{2,1,0:T(8,128)S(1)}, f32[10,128,128]{2,1,0:T(8,128)S(1)}, ...) custom-call(f32[664,128]{1,0:T(8,128)S(1)} %collective-permute-done., ...), custom_call_target="tpu_custom_call" | custom-call | tf_op jit(solution)/shard_map/forward/pallas_call | solution.py:390
  31.5 11.8 %all_to_all.16 = f32[32,1,128]{2,1,0:T(1,128)S(1)} all-to-all(f32[32,1,128]{2,1,0:T(1,128)S(1)} %bitcast.7), channel_id=1, replica_groups=mesh['tests'=16,'grid'=32] {'grid'}, dimensions={0} | all-to-all | bytes 32768 | tf_op jit(solution)/shard_map/all_to_all | solution.py:399
  43.3 6.0 %backward.1 = (f32[16,2,8,128]{3,2,1,0:T(8,128)S(1)}, f32[1,4]{1,0:T(1,128)}) custom-call(f32[664,128]{1,0:T(8,128)S(1)} %collective-permute-done.near2, f32[792,128]{1,0:T(8,128)S(1)} %collective-permute-done.3.near1, bf16[1,256,2048]{2,1,0:T(8,128)(2,1)S(1)} %get-tuple-element.39.at_rows.own_rows, ...), custom_call_target="tpu_custom_call" | custom-call | tf_op jit(solution)/shard_map/backward/pallas_call | solution.py:401
  49.2 25.4 %all_to_all.17 = f32[16,2,8,128]{3,2,1,0:T(8,128)S(1)} all-to-all(f32[16,2,8,128]{3,2,1,0:T(8,128)S(1)} %get-tuple-element.54), channel_id=1, replica_groups=mesh['tests'=16,'grid'=32] {'tests'}, dimensions={0} | all-to-all | bytes 262144 | tf_op jit(solution)/shard_map/all_to_all | solution.py:418
  74.6 0.6 reduce_sum.9
  (1 shorter events, 0.0 us)
Async XLA Ops:
  2.0 21.4 %collective-permute-start.2 = (f32[792,128]{1,0:T(8,128)S(1)}, f32[792,128]{1,0:T(8,128)S(1)}, u32[]{:S(2)}, u32[]{:S(2)}) collective-permute-start(f32[792,128]{1,0:T(8,128)S(1)} %get-tuple-element.30.own), channel_id=1, source_target_pairs={{2,0},{4,2},{6,4},{8,6},{10,8},{12,10},{14,12},{16,14},{18,16},{20... | collective-permute-start | bytes 1216520 | tf_op jit(solution)/shard_map/ppermute | solution.py:360
  9.7 15.5 %collective-permute-start.1 = (f32[792,128]{1,0:T(8,128)S(1)}, f32[792,128]{1,0:T(8,128)S(1)}, u32[]{:S(2)}, u32[]{:S(2)}) collective-permute-start(f32[792,128]{1,0:T(8,128)S(1)} %get-tuple-element.30.own), channel_id=1, source_target_pairs={{0,1},{1,0},{2,3},{3,2},{4,5},{5,4},{6,7},{7,6},{8,9},{9,8},{10,11... | collective-permute-start | bytes 1216520 | tf_op jit(solution)/shard_map/ppermute | solution.py:361
  11.7 14.2 %collective-permute-start = (f32[664,128]{1,0:T(8,128)S(1)}, f32[664,128]{1,0:T(8,128)S(1)}, u32[]{:S(2)}, u32[]{:S(2)}) collective-permute-start(f32[664,128]{1,0:T(8,128)S(1)} %get-tuple-element.29), channel_id=1, source_target_pairs={{0,2},{2,4},{4,6},{6,8},{8,10},{10,12},{12,14},{14,16},{16,18},{18... | collective-permute-start | bytes 1019912 | tf_op jit(solution)/shard_map/ppermute | solution.py:362
  23.4 3.6 %collective-permute-start.3 = (f32[792,128]{1,0:T(8,128)S(1)}, f32[792,128]{1,0:T(8,128)S(1)}, u32[]{:S(2)}, u32[]{:S(2)}) collective-permute-start(f32[792,128]{1,0:T(8,128)S(1)} %collective-permute-done.2.far2), channel_id=1, source_target_pairs={{0,1},{1,0},{2,3},{3,2},{4,5},{5,4},{6,7},{7,6},{8,9},{9,8},{10,11... | collective-permute-start | bytes 1216520 | tf_op jit(solution)/shard_map/ppermute | solution.py:384

commit v4 on v3

--- a/solution.py
+++ b/solution.py
@@ -13,10 +13,8 @@
 NZ = 128
 CELLS = 2 * NY
 EXT = 10
-PAD = 8
-YP = NY + 2 * PAD
-MID = slice(PAD, PAD + NY)
-CH = 32
+SUB = 8
+BLOCKS = NY // SUB
 Q0 = 0
 U0 = NY
 C0 = U0 + CELLS
@@ -45,72 +43,68 @@
     return jnp.where(i < 4, near, jnp.where(i < 8, 1.0, far))
 
 
-def lane_masks(rows):
-    lane = lax.broadcasted_iota(jnp.int32, (rows, NZ), 1)
-    return lane < NZ - 1, lane > 0
-
-
-def ahead_z(values, keep):
-    return jnp.where(keep, pltpu.roll(values, NZ - 1, 1), 0.0)
-
-
-def behind_z(values, keep):
-    return jnp.where(keep, pltpu.roll(values, 1, 1), 0.0)
-
-
-def zero_pads(ref, lead):
-    ref[lead, 0:PAD] = jnp.zeros((PAD, NZ), f32)
-    ref[lead, PAD + NY : YP] = jnp.zeros((PAD, NZ), f32)
-
-
-def coefficients(cond, kx, ky, kzp, kzm, keep):
-    ahead_keep, behind_keep = lane_masks(CH)
+def part(n):
+    return pl.ds(SUB * n, SUB)
+
+
+def coordinates():
+    s = lax.broadcasted_iota(jnp.int32, (SUB, NZ), 0)
+    z = lax.broadcasted_iota(jnp.int32, (SUB, NZ), 1)
+    return s, z
+
+
+def coefficients(cond, kx, ky, kz, keep):
+    s, z = coordinates()
+    z_ends = jnp.where((z == 0) | (z == NZ - 1), WZ, 0.0)
+    first_ends = z_ends + jnp.where(s == 0, WX, 0.0)
+    last_ends = z_ends + jnp.where(s == SUB - 1, WX, 0.0)
+    z_inside = jnp.where(z < NZ - 1, WZ, 0.0)
+    s_inside = jnp.where(s < SUB - 1, WX, 0.0)
 
     def row(i, carry):
-        for y in range(0, NY, CH):
-            here = pl.ds(PAD + y, CH)
-            c = cond[i, here]
-            cxp, cxm = cond[i + 1, here], cond[i - 1, here]
-            cyp, cym = cond[i, pl.ds(PAD + y + 1, CH)], cond[i, pl.ds(PAD + y - 1, CH)]
-            czp, czm = ahead_z(c, ahead_keep), behind_z(c, behind_keep)
-            kx[i, pl.ds(y, CH)] = WX * (c + cxp)
-            face_y = WX * (c + cyp)
-            if y + CH == NY:
-                edge = lax.broadcasted_iota(jnp.int32, (CH, NZ), 0) == CH - 1
-                face_y = jnp.where(edge, 0.0, face_y)
-            ky[i, here] = face_y
-            kzp[i, pl.ds(y, CH)] = jnp.where(ahead_keep, WZ * (c + czp), 0.0)
-            kzm[i, pl.ds(y, CH)] = jnp.where(behind_keep, WZ * (c + czm), 0.0)
-            total = WX * (((cxp + cxm) + (cyp + cym)) + 4.0 * c) + WZ * ((czp + czm) + 2.0 * c)
-            keep[i, pl.ds(y, CH)] = 1.0 - total
-        ky[i, 0:PAD] = jnp.zeros((PAD, NZ), f32)
+        c = [cond[i, part(n)] for n in range(BLOCKS)]
+        for n in range(BLOCKS):
+            kx[i, part(n)] = WX * (c[n] + cond[i + 1, part(n)])
+            if n < BLOCKS - 1:
+                ky[i, part(n)] = WX * (c[n] + c[n + 1])
+            else:
+                ky[i, part(n)] = s_inside * (c[n] + pltpu.roll(c[0], SUB - 1, 0))
+            kz[i, part(n)] = z_inside * (c[n] + pltpu.roll(c[n], NZ - 1, 1))
+            ends = first_ends if n == 0 else (last_ends if n == BLOCKS - 1 else z_ends)
+            keep[i, part(n)] = 1.0 - ends * c[n]
         return carry
 
-    kx[0] = WX * (cond[0, MID] + cond[1, MID])
-    lax.fori_loop(1, 9, row, 0)
+    kx[0] = WX * (cond[0] + cond[1])
+    lax.fori_loop(1, EXT - 1, row, 0)
 
 
 def advance(src, dst, first, last, coefs, load, near, far):
-    kx, ky, kzp, kzm, keep = coefs
-
-    def row(i, carry):
+    kx, ky, kz, keep = coefs
+
+    def row(i, below):
         inside = row_validity(i, near, far)
-        for y in range(0, NY, CH):
-            here, flat = pl.ds(PAD + y, CH), pl.ds(y, CH)
-            u = src[i, here]
-            new = keep[i, flat] * u
-            new += kx[i, flat] * src[i + 1, here]
-            new += kx[i - 1, flat] * src[i - 1, here]
-            new += ky[i, here] * src[i, pl.ds(PAD + y + 1, CH)]
-            new += ky[i, pl.ds(PAD + y - 1, CH)] * src[i, pl.ds(PAD + y - 1, CH)]
-            new += kzp[i, flat] * pltpu.roll(u, NZ - 1, 1)
-            new += kzm[i, flat] * pltpu.roll(u, 1, 1)
+        u = [src[i, part(n)] for n in range(BLOCKS)]
+        wrap = ky[i, part(BLOCKS - 1)] * (pltpu.roll(u[0], SUB - 1, 0) - u[-1])
+        left = pltpu.roll(wrap, 1, 0)
+        above = []
+        for n in range(BLOCKS):
+            across = kx[i, part(n)] * (src[i + 1, part(n)] - u[n])
+            right = ky[i, part(n)] * (u[n + 1] - u[n]) if n < BLOCKS - 1 else wrap
+            side = kz[i, part(n)] * (pltpu.roll(u[n], NZ - 1, 1) - u[n])
+            new = keep[i, part(n)] * u[n] + (across - below[n])
+            new += (right - left) + (side - pltpu.roll(side, 1, 1))
             if load is not None:
-                new += load[i, flat]
-            dst[i, here] = new * inside
-        return carry
-
-    lax.fori_loop(first, last + 1, row, 0)
+                new += load[i, part(n)]
+            dst[i, part(n)] = new * inside
+            left = right
+            above.append(across)
+        return tuple(above)
+
+    i = first - 1
+    start = tuple(
+        kx[i, part(n)] * (src[i + 1, part(n)] - src[i, part(n)]) for n in range(BLOCKS)
+    )
+    lax.fori_loop(first, last + 1, row, start)
 
 
 def parts_of(values, count):
@@ -148,7 +142,10 @@
     return cells >> 7, cells & (NZ - 1), segment
 
 
-def pack_kernel(log_cond, opening, heat, cells, segment, measured, full, near, cells_v, segment_v, measured_v, sems):
+def pack_kernel(
+    log_cond, opening, heat, cells, segment, measured, full, near,
+    rows_v, cells_v, segment_v, measured_v, sems,
+):
     g, core, _, _ = position()
     copies = []
 
@@ -156,21 +153,32 @@
         copies.append(pltpu.make_async_copy(src, dst, sems.at[len(copies)]))
         copies[-1].start()
 
+    targets = []
     for r in range(2):
         at = r ^ core
-        for out, skip in ((full, 0), (near, NY)):
-            copy(opening.at[0, at], out.at[pl.ds(U0 - skip + r * NY, NY)])
-            copy(log_cond.at[at], out.at[pl.ds(C0 - skip + r * NY, NY)])
-            if r == 1:
-                copy(heat.at[0, at], out.at[pl.ds(Q1 - skip, NY)])
-            elif skip == 0:
-                copy(heat.at[0, at], out.at[pl.ds(Q0, NY)])
+        sources = (
+            (opening.at[0, at], U0 + r * NY),
+            (log_cond.at[at], C0 + r * NY),
+            (heat.at[0, at], Q1 if r else Q0),
+        )
+        for src, base in sources:
+            copy(src, rows_v.at[len(targets)])
+            targets.append(base)
     copy(cells, cells_v)
     copy(segment, segment_v)
     copy(measured, measured_v)
     for each in copies:
         each.wait()
-    flipped = (cells_v[...] ^ (core * NY * NZ)).astype(f32)
+    for number, base in enumerate(targets):
+        for n in range(BLOCKS):
+            vector = rows_v[number, pl.ds(n, SUB, stride=BLOCKS)]
+            full[pl.ds(base + SUB * n, SUB)] = vector
+            if base >= NY:
+                near[pl.ds(base - NY + SUB * n, SUB)] = vector
+    cell = cells_v[...] ^ (core * NY * NZ)
+    y = (cell >> 7) & (NY - 1)
+    y = (y & (BLOCKS - 1)) * SUB + (y >> 4)
+    moved = ((cell & (NY * NZ)) + y * NZ + (cell & (NZ - 1))).astype(f32)
     lane = lax.broadcasted_iota(jnp.int32, (8, 128), 1)
     row = lax.broadcasted_iota(jnp.int32, (8, 128), 0)
     seg = segment_v[...].astype(f32)
@@ -179,8 +187,8 @@
         mine = (row == 2) & (lane == measured.shape[1] * g + n)
         extra = jnp.where(mine, measured_v[0:1, n : n + 1], extra)
     for out, skip in ((full, 0), (near, NY)):
-        out[pl.ds(D0 - skip, 8)] = flipped[:, :128]
-        out[pl.ds(D0 - skip + 8, 8)] = flipped[:, 128:]
+        out[pl.ds(D0 - skip, 8)] = moved[:, :128]
+        out[pl.ds(D0 - skip + 8, 8)] = moved[:, 128:]
         out[pl.ds(D0 - skip + 16, 8)] = extra
 
 
@@ -218,29 +226,21 @@
 
 def forward_kernel(
     near2, near1, own, far1, far2, at_rows, at_lanes, at_segments,
-    temp, sums, cond, kx, ky, kzp, kzm, keep, load,
+    temp, sums, cond, kx, ky, kz, keep, load,
 ):
     near, far = validity()
     for i, (slab, skip, r) in enumerate(slab_rows(near2, near1, own, far1, far2)):
         valid = near if i < 4 else (far if i > 7 else 1.0)
-        temp[0, i, MID] = slab[pl.ds(U0 - skip + r * NY, NY)]
-        cond[i, MID] = jnp.exp(slab[pl.ds(C0 - skip + r * NY, NY)]) * valid
+        temp[0, i] = slab[pl.ds(U0 - skip + r * NY, NY)]
+        cond[i] = jnp.exp(slab[pl.ds(C0 - skip + r * NY, NY)]) * valid
         if 1 <= i <= 8:
             load[i] = DT * slab[pl.ds((Q1 - skip) if r else Q0, NY)]
-
-    def pads(i, carry):
-        zero_pads(cond, i)
-        for k in range(STEPS):
-            zero_pads(temp.at[k], i)
-        return carry
-
-    lax.fori_loop(0, EXT, pads, 0)
-    coefficients(cond, kx, ky, kzp, kzm, keep)
-    coefs = (kx, ky, kzp, kzm, keep)
+    coefs = (kx, ky, kz, keep)
+    coefficients(cond, *coefs)
     for k in range(STEPS):
         advance(temp.at[k], temp.at[k + 1], k + 1, 8 - k, coefs, load, near, far)
 
-    across = jnp.concatenate([temp[STEPS, 4, MID].T, temp[STEPS, 5, MID].T], axis=1)
+    across = jnp.concatenate([temp[STEPS, 4].T, temp[STEPS, 5].T], axis=1)
     stack = jnp.concatenate([part.astype(bf16) for part in parts_of(across, 3)], axis=0)
     picked = jnp.zeros((NZ, 256), f32)
     for c in range(8):
@@ -261,7 +261,7 @@
 
 def backward_kernel(
     near2, near1, own_rows, own_lanes, own_segments, far_rows, far_lanes, far_segments, near2_segments,
-    temp, sums, cond, kx, ky, kzp, kzm, keep, grad, seg,
+    temp, sums, cond, kx, ky, kz, keep, grad, seg,
     costate, acc, weights, near_rows, near_lanes, near_segments,
 ):
     g, core, _, _ = position()
@@ -288,38 +288,47 @@
             at_rows[n], weights[j], (((1,), (1,)), ((), ())), preferred_element_type=f32
         )
         out = out[:, :NZ] + out[:, NZ:]
-        costate[0, 2 * j, MID] = out[:NY]
-        costate[0, 2 * j + 1, MID] = out[NY:]
-
-    def pads(i, carry):
-        for k in range(STEPS):
-            zero_pads(costate.at[k], i)
-        return carry
-
-    lax.fori_loop(0, EXT, pads, 0)
-    coefs = (kx, ky, kzp, kzm, keep)
+        costate[0, 2 * j] = out[:NY]
+        costate[0, 2 * j + 1] = out[NY:]
+
+    coefs = (kx, ky, kz, keep)
     for k in range(STEPS - 1):
         advance(costate.at[k], costate.at[k + 1], k + 1, 8 - k, coefs, None, near, far)
-    ahead_keep, behind_keep = lane_masks(CH)
+    s, z = coordinates()
     share = grad.shape[2]
 
     def sensitivity(i, carry):
         at = (i - 4) ^ core
-        for y in range(0, NY, CH):
-            here = pl.ds(PAD + y, CH)
-            left, right = pl.ds(PAD + y - 1, CH), pl.ds(PAD + y + 1, CH)
-            total = jnp.zeros((CH, NZ), f32)
+
+        def products(n):
+            across = jnp.zeros((SUB, NZ), f32)
+            right, side, own = across, across, across
             for k in range(STEPS):
                 u, a = temp.at[k], costate.at[STEPS - 1 - k]
-                uc, ac = u[i, here], a[i, here]
-                total += (uc - u[i + 1, here]) * (ac - a[i + 1, here])
-                total += (uc - u[i - 1, here]) * (ac - a[i - 1, here])
-                total += (uc - u[i, right]) * (ac - a[i, right])
-                total += (uc - u[i, left]) * (ac - a[i, left])
-                side = (uc - ahead_z(uc, ahead_keep)) * (ac - ahead_z(ac, ahead_keep))
-                side += (uc - behind_z(uc, behind_keep)) * (ac - behind_z(ac, behind_keep))
-                total += 0.5 * side
-            acc[pl.ds(y, CH)] = (-WX) * cond[i, here] * total
+                uc, ac = u[i, part(n)], a[i, part(n)]
+                across += (uc - u[i + 1, part(n)]) * (ac - a[i + 1, part(n)])
+                across += (uc - u[i - 1, part(n)]) * (ac - a[i - 1, part(n)])
+                if n < BLOCKS - 1:
+                    ur, ar = u[i, part(n + 1)], a[i, part(n + 1)]
+                else:
+                    ur = jnp.where(s < SUB - 1, pltpu.roll(u[i, part(0)], SUB - 1, 0), 0.0)
+                    ar = jnp.where(s < SUB - 1, pltpu.roll(a[i, part(0)], SUB - 1, 0), 0.0)
+                right += (ur - uc) * (ar - ac)
+                us = jnp.where(z < NZ - 1, pltpu.roll(uc, NZ - 1, 1), 0.0)
+                az = jnp.where(z < NZ - 1, pltpu.roll(ac, NZ - 1, 1), 0.0)
+                side += (us - uc) * (az - ac)
+                own += uc * ac
+            side += jnp.where(z > 0, pltpu.roll(side, 1, 1), own)
+            return across + 0.5 * side, right, own
+
+        last, last_right, _ = products(BLOCKS - 1)
+        left = None
+        for n in range(BLOCKS):
+            total, right, own = products(n) if n < BLOCKS - 1 else (last, last_right, None)
+            if n == 0:
+                left = jnp.where(s > 0, pltpu.roll(last_right, 1, 0), own)
+            acc[pl.ds(n, SUB, stride=BLOCKS)] = (-WX) * cond[i, part(n)] * (total + (right + left))
+            left = right
         for n in range(NY // share):
             grad[n, at] = acc[pl.ds(n * share, share)]
         return carry
@@ -327,8 +336,8 @@
     lax.fori_loop(4, 6, sensitivity, 0)
 
 
-def field(*lead, pad=True):
-    return (*lead, YP if pad else NY, NZ)
+def field(*lead):
+    return (*lead, NY, NZ)
 
 
 def in_hbm(values):
@@ -346,10 +355,11 @@
         in_specs=[pl.BlockSpec(memory_space=pltpu.HBM)] * 6,
         out_specs=(vmem, vmem),
         scratch_shapes=[
+            pltpu.VMEM(field(6), f32),
             pltpu.VMEM((8, 256), jnp.int32),
             pltpu.VMEM((1, 256), jnp.int32),
             pltpu.VMEM(measured.shape, f32),
-            pltpu.SemaphoreType.DMA((14,)),
+            pltpu.SemaphoreType.DMA((9,)),
         ],
         compiler_params=params,
         name="pack",
@@ -386,13 +396,13 @@
     near_hots = prepare(prepare_near_kernel, hots(1)[2:], "prepare_near", near2, far_hots[2])
     near2, near_hots, far_hots = lax.optimization_barrier((near2, near_hots, far_hots))
     packs = (near2, near1, pack, far1, far2)
-    coefs = [field(EXT), field(EXT, pad=False), field(EXT), field(EXT, pad=False), field(EXT, pad=False), field(EXT, pad=False)]
+    coefs = [field(EXT)] * 5
     temp, sums, *coefs = pl.pallas_call(
         forward_kernel,
         out_shape=tuple(pltpu.VMEM(shape, f32) for shape in (field(STEPS + 1, EXT), (grid, 128), *coefs)),
         in_specs=[vmem] * 8,
-        out_specs=(vmem,) * 8,
-        scratch_shapes=[pltpu.VMEM(field(EXT, pad=False), f32)],
+        out_specs=(vmem,) * 7,
+        scratch_shapes=[pltpu.VMEM(field(EXT), f32)],
         compiler_params=params,
         name="forward",
     )(*packs, *own_hots)
@@ -404,7 +414,7 @@
             pltpu.VMEM((tests, 2, share, NZ), f32),
             jax.ShapeDtypeStruct(measured.shape, f32),
         ),
-        in_specs=[vmem] * 17,
+        in_specs=[vmem] * 16,
         out_specs=(vmem, vmem),
         scratch_shapes=[
             pltpu.VMEM(field(STEPS, EXT), f32),

time: 75.5 us -> 76.5 us (1.013)
  Pallas kernels: 12.6 us -> 13.6 us
where the time goes in v4:
time: 76.5 us; the launch traced here: 76.2 us
  blocking collectives  37.2 us (49%)
  Pallas kernels  13.6 us (18%)
  starting transfers between devices  13.5 us (18%)
  waiting for transfers between devices  10.6 us (14%)
    all_to_all x1, blocking collectives, local(): lax.all_to_all(grad, 'tests', split_axis=0, concat_axis=0, tiled=True)  25.4 us
    all_to_all x1, blocking collectives, local(): sums = lax.all_to_all(sums, 'grid', split_axis=0, concat_axis=0, tiled=True)  11.8 us
    ppermute x1, waiting for transfers between devices, local(): far2 = lax.ppermute(pack, 'grid', to_far)  9.48 us
    ppermute x1, starting transfers between devices, local(): far2 = lax.ppermute(pack, 'grid', to_far)  7.73 us
    pallas_call x1, Pallas kernels, local(): pl.pallas_call(backward_kernel, out_shape=(pltpu.VMEM((tests, 2, share, N...  6.64 us
    pallas_call x1, Pallas kernels, local(): pl.pallas_call(forward_kernel, out_shape=tuple((pltpu.VMEM(shape, f32) fo...  4.89 us
    ppermute x1, starting transfers between devices, local(): far1 = lax.ppermute(pack, 'grid', swap)  1.92 us
    ppermute x1, starting transfers between devices, local(): near2 = lax.ppermute(pack_near, 'grid', to_near)  1.92 us
  transfers between devices with their start and end apart: 4, of which 2 were waited for; matrix products, arithmetic and copies ran while one was open for 0% of the time, Pallas kernels for 1%

profile of v4, /device:TPU:8, one launch (start us, length us, event | category | flops | bytes accessed | tf_op | source)
XLA Modules:
  0.0 76.2 jit_solution(13626714621717429679)
XLA Ops:
  0.6 1.2 %pack.1 = (f32[792,128]{1,0:T(8,128)S(1)}, f32[664,128]{1,0:T(8,128)S(1)}) custom-call(f32[2,128,128]{2,1,0:T(8,128)} %log_cond.1, f32[1,2,128,128]{3,2,1,0:T(8,128)} %opening.1, f32[1,2,128,128]{3,2,1,0:T(8,128)} %heat.1, s32[8,256]{1,0:T(8,128)} %bitcast.8, s32[1,256]{1,0:T(1,128)} %bitcast.9, f32[1,4]{1,0:T(1,128)} %measured.1), custom_call_target="tpu_custom_call" | custom-call | tf_op jit(solution)/shard_map/pack/pallas_call | solution.py:352
  1.9 7.7 %collective-permute-start.2 = (f32[792,128]{1,0:T(8,128)S(1)}, f32[792,128]{1,0:T(8,128)S(1)}, u32[]{:S(2)}, u32[]{:S(2)}) collective-permute-start(f32[792,128]{1,0:T(8,128)S(1)} %get-tuple-element.29.own), channel_id=1, source_target_pairs={{2,0},{4,2},{6,4},{8,6},{10,8},{12,10},{14,12},{16,14},{18,16},{20... | collective-permute-start | bytes 1216520 | tf_op jit(solution)/shard_map/ppermute | solution.py:370
  9.6 1.9 %collective-permute-start.1 = (f32[792,128]{1,0:T(8,128)S(1)}, f32[792,128]{1,0:T(8,128)S(1)}, u32[]{:S(2)}, u32[]{:S(2)}) collective-permute-start(f32[792,128]{1,0:T(8,128)S(1)} %get-tuple-element.29.own), channel_id=1, source_target_pairs={{0,1},{1,0},{2,3},{3,2},{4,5},{5,4},{6,7},{7,6},{8,9},{9,8},{10,11... | collective-permute-start | bytes 1216520 | tf_op jit(solution)/shard_map/ppermute | solution.py:371
  11.5 1.9 %collective-permute-start = (f32[664,128]{1,0:T(8,128)S(1)}, f32[664,128]{1,0:T(8,128)S(1)}, u32[]{:S(2)}, u32[]{:S(2)}) collective-permute-start(f32[664,128]{1,0:T(8,128)S(1)} %get-tuple-element.28), channel_id=1, source_target_pairs={{0,2},{2,4},{4,6},{6,8},{8,10},{10,12},{12,14},{14,16},{16,18},{18... | collective-permute-start | bytes 1019912 | tf_op jit(solution)/shard_map/ppermute | solution.py:372
  13.5 0.3 prepare_own.1
  13.7 9.5 %collective-permute-done.2.far2 = f32[792,128]{1,0:T(8,128)S(1)} collective-permute-done((f32[792,128]{1,0:T(8,128)S(1)}, f32[792,128]{1,0:T(8,128)S(1)}, u32[]{:S(2)}, u32[]{:S(2)}) %collective-permute-start.2) | collective-permute-done | bytes 405536 | tf_op jit(solution)/shard_map/ppermute | solution.py:370
  23.2 1.9 %collective-permute-start.3 = (f32[792,128]{1,0:T(8,128)S(1)}, f32[792,128]{1,0:T(8,128)S(1)}, u32[]{:S(2)}, u32[]{:S(2)}) collective-permute-start(f32[792,128]{1,0:T(8,128)S(1)} %collective-permute-done.2.far2), channel_id=1, source_target_pairs={{0,1},{1,0},{2,3},{3,2},{4,5},{5,4},{6,7},{7,6},{8,9},{9,8},{10,11... | collective-permute-start | bytes 1216520 | tf_op jit(solution)/shard_map/ppermute | solution.py:394
  25.1 0.0 collective-permute-done.1.far1
  25.2 0.6 prepare_far.1
  25.7 0.0 collective-permute-done.near2
  25.8 1.1 %collective-permute-done.3.near1 = f32[792,128]{1,0:T(8,128)S(1)} collective-permute-done((f32[792,128]{1,0:T(8,128)S(1)}, f32[792,128]{1,0:T(8,128)S(1)}, u32[]{:S(2)}, u32[]{:S(2)}) %collective-permute-start.3) | collective-permute-done | bytes 405536 | tf_op jit(solution)/shard_map/ppermute | solution.py:394
  26.9 4.9 %forward.1 = (f32[5,10,128,128]{3,2,1,0:T(8,128)S(1)}, f32[32,128]{1,0:T(8,128)S(1)}, f32[10,128,128]{2,1,0:T(8,128)S(1)}, f32[10,128,128]{2,1,0:T(8,128)S(1)}, ...) custom-call(f32[664,128]{1,0:T(8,128)S(1)} %collective-permute-done.near2, ...), custom_call_target="tpu_custom_call" | custom-call | tf_op jit(solution)/shard_map/forward/pallas_call | solution.py:400
  31.7 11.8 %all_to_all.16 = f32[32,1,128]{2,1,0:T(1,128)S(1)} all-to-all(f32[32,1,128]{2,1,0:T(1,128)S(1)} %bitcast.7), channel_id=1, replica_groups=mesh['tests'=16,'grid'=32] {'grid'}, dimensions={0} | all-to-all | bytes 32768 | tf_op jit(solution)/shard_map/all_to_all | solution.py:409
  43.6 6.6 %backward.1 = (f32[16,2,8,128]{3,2,1,0:T(8,128)S(1)}, f32[1,4]{1,0:T(1,128)}) custom-call(f32[664,128]{1,0:T(8,128)S(1)} %collective-permute-done.near2, f32[792,128]{1,0:T(8,128)S(1)} %collective-permute-done.3.near1, bf16[1,256,2048]{2,1,0:T(8,128)(2,1)S(1)} %get-tuple-element.38.at_rows.own_rows, ...), custom_call_target="tpu_custom_call" | custom-call | tf_op jit(solution)/shard_map/backward/pallas_call | solution.py:411
  50.2 25.4 %all_to_all.17 = f32[16,2,8,128]{3,2,1,0:T(8,128)S(1)} all-to-all(f32[16,2,8,128]{3,2,1,0:T(8,128)S(1)} %get-tuple-element.52), channel_id=1, replica_groups=mesh['tests'=16,'grid'=32] {'tests'}, dimensions={0} | all-to-all | bytes 262144 | tf_op jit(solution)/shard_map/all_to_all | solution.py:428
  75.6 0.6 reduce_sum.9
  (1 shorter events, 0.0 us)
Async XLA Ops:
  1.9 21.4 %collective-permute-start.2 = (f32[792,128]{1,0:T(8,128)S(1)}, f32[792,128]{1,0:T(8,128)S(1)}, u32[]{:S(2)}, u32[]{:S(2)}) collective-permute-start(f32[792,128]{1,0:T(8,128)S(1)} %get-tuple-element.29.own), channel_id=1, source_target_pairs={{2,0},{4,2},{6,4},{8,6},{10,8},{12,10},{14,12},{16,14},{18,16},{20... | collective-permute-start | bytes 1216520 | tf_op jit(solution)/shard_map/ppermute | solution.py:370
  9.6 15.5 %collective-permute-start.1 = (f32[792,128]{1,0:T(8,128)S(1)}, f32[792,128]{1,0:T(8,128)S(1)}, u32[]{:S(2)}, u32[]{:S(2)}) collective-permute-start(f32[792,128]{1,0:T(8,128)S(1)} %get-tuple-element.29.own), channel_id=1, source_target_pairs={{0,1},{1,0},{2,3},{3,2},{4,5},{5,4},{6,7},{7,6},{8,9},{9,8},{10,11... | collective-permute-start | bytes 1216520 | tf_op jit(solution)/shard_map/ppermute | solution.py:371
  11.5 14.2 %collective-permute-start = (f32[664,128]{1,0:T(8,128)S(1)}, f32[664,128]{1,0:T(8,128)S(1)}, u32[]{:S(2)}, u32[]{:S(2)}) collective-permute-start(f32[664,128]{1,0:T(8,128)S(1)} %get-tuple-element.28), channel_id=1, source_target_pairs={{0,2},{2,4},{4,6},{6,8},{8,10},{10,12},{12,14},{14,16},{16,18},{18... | collective-permute-start | bytes 1019912 | tf_op jit(solution)/shard_map/ppermute | solution.py:372
  23.2 3.6 %collective-permute-start.3 = (f32[792,128]{1,0:T(8,128)S(1)}, f32[792,128]{1,0:T(8,128)S(1)}, u32[]{:S(2)}, u32[]{:S(2)}) collective-permute-start(f32[792,128]{1,0:T(8,128)S(1)} %collective-permute-done.2.far2), channel_id=1, source_target_pairs={{0,1},{1,0},{2,3},{3,2},{4,5},{5,4},{6,7},{7,6},{8,9},{9,8},{10,11... | collective-permute-start | bytes 1216520 | tf_op jit(solution)/shard_map/ppermute | solution.py:394

commit v5 on v4

--- a/solution.py
+++ b/solution.py
@@ -53,58 +53,83 @@
     return s, z
 
 
-def coefficients(cond, kx, ky, kz, keep):
+def coefficients(cond, kx, ky, kzp, kzm, keep):
     s, z = coordinates()
-    z_ends = jnp.where((z == 0) | (z == NZ - 1), WZ, 0.0)
-    first_ends = z_ends + jnp.where(s == 0, WX, 0.0)
-    last_ends = z_ends + jnp.where(s == SUB - 1, WX, 0.0)
-    z_inside = jnp.where(z < NZ - 1, WZ, 0.0)
+    z_above, z_below = jnp.where(z < NZ - 1, WZ, 0.0), jnp.where(z > 0, WZ, 0.0)
     s_inside = jnp.where(s < SUB - 1, WX, 0.0)
-
-    def row(i, carry):
-        c = [cond[i, part(n)] for n in range(BLOCKS)]
+    first_end, last_end = jnp.where(s == 0, WX, 0.0), jnp.where(s == SUB - 1, WX, 0.0)
+
+    def rows(b, carry):
+        first = 1 + 2 * b
+        for i in (first, first + 1):
+            c = [cond[i, part(n)] for n in range(BLOCKS)]
+            for n in range(BLOCKS):
+                kx[i, part(n)] = WX * (c[n] + cond[i + 1, part(n)])
+                if n < BLOCKS - 1:
+                    ky[i, part(n)] = WX * (c[n] + c[n + 1])
+                else:
+                    ky[i, part(n)] = s_inside * (c[n] + pltpu.roll(c[0], SUB - 1, 0))
+                above = z_above * (c[n] + pltpu.roll(c[n], NZ - 1, 1))
+                below = z_below * (c[n] + pltpu.roll(c[n], 1, 1))
+                kzp[i, part(n)], kzm[i, part(n)] = above, below
+                ends = jnp.where((z == 0) | (z == NZ - 1), WZ, 0.0)
+                if n == 0:
+                    ends = ends + first_end
+                elif n == BLOCKS - 1:
+                    ends = ends + last_end
+                keep[i, part(n)] = 1.0 - ((above + below) + ends * c[n])
+        return carry
+
+    kx[0] = WX * (cond[0] + cond[1])
+    lax.fori_loop(0, EXT // 2 - 1, rows, 0)
+
+
+def advance(src, dst, first, last, coefs, load, near, far):
+    kx, ky, kzp, kzm, keep = coefs
+    count = last - first + 1
+    group = 3 if count % 3 == 0 else min(count, 4)
+
+    def rows(b, carry):
+        base = first + group * b
+        places = range(group)
+        inside = [row_validity(base + r, near, far) for r in places]
+        u = [src[base + r, part(0)] for r in places]
+        wrap = [
+            ky[base + r, part(BLOCKS - 1)]
+            * (pltpu.roll(u[r], SUB - 1, 0) - src[base + r, part(BLOCKS - 1)])
+            for r in places
+        ]
+        left = [pltpu.roll(each, 1, 0) for each in wrap]
         for n in range(BLOCKS):
-            kx[i, part(n)] = WX * (c[n] + cond[i + 1, part(n)])
-            if n < BLOCKS - 1:
-                ky[i, part(n)] = WX * (c[n] + c[n + 1])
-            else:
-                ky[i, part(n)] = s_inside * (c[n] + pltpu.roll(c[0], SUB - 1, 0))
-            kz[i, part(n)] = z_inside * (c[n] + pltpu.roll(c[n], NZ - 1, 1))
-            ends = first_ends if n == 0 else (last_ends if n == BLOCKS - 1 else z_ends)
-            keep[i, part(n)] = 1.0 - ends * c[n]
+            below = kx[base - 1, part(n)] * (u[0] - src[base - 1, part(n)])
+            following = wrap
+            for r in places:
+                i = base + r
+                beyond = u[r + 1] if r < group - 1 else src[i + 1, part(n)]
+                across = kx[i, part(n)] * (beyond - u[r])
+                new = keep[i, part(n)] * u[r] + (across - below)
+                new += kzp[i, part(n)] * pltpu.roll(u[r], NZ - 1, 1)
+                new += kzm[i, part(n)] * pltpu.roll(u[r], 1, 1)
+                if load is not None:
+                    new += load[i, part(n)]
+                below = across
+                if n < BLOCKS - 1:
+                    after = src[i, part(n + 1)]
+                    right = ky[i, part(n)] * (after - u[r])
+                else:
+                    after, right = None, wrap[r]
+                dst[i, part(n)] = (new + (right - left[r])) * inside[r]
+                left[r] = right
+                if r == 0:
+                    following = []
+                following.append(after)
+            u = following
         return carry
 
-    kx[0] = WX * (cond[0] + cond[1])
-    lax.fori_loop(1, EXT - 1, row, 0)
-
-
-def advance(src, dst, first, last, coefs, load, near, far):
-    kx, ky, kz, keep = coefs
-
-    def row(i, below):
-        inside = row_validity(i, near, far)
-        u = [src[i, part(n)] for n in range(BLOCKS)]
-        wrap = ky[i, part(BLOCKS - 1)] * (pltpu.roll(u[0], SUB - 1, 0) - u[-1])
-        left = pltpu.roll(wrap, 1, 0)
-        above = []
-        for n in range(BLOCKS):
-            across = kx[i, part(n)] * (src[i + 1, part(n)] - u[n])
-            right = ky[i, part(n)] * (u[n + 1] - u[n]) if n < BLOCKS - 1 else wrap
-            side = kz[i, part(n)] * (pltpu.roll(u[n], NZ - 1, 1) - u[n])
-            new = keep[i, part(n)] * u[n] + (across - below[n])
-            new += (right - left) + (side - pltpu.roll(side, 1, 1))
-            if load is not None:
-                new += load[i, part(n)]
-            dst[i, part(n)] = new * inside
-            left = right
-            above.append(across)
-        return tuple(above)
-
-    i = first - 1
-    start = tuple(
-        kx[i, part(n)] * (src[i + 1, part(n)] - src[i, part(n)]) for n in range(BLOCKS)
-    )
-    lax.fori_loop(first, last + 1, row, start)
+    if group == count:
+        rows(0, 0)
+    else:
+        lax.fori_loop(0, count // group, rows, 0)
 
 
 def parts_of(values, count):
@@ -226,21 +251,22 @@
 
 def forward_kernel(
     near2, near1, own, far1, far2, at_rows, at_lanes, at_segments,
-    temp, sums, cond, kx, ky, kz, keep, load,
+    temp0, temp1, temp2, temp3, temp4, cond, kx, ky, kzp, kzm, keep, sums, load,
 ):
     near, far = validity()
+    temp = (temp0, temp1, temp2, temp3, temp4)
     for i, (slab, skip, r) in enumerate(slab_rows(near2, near1, own, far1, far2)):
         valid = near if i < 4 else (far if i > 7 else 1.0)
-        temp[0, i] = slab[pl.ds(U0 - skip + r * NY, NY)]
+        temp0[i] = slab[pl.ds(U0 - skip + r * NY, NY)]
         cond[i] = jnp.exp(slab[pl.ds(C0 - skip + r * NY, NY)]) * valid
         if 1 <= i <= 8:
             load[i] = DT * slab[pl.ds((Q1 - skip) if r else Q0, NY)]
-    coefs = (kx, ky, kz, keep)
+    coefs = (kx, ky, kzp, kzm, keep)
     coefficients(cond, *coefs)
     for k in range(STEPS):
-        advance(temp.at[k], temp.at[k + 1], k + 1, 8 - k, coefs, load, near, far)
-
-    across = jnp.concatenate([temp[STEPS, 4].T, temp[STEPS, 5].T], axis=1)
+        advance(temp[k], temp[k + 1], k + 1, 8 - k, coefs, load, near, far)
+
+    across = jnp.concatenate([temp4[4].T, temp4[5].T], axis=1)
     stack = jnp.concatenate([part.astype(bf16) for part in parts_of(across, 3)], axis=0)
     picked = jnp.zeros((NZ, 256), f32)
     for c in range(8):
@@ -261,11 +287,12 @@
 
 def backward_kernel(
     near2, near1, own_rows, own_lanes, own_segments, far_rows, far_lanes, far_segments, near2_segments,
-    temp, sums, cond, kx, ky, kz, keep, grad, seg,
-    costate, acc, weights, near_rows, near_lanes, near_segments,
+    sums, temp0, temp1, temp2, temp3, cond, kx, ky, kzp, kzm, keep, grad, seg,
+    costate4, costate3, costate2, costate1, acc, weights, near_rows, near_lanes, near_segments,
 ):
     g, core, _, _ = position()
     near, far = validity()
+    temp, costate = (temp0, temp1, temp2, temp3), (costate4, costate3, costate2, costate1)
     resid = jnp.sum(sums[...], axis=0, keepdims=True)
     shift = lax.rem(128 - seg.shape[1] * g, 128)
     seg[...] = pltpu.roll(jnp.broadcast_to(resid, (8, 128)), shift, 1)[0:1, 0 : seg.shape[1]]
@@ -288,12 +315,12 @@
             at_rows[n], weights[j], (((1,), (1,)), ((), ())), preferred_element_type=f32
         )
         out = out[:, :NZ] + out[:, NZ:]
-        costate[0, 2 * j] = out[:NY]
-        costate[0, 2 * j + 1] = out[NY:]
-
-    coefs = (kx, ky, kz, keep)
+        costate4[2 * j] = out[:NY]
+        costate4[2 * j + 1] = out[NY:]
+
+    coefs = (kx, ky, kzp, kzm, keep)
     for k in range(STEPS - 1):
-        advance(costate.at[k], costate.at[k + 1], k + 1, 8 - k, coefs, None, near, far)
+        advance(costate[k], costate[k + 1], k + 1, 8 - k, coefs, None, near, far)
     s, z = coordinates()
     share = grad.shape[2]
 
@@ -304,7 +331,7 @@
             across = jnp.zeros((SUB, NZ), f32)
             right, side, own = across, across, across
             for k in range(STEPS):
-                u, a = temp.at[k], costate.at[STEPS - 1 - k]
+                u, a = temp[k], costate[STEPS - 1 - k]
                 uc, ac = u[i, part(n)], a[i, part(n)]
                 across += (uc - u[i + 1, part(n)]) * (ac - a[i + 1, part(n)])
                 across += (uc - u[i - 1, part(n)]) * (ac - a[i - 1, part(n)])
@@ -396,12 +423,13 @@
     near_hots = prepare(prepare_near_kernel, hots(1)[2:], "prepare_near", near2, far_hots[2])
     near2, near_hots, far_hots = lax.optimization_barrier((near2, near_hots, far_hots))
     packs = (near2, near1, pack, far1, far2)
-    coefs = [field(EXT)] * 5
-    temp, sums, *coefs = pl.pallas_call(
+    coefs = [field(EXT)] * 6
+    levels = [field(EXT)] * (STEPS + 1)
+    *results, sums = pl.pallas_call(
         forward_kernel,
-        out_shape=tuple(pltpu.VMEM(shape, f32) for shape in (field(STEPS + 1, EXT), (grid, 128), *coefs)),
+        out_shape=tuple(pltpu.VMEM(shape, f32) for shape in (*levels, *coefs, (grid, 128))),
         in_specs=[vmem] * 8,
-        out_specs=(vmem,) * 7,
+        out_specs=(vmem,) * 12,
         scratch_shapes=[pltpu.VMEM(field(EXT), f32)],
         compiler_params=params,
         name="forward",
@@ -414,17 +442,17 @@
             pltpu.VMEM((tests, 2, share, NZ), f32),
             jax.ShapeDtypeStruct(measured.shape, f32),
         ),
-        in_specs=[vmem] * 16,
+        in_specs=[vmem] * 20,
         out_specs=(vmem, vmem),
         scratch_shapes=[
-            pltpu.VMEM(field(STEPS, EXT), f32),
+            *[pltpu.VMEM(field(EXT), f32)] * STEPS,
             pltpu.VMEM((NY, NZ), f32),
             pltpu.VMEM((5, CELLS, 2048), bf16),
             *hots(2),
         ],
         compiler_params=params,
         name="backward",
-    )(near2, near1, *own_hots, *far_hots, *near_hots, temp, sums, *coefs)
+    )(near2, near1, *own_hots, *far_hots, *near_hots, sums, *results[:STEPS], *results[STEPS + 1 :])
     grad = lax.all_to_all(grad, "tests", split_axis=0, concat_axis=0, tiled=True)
     return jnp.sum(grad, axis=0), seg
 

time: 76.5 us -> 73.4 us (0.959)
  Pallas kernels: 13.6 us -> 10.6 us
    pallas_call x1, Pallas kernels: 6.64 us -> 5.1 us  [local(): pl.pallas_call(backward_kernel, out_shape=(pltpu.VMEM((tests, 2, share, N...]
    pallas_call x1, Pallas kernels: 4.89 us -> 3.38 us  [local(): pl.pallas_call(forward_kernel, out_shape=tuple((pltpu.VMEM(shape, f32) fo...]
where the time goes in v5:
time: 73.4 us; the launch traced here: 73.1 us
  blocking collectives  37.2 us (51%)
  starting transfers between devices  13.5 us (18%)
  Pallas kernels  10.6 us (14%)
  waiting for transfers between devices  10.6 us (14%)
    all_to_all x1, blocking collectives, local(): lax.all_to_all(grad, 'tests', split_axis=0, concat_axis=0, tiled=True)  25.4 us
    all_to_all x1, blocking collectives, local(): sums = lax.all_to_all(sums, 'grid', split_axis=0, concat_axis=0, tiled=True)  11.8 us
    ppermute x1, waiting for transfers between devices, local(): far2 = lax.ppermute(pack, 'grid', to_far)  9.48 us
    ppermute x1, starting transfers between devices, local(): far2 = lax.ppermute(pack, 'grid', to_far)  7.73 us
    pallas_call x1, Pallas kernels, local(): pl.pallas_call(backward_kernel, out_shape=(pltpu.VMEM((tests, 2, share, N...  5.1 us
    pallas_call x1, Pallas kernels, local(): pl.pallas_call(forward_kernel, out_shape=tuple((pltpu.VMEM(shape, f32) fo...  3.38 us
    ppermute x1, starting transfers between devices, local(): far1 = lax.ppermute(pack, 'grid', swap)  1.92 us
    ppermute x1, starting transfers between devices, local(): near2 = lax.ppermute(pack_near, 'grid', to_near)  1.92 us
  transfers between devices with their start and end apart: 4, of which 2 were waited for; matrix products, arithmetic and copies ran while one was open for 0% of the time, Pallas kernels for 1%

profile of v5, /device:TPU:8, one launch (start us, length us, event | category | flops | bytes accessed | tf_op | source)
XLA Modules:
  0.0 73.1 jit_solution(2493482379485089679)
XLA Ops:
  0.6 1.2 %pack.1 = (f32[792,128]{1,0:T(8,128)S(1)}, f32[664,128]{1,0:T(8,128)S(1)}) custom-call(f32[2,128,128]{2,1,0:T(8,128)} %log_cond.1, f32[1,2,128,128]{3,2,1,0:T(8,128)} %opening.1, f32[1,2,128,128]{3,2,1,0:T(8,128)} %heat.1, s32[8,256]{1,0:T(8,128)} %bitcast.8, s32[1,256]{1,0:T(1,128)} %bitcast.9, f32[1,4]{1,0:T(1,128)} %measured.1), custom_call_target="tpu_custom_call" | custom-call | tf_op jit(solution)/shard_map/pack/pallas_call | solution.py:379
  1.9 7.7 %collective-permute-start.2 = (f32[792,128]{1,0:T(8,128)S(1)}, f32[792,128]{1,0:T(8,128)S(1)}, u32[]{:S(2)}, u32[]{:S(2)}) collective-permute-start(f32[792,128]{1,0:T(8,128)S(1)} %get-tuple-element.33.own), channel_id=1, source_target_pairs={{2,0},{4,2},{6,4},{8,6},{10,8},{12,10},{14,12},{16,14},{18,16},{20... | collective-permute-start | bytes 1216520 | tf_op jit(solution)/shard_map/ppermute | solution.py:397
  9.6 1.9 %collective-permute-start.1 = (f32[792,128]{1,0:T(8,128)S(1)}, f32[792,128]{1,0:T(8,128)S(1)}, u32[]{:S(2)}, u32[]{:S(2)}) collective-permute-start(f32[792,128]{1,0:T(8,128)S(1)} %get-tuple-element.33.own), channel_id=1, source_target_pairs={{0,1},{1,0},{2,3},{3,2},{4,5},{5,4},{6,7},{7,6},{8,9},{9,8},{10,11... | collective-permute-start | bytes 1216520 | tf_op jit(solution)/shard_map/ppermute | solution.py:398
  11.5 1.9 %collective-permute-start = (f32[664,128]{1,0:T(8,128)S(1)}, f32[664,128]{1,0:T(8,128)S(1)}, u32[]{:S(2)}, u32[]{:S(2)}) collective-permute-start(f32[664,128]{1,0:T(8,128)S(1)} %get-tuple-element.32), channel_id=1, source_target_pairs={{0,2},{2,4},{4,6},{6,8},{8,10},{10,12},{12,14},{14,16},{16,18},{18... | collective-permute-start | bytes 1019912 | tf_op jit(solution)/shard_map/ppermute | solution.py:399
  13.5 0.3 prepare_own.1
  13.7 9.5 %collective-permute-done.2.far2 = f32[792,128]{1,0:T(8,128)S(1)} collective-permute-done((f32[792,128]{1,0:T(8,128)S(1)}, f32[792,128]{1,0:T(8,128)S(1)}, u32[]{:S(2)}, u32[]{:S(2)}) %collective-permute-start.2) | collective-permute-done | bytes 405536 | tf_op jit(solution)/shard_map/ppermute | solution.py:397
  23.2 1.9 %collective-permute-start.3 = (f32[792,128]{1,0:T(8,128)S(1)}, f32[792,128]{1,0:T(8,128)S(1)}, u32[]{:S(2)}, u32[]{:S(2)}) collective-permute-start(f32[792,128]{1,0:T(8,128)S(1)} %collective-permute-done.2.far2), channel_id=1, source_target_pairs={{0,1},{1,0},{2,3},{3,2},{4,5},{5,4},{6,7},{7,6},{8,9},{9,8},{10,11... | collective-permute-start | bytes 1216520 | tf_op jit(solution)/shard_map/ppermute | solution.py:421
  25.1 0.0 collective-permute-done.1.far1
  25.2 0.6 prepare_far.1
  25.7 0.0 collective-permute-done.near2
  25.8 1.1 %collective-permute-done.3.near1 = f32[792,128]{1,0:T(8,128)S(1)} collective-permute-done((f32[792,128]{1,0:T(8,128)S(1)}, f32[792,128]{1,0:T(8,128)S(1)}, u32[]{:S(2)}, u32[]{:S(2)}) %collective-permute-start.3) | collective-permute-done | bytes 405536 | tf_op jit(solution)/shard_map/ppermute | solution.py:421
  26.9 3.4 %forward.1 = (f32[10,128,128]{2,1,0:T(8,128)S(1)}, f32[10,128,128]{2,1,0:T(8,128)S(1)}, f32[10,128,128]{2,1,0:T(8,128)S(1)}, f32[10,128,128]{2,1,0:T(8,128)S(1)}...) custom-call(f32[664,128]{1,0:T(8,128)S(1)} %collective-permute-done., ...), custom_call_target="tpu_custom_call" | custom-call | tf_op jit(solution)/shard_map/forward/pallas_call | solution.py:428
  30.2 11.8 %all_to_all.16 = f32[32,1,128]{2,1,0:T(1,128)S(1)} all-to-all(f32[32,1,128]{2,1,0:T(1,128)S(1)} %bitcast.7), channel_id=1, replica_groups=mesh['tests'=16,'grid'=32] {'grid'}, dimensions={0} | all-to-all | bytes 32768 | tf_op jit(solution)/shard_map/all_to_all | solution.py:437
  42.0 5.1 %backward.1 = (f32[16,2,8,128]{3,2,1,0:T(8,128)S(1)}, f32[1,4]{1,0:T(1,128)}) custom-call(f32[664,128]{1,0:T(8,128)S(1)} %collective-permute-done.near2, f32[792,128]{1,0:T(8,128)S(1)} %collective-permute-done.3.near1, bf16[1,256,2048]{2,1,0:T(8,128)(2,1)S(1)} %get-tuple-element.42.at_rows.own_rows, ...), custom_call_target="tpu_custom_call" | custom-call | tf_op jit(solution)/shard_map/backward/pallas_call | solution.py:439
  47.1 25.4 %all_to_all.17 = f32[16,2,8,128]{3,2,1,0:T(8,128)S(1)} all-to-all(f32[16,2,8,128]{3,2,1,0:T(8,128)S(1)} %get-tuple-element.60), channel_id=1, replica_groups=mesh['tests'=16,'grid'=32] {'tests'}, dimensions={0} | all-to-all | bytes 262144 | tf_op jit(solution)/shard_map/all_to_all | solution.py:456
  72.5 0.6 reduce_sum.9
  (1 shorter events, 0.0 us)
Async XLA Ops:
  1.9 21.4 %collective-permute-start.2 = (f32[792,128]{1,0:T(8,128)S(1)}, f32[792,128]{1,0:T(8,128)S(1)}, u32[]{:S(2)}, u32[]{:S(2)}) collective-permute-start(f32[792,128]{1,0:T(8,128)S(1)} %get-tuple-element.33.own), channel_id=1, source_target_pairs={{2,0},{4,2},{6,4},{8,6},{10,8},{12,10},{14,12},{16,14},{18,16},{20... | collective-permute-start | bytes 1216520 | tf_op jit(solution)/shard_map/ppermute | solution.py:397
  9.6 15.5 %collective-permute-start.1 = (f32[792,128]{1,0:T(8,128)S(1)}, f32[792,128]{1,0:T(8,128)S(1)}, u32[]{:S(2)}, u32[]{:S(2)}) collective-permute-start(f32[792,128]{1,0:T(8,128)S(1)} %get-tuple-element.33.own), channel_id=1, source_target_pairs={{0,1},{1,0},{2,3},{3,2},{4,5},{5,4},{6,7},{7,6},{8,9},{9,8},{10,11... | collective-permute-start | bytes 1216520 | tf_op jit(solution)/shard_map/ppermute | solution.py:398
  11.5 14.2 %collective-permute-start = (f32[664,128]{1,0:T(8,128)S(1)}, f32[664,128]{1,0:T(8,128)S(1)}, u32[]{:S(2)}, u32[]{:S(2)}) collective-permute-start(f32[664,128]{1,0:T(8,128)S(1)} %get-tuple-element.32), channel_id=1, source_target_pairs={{0,2},{2,4},{4,6},{6,8},{8,10},{10,12},{12,14},{14,16},{16,18},{18... | collective-permute-start | bytes 1019912 | tf_op jit(solution)/shard_map/ppermute | solution.py:399
  23.2 3.6 %collective-permute-start.3 = (f32[792,128]{1,0:T(8,128)S(1)}, f32[792,128]{1,0:T(8,128)S(1)}, u32[]{:S(2)}, u32[]{:S(2)}) collective-permute-start(f32[792,128]{1,0:T(8,128)S(1)} %collective-permute-done.2.far2), channel_id=1, source_target_pairs={{0,1},{1,0},{2,3},{3,2},{4,5},{5,4},{6,7},{7,6},{8,9},{9,8},{10,11... | collective-permute-start | bytes 1216520 | tf_op jit(solution)/shard_map/ppermute | solution.py:421

commit v6 on v5

--- a/solution.py
+++ b/solution.py
@@ -21,6 +21,10 @@
 D0 = C0 + CELLS
 Q1 = D0 + 24
 PACK = Q1 + NY
+PARTLY = NY
+NEAR_C0 = 2 * NY
+NEAR_D0 = 4 * NY
+NEAR_PACK = NEAR_D0 + 24
 COST_ESTIMATE = 2_000_000_000
 bf16 = jnp.bfloat16
 f32 = jnp.float32
@@ -168,7 +172,7 @@
 
 
 def pack_kernel(
-    log_cond, opening, heat, cells, segment, measured, full, near,
+    log_cond, opening, heat, cells, segment, measured, full,
     rows_v, cells_v, segment_v, measured_v, sems,
 ):
     g, core, _, _ = position()
@@ -196,10 +200,7 @@
         each.wait()
     for number, base in enumerate(targets):
         for n in range(BLOCKS):
-            vector = rows_v[number, pl.ds(n, SUB, stride=BLOCKS)]
-            full[pl.ds(base + SUB * n, SUB)] = vector
-            if base >= NY:
-                near[pl.ds(base - NY + SUB * n, SUB)] = vector
+            full[pl.ds(base + SUB * n, SUB)] = rows_v[number, pl.ds(n, SUB, stride=BLOCKS)]
     cell = cells_v[...] ^ (core * NY * NZ)
     y = (cell >> 7) & (NY - 1)
     y = (y & (BLOCKS - 1)) * SUB + (y >> 4)
@@ -211,10 +212,40 @@
     for n in range(measured.shape[1]):
         mine = (row == 2) & (lane == measured.shape[1] * g + n)
         extra = jnp.where(mine, measured_v[0:1, n : n + 1], extra)
-    for out, skip in ((full, 0), (near, NY)):
-        out[pl.ds(D0 - skip, 8)] = moved[:, :128]
-        out[pl.ds(D0 - skip + 8, 8)] = moved[:, 128:]
-        out[pl.ds(D0 - skip + 16, 8)] = extra
+    full[D0 : D0 + 8] = moved[:, :128]
+    full[D0 + 8 : D0 + 16] = moved[:, 128:]
+    full[D0 + 16 : D0 + 24] = extra
+
+
+def pack_near_kernel(full, near):
+    s, z = coordinates()
+    z_above, z_below = jnp.where(z < NZ - 1, WZ, 0.0), jnp.where(z > 0, WZ, 0.0)
+    z_ends = jnp.where((z == 0) | (z == NZ - 1), WZ, 0.0)
+
+    def at(base, n):
+        return full[pl.ds(base + SUB * n, SUB)]
+
+    def turned(last, first):
+        return jnp.where(s < SUB - 1, pltpu.roll(first, SUB - 1, 0), 0.0), last
+
+    c = [jnp.exp(at(C0 + NY, n)) for n in range(BLOCKS)]
+    u = [at(U0 + NY, n) for n in range(BLOCKS)]
+    c_next, c_last = turned(c[-1], c[0])
+    u_next, u_last = turned(u[-1], u[0])
+    top = WX * (c_last + c_next) * (u_next - u_last)
+    left = jnp.where(s > 0, pltpu.roll(top, 1, 0), WX * c[0] * u[0])
+    for n in range(BLOCKS):
+        right = WX * (c[n] + c[n + 1]) * (u[n + 1] - u[n]) if n < BLOCKS - 1 else top
+        below = WX * (c[n] + jnp.exp(at(C0, n))) * (at(U0, n) - u[n])
+        kzp = z_above * (c[n] + pltpu.roll(c[n], NZ - 1, 1))
+        kzm = z_below * (c[n] + pltpu.roll(c[n], 1, 1))
+        side = kzp * pltpu.roll(u[n], NZ - 1, 1) + kzm * pltpu.roll(u[n], 1, 1)
+        side -= (kzp + kzm + z_ends * c[n]) * u[n]
+        near[pl.ds(SUB * n, SUB)] = u[n]
+        near[pl.ds(PARTLY + SUB * n, SUB)] = u[n] + DT * at(Q1, n) + (below + (right - left) + side)
+        left = right
+    near[NEAR_C0 : NEAR_D0] = full[C0 : C0 + CELLS]
+    near[NEAR_D0 : NEAR_PACK] = full[D0 : D0 + 24]
 
 
 def write_hots(duct, base, flip, j, at_rows, at_lanes, at_segments):
@@ -237,16 +268,8 @@
 
 
 def prepare_near_kernel(near2, far_segments, at_segments):
-    _, _, segment = duct_lists(near2, D0 - NY, False)
+    _, _, segment = duct_lists(near2, NEAR_D0, False)
     at_segments[0] = as_bf16(hot(segment, 128))
-
-
-def slab_rows(near2, near1, own, far1, far2):
-    out = []
-    for j, slab in enumerate((near2, near1, own, far1, far2)):
-        for r in range(2):
-            out.append((slab, NY if j == 0 else 0, 1 - r if j in (1, 3) else r))
-    return out
 
 
 def forward_kernel(
@@ -255,16 +278,25 @@
 ):
     near, far = validity()
     temp = (temp0, temp1, temp2, temp3, temp4)
-    for i, (slab, skip, r) in enumerate(slab_rows(near2, near1, own, far1, far2)):
-        valid = near if i < 4 else (far if i > 7 else 1.0)
-        temp0[i] = slab[pl.ds(U0 - skip + r * NY, NY)]
-        cond[i] = jnp.exp(slab[pl.ds(C0 - skip + r * NY, NY)]) * valid
-        if 1 <= i <= 8:
-            load[i] = DT * slab[pl.ds((Q1 - skip) if r else Q0, NY)]
+    temp0[0] = jnp.zeros((NY, NZ), f32)
+    load[1] = jnp.zeros((NY, NZ), f32)
+    temp0[1] = near2[0:NY]
+    for r in range(2):
+        cond[r] = jnp.exp(near2[pl.ds(NEAR_C0 + r * NY, NY)]) * near
+    for j, slab in enumerate((near1, own, far1, far2)):
+        for r in range(2):
+            i, at = 2 * j + 2 + r, 1 - r if j in (0, 2) else r
+            temp0[i] = slab[pl.ds(U0 + at * NY, NY)]
+            conductivity = jnp.exp(slab[pl.ds(C0 + at * NY, NY)])
+            cond[i] = conductivity * (near, 1.0, 1.0, far)[j] if j in (0, 3) else conductivity
+            if i <= 8:
+                load[i] = DT * slab[pl.ds(Q1 if at else Q0, NY)]
     coefs = (kx, ky, kzp, kzm, keep)
     coefficients(cond, *coefs)
     for k in range(STEPS):
         advance(temp[k], temp[k + 1], k + 1, 8 - k, coefs, load, near, far)
+        if k == 0:
+            temp1[1] = near * (near2[PARTLY : PARTLY + NY] + kx[1] * (temp0[2] - temp0[1]))
 
     across = jnp.concatenate([temp4[4].T, temp4[5].T], axis=1)
     stack = jnp.concatenate([part.astype(bf16) for part in parts_of(across, 3)], axis=0)
@@ -297,7 +329,7 @@
     shift = lax.rem(128 - seg.shape[1] * g, 128)
     seg[...] = pltpu.roll(jnp.broadcast_to(resid, (8, 128)), shift, 1)[0:1, 0 : seg.shape[1]]
     stack = stacked_rows(parts_of(0.5 * resid, 3))
-    write_hots(near2, D0 - NY, False, 0, near_rows, near_lanes, None)
+    write_hots(near2, NEAR_D0, False, 0, near_rows, near_lanes, None)
     near_segments[0] = near2_segments[0]
     write_hots(near1, D0, True, 1, near_rows, near_lanes, near_segments)
     own, fars = (own_rows, own_lanes, own_segments), (far_rows, far_lanes, far_segments)
@@ -376,11 +408,11 @@
     tests = lax.axis_size("tests")
     vmem = pl.BlockSpec(memory_space=pltpu.VMEM)
     params = pltpu.CompilerParams(vmem_limit_bytes=24 * 1024 * 1024)
-    pack, pack_near = pl.pallas_call(
+    pack = pl.pallas_call(
         pack_kernel,
-        out_shape=(pltpu.VMEM((PACK, NZ), f32), pltpu.VMEM((PACK - NY, NZ), f32)),
+        out_shape=pltpu.VMEM((PACK, NZ), f32),
         in_specs=[pl.BlockSpec(memory_space=pltpu.HBM)] * 6,
-        out_specs=(vmem, vmem),
+        out_specs=vmem,
         scratch_shapes=[
             pltpu.VMEM(field(6), f32),
             pltpu.VMEM((8, 256), jnp.int32),
@@ -391,6 +423,14 @@
         compiler_params=params,
         name="pack",
     )(*map(in_hbm, (log_cond, opening_increase, heat_load, duct_cells.T, duct_segment.T, measured)))
+    pack_near = pl.pallas_call(
+        pack_near_kernel,
+        out_shape=pltpu.VMEM((NEAR_PACK, NZ), f32),
+        in_specs=[vmem],
+        out_specs=vmem,
+        compiler_params=params,
+        name="pack_near",
+    )(pack)
     to_far = [(s, s - 2) for s in range(2, grid, 2)] + [(s, s + 2) for s in range(1, grid - 2, 2)]
     to_near = [(s, s + 2) for s in range(0, grid - 2, 2)] + [(s, s - 2) for s in range(3, grid, 2)]
     swap = [(s, s ^ 1) for s in range(grid)]

time: 73.4 us -> 73 us (level)
  waiting for transfers between devices: 10.6 us -> 9.8 us
    ppermute x1, waiting for transfers between devices: 9.48 us -> 8.7 us  [local(): far2 = lax.ppermute(pack, 'grid', to_far)]
where the time goes in v6:
time: 73 us; the launch traced here: 72.7 us
  blocking collectives  37.4 us (51%)
  starting transfers between devices  13.5 us (18%)
  Pallas kernels  10.8 us (15%)
  waiting for transfers between devices  9.8 us (13%)
    all_to_all x1, blocking collectives, local(): lax.all_to_all(grad, 'tests', split_axis=0, concat_axis=0, tiled=True)  25.7 us
    all_to_all x1, blocking collectives, local(): sums = lax.all_to_all(sums, 'grid', split_axis=0, concat_axis=0, tiled=True)  11.7 us
    ppermute x1, waiting for transfers between devices, local(): far2 = lax.ppermute(pack, 'grid', to_far)  8.7 us
    ppermute x1, starting transfers between devices, local(): far2 = lax.ppermute(pack, 'grid', to_far)  7.73 us
    pallas_call x1, Pallas kernels, local(): pl.pallas_call(backward_kernel, out_shape=(pltpu.VMEM((tests, 2, share, N...  5.1 us
    pallas_call x1, Pallas kernels, local(): pl.pallas_call(forward_kernel, out_shape=tuple((pltpu.VMEM(shape, f32) fo...  3.37 us
    ppermute x1, starting transfers between devices, local(): far1 = lax.ppermute(pack, 'grid', swap)  1.92 us
    ppermute x1, starting transfers between devices, local(): near2 = lax.ppermute(pack_near, 'grid', to_near)  1.92 us
  transfers between devices with their start and end apart: 4, of which 2 were waited for; matrix products, arithmetic and copies ran while one was open for 0% of the time, Pallas kernels for 1%

profile of v6, /device:TPU:8, one launch (start us, length us, event | category | flops | bytes accessed | tf_op | source)
XLA Modules:
  0.0 72.7 jit_solution(16437178189370528706)
XLA Ops:
  0.6 1.3 %pack.1.full.own = f32[792,128]{1,0:T(8,128)S(1)} custom-call(f32[2,128,128]{2,1,0:T(8,128)} %log_cond.1, f32[1,2,128,128]{3,2,1,0:T(8,128)} %opening.1, f32[1,2,128,128]{3,2,1,0:T(8,128)} %heat.1, s32[8,256]{1,0:T(8,128)} %bitcast.8, s32[1,256]{1,0:T(1,128)} %bitcast.9, f32[1,4]{1,0:T(1,128)} %measured.1), custom_call_target="tpu_custom_call" | custom-call | tf_op jit(solution)/shard_map/pack/pallas_call | solution.py:411
  1.9 7.7 %collective-permute-start.2 = (f32[792,128]{1,0:T(8,128)S(1)}, f32[792,128]{1,0:T(8,128)S(1)}, u32[]{:S(2)}, u32[]{:S(2)}) collective-permute-start(f32[792,128]{1,0:T(8,128)S(1)} %pack.1.full.own), channel_id=1, source_target_pairs={{2,0},{4,2},{6,4},{8,6},{10,8},{12,10},{14,12},{16,14},{18,16},{20... | collective-permute-start | bytes 1216520 | tf_op jit(solution)/shard_map/ppermute | solution.py:437
  9.7 1.9 %collective-permute-start.1 = (f32[792,128]{1,0:T(8,128)S(1)}, f32[792,128]{1,0:T(8,128)S(1)}, u32[]{:S(2)}, u32[]{:S(2)}) collective-permute-start(f32[792,128]{1,0:T(8,128)S(1)} %pack.1.full.own), channel_id=1, source_target_pairs={{0,1},{1,0},{2,3},{3,2},{4,5},{5,4},{6,7},{7,6},{8,9},{9,8},{10,11... | collective-permute-start | bytes 1216520 | tf_op jit(solution)/shard_map/ppermute | solution.py:438
  11.6 0.1 pack_near.1
  11.7 1.9 %collective-permute-start = (f32[536,128]{1,0:T(8,128)S(1)}, f32[536,128]{1,0:T(8,128)S(1)}, u32[]{:S(2)}, u32[]{:S(2)}) collective-permute-start(f32[536,128]{1,0:T(8,128)S(1)} %pack_near.1), channel_id=1, source_target_pairs={{0,2},{2,4},{4,6},{6,8},{8,10},{10,12},{12,14},{14,16},{16,18},{18... | collective-permute-start | bytes 823304 | tf_op jit(solution)/shard_map/ppermute | solution.py:439
  13.7 0.3 prepare_own.1
  14.0 8.7 %collective-permute-done.2.far2 = f32[792,128]{1,0:T(8,128)S(1)} collective-permute-done((f32[792,128]{1,0:T(8,128)S(1)}, f32[792,128]{1,0:T(8,128)S(1)}, u32[]{:S(2)}, u32[]{:S(2)}) %collective-permute-start.2) | collective-permute-done | bytes 405536 | tf_op jit(solution)/shard_map/ppermute | solution.py:437
  22.7 1.9 %collective-permute-start.3 = (f32[792,128]{1,0:T(8,128)S(1)}, f32[792,128]{1,0:T(8,128)S(1)}, u32[]{:S(2)}, u32[]{:S(2)}) collective-permute-start(f32[792,128]{1,0:T(8,128)S(1)} %collective-permute-done.2.far2), channel_id=1, source_target_pairs={{0,1},{1,0},{2,3},{3,2},{4,5},{5,4},{6,7},{7,6},{8,9},{9,8},{10,11... | collective-permute-start | bytes 1216520 | tf_op jit(solution)/shard_map/ppermute | solution.py:461
  24.6 0.0 collective-permute-done.1.far1
  24.6 0.6 prepare_far.1
  25.1 0.0 collective-permute-done.near2
  25.2 1.1 %collective-permute-done.3.near1 = f32[792,128]{1,0:T(8,128)S(1)} collective-permute-done((f32[792,128]{1,0:T(8,128)S(1)}, f32[792,128]{1,0:T(8,128)S(1)}, u32[]{:S(2)}, u32[]{:S(2)}) %collective-permute-start.3) | collective-permute-done | bytes 405536 | tf_op jit(solution)/shard_map/ppermute | solution.py:461
  26.3 3.4 %forward.1 = (f32[10,128,128]{2,1,0:T(8,128)S(1)}, f32[10,128,128]{2,1,0:T(8,128)S(1)}, f32[10,128,128]{2,1,0:T(8,128)S(1)}, f32[10,128,128]{2,1,0:T(8,128)S(1)}...) custom-call(f32[536,128]{1,0:T(8,128)S(1)} %collective-permute-done., ...), custom_call_target="tpu_custom_call" | custom-call | tf_op jit(solution)/shard_map/forward/pallas_call | solution.py:468
  29.6 11.7 %all_to_all.16 = f32[32,1,128]{2,1,0:T(1,128)S(1)} all-to-all(f32[32,1,128]{2,1,0:T(1,128)S(1)} %bitcast.7), channel_id=1, replica_groups=mesh['tests'=16,'grid'=32] {'grid'}, dimensions={0} | all-to-all | bytes 32768 | tf_op jit(solution)/shard_map/all_to_all | solution.py:477
  41.3 5.1 %backward.1 = (f32[16,2,8,128]{3,2,1,0:T(8,128)S(1)}, f32[1,4]{1,0:T(1,128)}) custom-call(f32[536,128]{1,0:T(8,128)S(1)} %collective-permute-done.near2, f32[792,128]{1,0:T(8,128)S(1)} %collective-permute-done.3.near1, bf16[1,256,2048]{2,1,0:T(8,128)(2,1)S(1)} %get-tuple-element.38.at_rows.own_rows, ...), custom_call_target="tpu_custom_call" | custom-call | tf_op jit(solution)/shard_map/backward/pallas_call | solution.py:479
  46.4 25.7 %all_to_all.17 = f32[16,2,8,128]{3,2,1,0:T(8,128)S(1)} all-to-all(f32[16,2,8,128]{3,2,1,0:T(8,128)S(1)} %get-tuple-element.56), channel_id=1, replica_groups=mesh['tests'=16,'grid'=32] {'tests'}, dimensions={0} | all-to-all | bytes 262144 | tf_op jit(solution)/shard_map/all_to_all | solution.py:496
  72.1 0.6 reduce_sum.9
  (1 shorter events, 0.0 us)
Async XLA Ops:
  1.9 20.7 %collective-permute-start.2 = (f32[792,128]{1,0:T(8,128)S(1)}, f32[792,128]{1,0:T(8,128)S(1)}, u32[]{:S(2)}, u32[]{:S(2)}) collective-permute-start(f32[792,128]{1,0:T(8,128)S(1)} %pack.1.full.own), channel_id=1, source_target_pairs={{2,0},{4,2},{6,4},{8,6},{10,8},{12,10},{14,12},{16,14},{18,16},{20... | collective-permute-start | bytes 1216520 | tf_op jit(solution)/shard_map/ppermute | solution.py:437
  9.7 14.9 %collective-permute-start.1 = (f32[792,128]{1,0:T(8,128)S(1)}, f32[792,128]{1,0:T(8,128)S(1)}, u32[]{:S(2)}, u32[]{:S(2)}) collective-permute-start(f32[792,128]{1,0:T(8,128)S(1)} %pack.1.full.own), channel_id=1, source_target_pairs={{0,1},{1,0},{2,3},{3,2},{4,5},{5,4},{6,7},{7,6},{8,9},{9,8},{10,11... | collective-permute-start | bytes 1216520 | tf_op jit(solution)/shard_map/ppermute | solution.py:438
  11.7 13.4 %collective-permute-start = (f32[536,128]{1,0:T(8,128)S(1)}, f32[536,128]{1,0:T(8,128)S(1)}, u32[]{:S(2)}, u32[]{:S(2)}) collective-permute-start(f32[536,128]{1,0:T(8,128)S(1)} %pack_near.1), channel_id=1, source_target_pairs={{0,2},{2,4},{4,6},{6,8},{8,10},{10,12},{12,14},{14,16},{16,18},{18... | collective-permute-start | bytes 823304 | tf_op jit(solution)/shard_map/ppermute | solution.py:439
  22.7 3.6 %collective-permute-start.3 = (f32[792,128]{1,0:T(8,128)S(1)}, f32[792,128]{1,0:T(8,128)S(1)}, u32[]{:S(2)}, u32[]{:S(2)}) collective-permute-start(f32[792,128]{1,0:T(8,128)S(1)} %collective-permute-done.2.far2), channel_id=1, source_target_pairs={{0,1},{1,0},{2,3},{3,2},{4,5},{5,4},{6,7},{7,6},{8,9},{9,8},{10,11... | collective-permute-start | bytes 1216520 | tf_op jit(solution)/shard_map/ppermute | solution.py:461

commit v7 on v6

--- a/solution.py
+++ b/solution.py
@@ -25,6 +25,7 @@
 NEAR_C0 = 2 * NY
 NEAR_D0 = 4 * NY
 NEAR_PACK = NEAR_D0 + 24
+FIELDS = 10
 COST_ESTIMATE = 2_000_000_000
 bf16 = jnp.bfloat16
 f32 = jnp.float32
@@ -57,14 +58,14 @@
     return s, z
 
 
-def coefficients(cond, kx, ky, kzp, kzm, keep):
+def coefficients(cond, kx, ky, kzp, kzm, keep, first_row, pairs):
     s, z = coordinates()
     z_above, z_below = jnp.where(z < NZ - 1, WZ, 0.0), jnp.where(z > 0, WZ, 0.0)
     s_inside = jnp.where(s < SUB - 1, WX, 0.0)
     first_end, last_end = jnp.where(s == 0, WX, 0.0), jnp.where(s == SUB - 1, WX, 0.0)
 
     def rows(b, carry):
-        first = 1 + 2 * b
+        first = first_row + 2 * b
         for i in (first, first + 1):
             c = [cond[i, part(n)] for n in range(BLOCKS)]
             for n in range(BLOCKS):
@@ -84,8 +85,11 @@
                 keep[i, part(n)] = 1.0 - ((above + below) + ends * c[n])
         return carry
 
-    kx[0] = WX * (cond[0] + cond[1])
-    lax.fori_loop(0, EXT // 2 - 1, rows, 0)
+    kx[first_row - 1] = WX * (cond[first_row - 1] + cond[first_row])
+    if pairs == 1:
+        rows(0, 0)
+    else:
+        lax.fori_loop(0, pairs, rows, 0)
 
 
 def advance(src, dst, first, last, coefs, load, near, far):
@@ -258,11 +262,30 @@
         at_segments[j] = as_bf16(hot(segment, 128))
 
 
-def prepare_own_kernel(own, at_rows, at_lanes, at_segments):
+def place(slab, first, turned, valid, temp0, cond, load):
+    for r in range(2):
+        i, at = first + r, 1 - r if turned else r
+        temp0[i] = slab[pl.ds(U0 + at * NY, NY)]
+        conductivity = jnp.exp(slab[pl.ds(C0 + at * NY, NY)])
+        cond[i] = conductivity if valid is None else conductivity * valid
+        if i < EXT - 1:
+            load[i] = DT * slab[pl.ds(Q1 if at else Q0, NY)]
+
+
+def prepare_own_kernel(own, at_rows, at_lanes, at_segments, temp0, load, cond):
+    place(own, 4, False, None, temp0, cond, load)
     write_hots(own, D0, False, 0, at_rows, at_lanes, at_segments)
 
 
-def prepare_far_kernel(far1, far2, at_rows, at_lanes, at_segments):
+def prepare_far_kernel(far1, far2, *refs):
+    at_rows, at_lanes, at_segments, temp2, temp1, kx, ky, kzp, kzm, keep, temp0, load, cond = refs[3:]
+    near, far = validity()
+    coefs = (kx, ky, kzp, kzm, keep)
+    place(far1, 6, True, None, temp0, cond, load)
+    place(far2, 8, False, far, temp0, cond, load)
+    coefficients(cond, *coefs, 5, 2)
+    advance(temp0, temp1, 5, 8, coefs, load, near, far)
+    advance(temp1, temp2, 6, 7, coefs, load, near, far)
     write_hots(far1, D0, True, 0, at_rows, at_lanes, at_segments)
     write_hots(far2, D0, False, 1, at_rows, at_lanes, at_segments)
 
@@ -272,31 +295,21 @@
     at_segments[0] = as_bf16(hot(segment, 128))
 
 
-def forward_kernel(
-    near2, near1, own, far1, far2, at_rows, at_lanes, at_segments,
-    temp0, temp1, temp2, temp3, temp4, cond, kx, ky, kzp, kzm, keep, sums, load,
-):
+def forward_kernel(near2, near1, own, at_rows, at_lanes, at_segments, *refs):
+    temp3, temp4, sums, temp2, temp1, *coefs, temp0, load, cond = refs[FIELDS:]
     near, far = validity()
-    temp = (temp0, temp1, temp2, temp3, temp4)
     temp0[0] = jnp.zeros((NY, NZ), f32)
     load[1] = jnp.zeros((NY, NZ), f32)
     temp0[1] = near2[0:NY]
     for r in range(2):
         cond[r] = jnp.exp(near2[pl.ds(NEAR_C0 + r * NY, NY)]) * near
-    for j, slab in enumerate((near1, own, far1, far2)):
-        for r in range(2):
-            i, at = 2 * j + 2 + r, 1 - r if j in (0, 2) else r
-            temp0[i] = slab[pl.ds(U0 + at * NY, NY)]
-            conductivity = jnp.exp(slab[pl.ds(C0 + at * NY, NY)])
-            cond[i] = conductivity * (near, 1.0, 1.0, far)[j] if j in (0, 3) else conductivity
-            if i <= 8:
-                load[i] = DT * slab[pl.ds(Q1 if at else Q0, NY)]
-    coefs = (kx, ky, kzp, kzm, keep)
-    coefficients(cond, *coefs)
-    for k in range(STEPS):
-        advance(temp[k], temp[k + 1], k + 1, 8 - k, coefs, load, near, far)
-        if k == 0:
-            temp1[1] = near * (near2[PARTLY : PARTLY + NY] + kx[1] * (temp0[2] - temp0[1]))
+    place(near1, 2, True, near, temp0, cond, load)
+    coefficients(cond, *coefs, 1, 2)
+    advance(temp0, temp1, 1, 4, coefs, load, near, far)
+    temp1[1] = near * (near2[PARTLY : PARTLY + NY] + coefs[0][1] * (temp0[2] - temp0[1]))
+    advance(temp1, temp2, 2, 5, coefs, load, near, far)
+    advance(temp2, temp3, 3, 6, coefs, load, near, far)
+    advance(temp3, temp4, 4, 5, coefs, load, near, far)
 
     across = jnp.concatenate([temp4[4].T, temp4[5].T], axis=1)
     stack = jnp.concatenate([part.astype(bf16) for part in parts_of(across, 3)], axis=0)
@@ -445,35 +458,35 @@
             pltpu.VMEM((slabs, 128, 256), bf16),
         )
 
-    def prepare(kernel, out_shape, name, *slabs):
+    field_shape = pltpu.VMEM(field(EXT), f32)
+
+    def stage(kernel, out_shape, name, *operands, fields=(), cost=COST_ESTIMATE):
+        shapes = (*out_shape, *[field_shape] * len(fields))
         return pl.pallas_call(
             kernel,
-            out_shape=out_shape,
-            in_specs=[vmem] * len(slabs),
-            out_specs=(vmem,) * len(out_shape),
+            out_shape=shapes,
+            in_specs=[vmem] * (len(operands) + len(fields)),
+            out_specs=(vmem,) * len(shapes),
+            input_output_aliases={len(operands) + n: len(out_shape) + n for n in range(len(fields))},
             compiler_params=params,
-            cost_estimate=pl.CostEstimate(flops=COST_ESTIMATE, bytes_accessed=4_000_000, transcendentals=0),
+            cost_estimate=pl.CostEstimate(flops=cost, bytes_accessed=4_000_000, transcendentals=0),
             name=name,
-        )(*slabs)
-
-    own_hots = prepare(prepare_own_kernel, hots(1), "prepare_own", pack)
-    far2, *own_hots = lax.optimization_barrier((far2, *own_hots))
+        )(*operands, *fields)
+
+    results = stage(prepare_own_kernel, (*hots(1), *[field_shape] * 3), "prepare_own", pack)
+    own_hots, fields = results[:3], results[3:]
+    far2, own_hots = lax.optimization_barrier((far2, own_hots))
     near1 = lax.ppermute(far2, "grid", swap)
-    far_hots = prepare(prepare_far_kernel, hots(2), "prepare_far", far1, far2)
-    near_hots = prepare(prepare_near_kernel, hots(1)[2:], "prepare_near", near2, far_hots[2])
+    results = stage(
+        prepare_far_kernel, (*hots(2), *[field_shape] * 7), "prepare_far", far1, far2, fields=fields
+    )
+    far_hots, fields = results[:3], results[3:]
+    near_hots = stage(prepare_near_kernel, hots(1)[2:], "prepare_near", near2, far_hots[2])
     near2, near_hots, far_hots = lax.optimization_barrier((near2, near_hots, far_hots))
-    packs = (near2, near1, pack, far1, far2)
-    coefs = [field(EXT)] * 6
-    levels = [field(EXT)] * (STEPS + 1)
-    *results, sums = pl.pallas_call(
-        forward_kernel,
-        out_shape=tuple(pltpu.VMEM(shape, f32) for shape in (*levels, *coefs, (grid, 128))),
-        in_specs=[vmem] * 8,
-        out_specs=(vmem,) * 12,
-        scratch_shapes=[pltpu.VMEM(field(EXT), f32)],
-        compiler_params=params,
-        name="forward",
-    )(*packs, *own_hots)
+    out_shape = (field_shape, field_shape, pltpu.VMEM((grid, 128), f32))
+    temp3, _, sums, temp2, temp1, *coefs, temp0, _, cond = stage(
+        forward_kernel, out_shape, "forward", near2, near1, pack, *own_hots, fields=fields
+    )
     sums = lax.all_to_all(sums, "grid", split_axis=0, concat_axis=0, tiled=True)
     share = NY // tests
     grad, seg = pl.pallas_call(
@@ -492,7 +505,7 @@
         ],
         compiler_params=params,
         name="backward",
-    )(near2, near1, *own_hots, *far_hots, *near_hots, sums, *results[:STEPS], *results[STEPS + 1 :])
+    )(near2, near1, *own_hots, *far_hots, *near_hots, sums, temp0, temp1, temp2, temp3, cond, *coefs)
     grad = lax.all_to_all(grad, "tests", split_axis=0, concat_axis=0, tiled=True)
     return jnp.sum(grad, axis=0), seg
 

time: 73 us -> 72.5 us (level)
  waiting for transfers between devices: 9.8 us -> 8.68 us
    ppermute x1, waiting for transfers between devices: 1.1 us -> 0.01 us  [local(): near1 = lax.ppermute(far2, 'grid', swap)]
  transfers between devices with their start and end apart: 4 -> 4, of which waited for: 2 -> 1; matrix products, arithmetic and copies ran while one was open for 0% -> 0% of each run, Pallas kernels for 1% -> 3%
where the time goes in v7:
time: 72.5 us; the launch traced here: 72.2 us
  blocking collectives  37.5 us (52%)
  starting transfers between devices  13.5 us (19%)
  Pallas kernels  11.3 us (16%)
  waiting for transfers between devices  8.68 us (12%)
    all_to_all x1, blocking collectives, local(): lax.all_to_all(grad, 'tests', split_axis=0, concat_axis=0, tiled=True)  25.8 us
    all_to_all x1, blocking collectives, local(): sums = lax.all_to_all(sums, 'grid', split_axis=0, concat_axis=0, tiled=True)  11.7 us
    ppermute x1, waiting for transfers between devices, local(): far2 = lax.ppermute(pack, 'grid', to_far)  8.67 us
    ppermute x1, starting transfers between devices, local(): far2 = lax.ppermute(pack, 'grid', to_far)  7.73 us
    pallas_call x1, Pallas kernels, local(): pl.pallas_call(backward_kernel, out_shape=(pltpu.VMEM((tests, 2, share, N...  5.09 us
    pallas_call x4, Pallas kernels, stage(): pl.pallas_call(kernel, out_shape=shapes, in_specs=[vmem] * (len(operands)...  4.75 us
    ppermute x1, starting transfers between devices, local(): far1 = lax.ppermute(pack, 'grid', swap)  1.92 us
    ppermute x1, starting transfers between devices, local(): near2 = lax.ppermute(pack_near, 'grid', to_near)  1.92 us
  transfers between devices with their start and end apart: 4, of which 1 were waited for; matrix products, arithmetic and copies ran while one was open for 0% of the time, Pallas kernels for 3%

profile of v7, /device:TPU:8, one launch (start us, length us, event | category | flops | bytes accessed | tf_op | source)
XLA Modules:
  0.0 72.2 jit_solution(17752885085815387400)
XLA Ops:
  0.6 1.3 %pack.1.full.own = f32[792,128]{1,0:T(8,128)S(1)} custom-call(f32[2,128,128]{2,1,0:T(8,128)} %log_cond.1, f32[1,2,128,128]{3,2,1,0:T(8,128)} %opening.1, f32[1,2,128,128]{3,2,1,0:T(8,128)} %heat.1, s32[8,256]{1,0:T(8,128)} %bitcast.8, s32[1,256]{1,0:T(1,128)} %bitcast.9, f32[1,4]{1,0:T(1,128)} %measured.1), custom_call_target="tpu_custom_call" | custom-call | tf_op jit(solution)/shard_map/pack/pallas_call | solution.py:424
  1.9 7.7 %collective-permute-start.2 = (f32[792,128]{1,0:T(8,128)S(1)}, f32[792,128]{1,0:T(8,128)S(1)}, u32[]{:S(2)}, u32[]{:S(2)}) collective-permute-start(f32[792,128]{1,0:T(8,128)S(1)} %pack.1.full.own), channel_id=1, source_target_pairs={{2,0},{4,2},{6,4},{8,6},{10,8},{12,10},{14,12},{16,14},{18,16},{20... | collective-permute-start | bytes 1216520 | tf_op jit(solution)/shard_map/ppermute | solution.py:450
  9.7 1.9 %collective-permute-start.1 = (f32[792,128]{1,0:T(8,128)S(1)}, f32[792,128]{1,0:T(8,128)S(1)}, u32[]{:S(2)}, u32[]{:S(2)}) collective-permute-start(f32[792,128]{1,0:T(8,128)S(1)} %pack.1.full.own), channel_id=1, source_target_pairs={{0,1},{1,0},{2,3},{3,2},{4,5},{5,4},{6,7},{7,6},{8,9},{9,8},{10,11... | collective-permute-start | bytes 1216520 | tf_op jit(solution)/shard_map/ppermute | solution.py:451
  11.6 0.1 pack_near.1
  11.7 1.9 %collective-permute-start = (f32[536,128]{1,0:T(8,128)S(1)}, f32[536,128]{1,0:T(8,128)S(1)}, u32[]{:S(2)}, u32[]{:S(2)}) collective-permute-start(f32[536,128]{1,0:T(8,128)S(1)} %pack_near.1), channel_id=1, source_target_pairs={{0,2},{2,4},{4,6},{6,8},{8,10},{10,12},{12,14},{14,16},{16,18},{18... | collective-permute-start | bytes 823304 | tf_op jit(solution)/shard_map/ppermute | solution.py:452
  13.7 0.3 prepare_own.1
  14.0 8.7 %collective-permute-done.2.far2 = f32[792,128]{1,0:T(8,128)S(1)} collective-permute-done((f32[792,128]{1,0:T(8,128)S(1)}, f32[792,128]{1,0:T(8,128)S(1)}, u32[]{:S(2)}, u32[]{:S(2)}) %collective-permute-start.2) | collective-permute-done | bytes 405536 | tf_op jit(solution)/shard_map/ppermute | solution.py:450
  22.7 1.9 %collective-permute-start.3 = (f32[792,128]{1,0:T(8,128)S(1)}, f32[792,128]{1,0:T(8,128)S(1)}, u32[]{:S(2)}, u32[]{:S(2)}) collective-permute-start(f32[792,128]{1,0:T(8,128)S(1)} %collective-permute-done.2.far2), channel_id=1, source_target_pairs={{0,1},{1,0},{2,3},{3,2},{4,5},{5,4},{6,7},{7,6},{8,9},{9,8},{10,11... | collective-permute-start | bytes 1216520 | tf_op jit(solution)/shard_map/ppermute | solution.py:479
  24.6 0.0 collective-permute-done.1.far1
  24.6 1.9 %prepare_far.1 = (bf16[2,256,2048]{2,1,0:T(8,128)(2,1)S(1)}, bf16[2,128,2048]{2,1,0:T(8,128)(2,1)S(1)}, bf16[2,128,256]{2,1,0:T(8,128)(2,1)S(1)}, f32[10,128,128...) custom-call(f32[792,128]{1,0:T(8,128)S(1)} %collective-permute-done., ...), custom_call_target="tpu_custom_call", output_to_operand_aliasing={{10}: (2, {}), {11}: (3, {}), {12}: (4, {})} | custom-call | flops 2000000000 | bytes 4000000 | tf_op jit(solution)/shard_map/prepare_far/pallas_call | solution.py:465
  26.5 0.0 collective-permute-done.near2
  26.6 0.0 collective-permute-done.3.near1
  26.6 2.5 %forward.1 = (f32[10,128,128]{2,1,0:T(8,128)S(1)}, f32[10,128,128]{2,1,0:T(8,128)}, f32[32,128]{1,0:T(8,128)S(1)}, f32[10,128,128]{2,1,0:T(8,128)S(1)}, f32[10,1...) custom-call(f32[536,128]{1,0:T(8,128)S(1)} %collective-permute-done., ...), custom_call_target="tpu_custom_call", output_to_operand_aliasing={{3}: (6, {}), {4}: (7, {}), {5}: (8, {}), {6}: (9, {}), {7}... | custom-call | flops 2000000000 | bytes 4000000 | tf_op jit(solution)/shard_map/forward/pallas_call | solution.py:465
  29.1 11.7 %all_to_all.16 = f32[32,1,128]{2,1,0:T(1,128)S(1)} all-to-all(f32[32,1,128]{2,1,0:T(1,128)S(1)} %bitcast.7), channel_id=1, replica_groups=mesh['tests'=16,'grid'=32] {'grid'}, dimensions={0} | all-to-all | bytes 32768 | tf_op jit(solution)/shard_map/all_to_all | solution.py:490
  40.7 5.1 %backward.1 = (f32[16,2,8,128]{3,2,1,0:T(8,128)S(1)}, f32[1,4]{1,0:T(1,128)}) custom-call(f32[536,128]{1,0:T(8,128)S(1)} %collective-permute-done.near2, f32[792,128]{1,0:T(8,128)S(1)} %collective-permute-done.3.near1, bf16[1,256,2048]{2,1,0:T(8,128)(2,1)S(1)} %get-tuple-element.54.at_rows.own_rows, ...), custom_call_target="tpu_custom_call" | custom-call | tf_op jit(solution)/shard_map/backward/pallas_call | solution.py:492
  45.8 25.8 %all_to_all.17 = f32[16,2,8,128]{3,2,1,0:T(8,128)S(1)} all-to-all(f32[16,2,8,128]{3,2,1,0:T(8,128)S(1)} %get-tuple-element.82), channel_id=1, replica_groups=mesh['tests'=16,'grid'=32] {'tests'}, dimensions={0} | all-to-all | bytes 262144 | tf_op jit(solution)/shard_map/all_to_all | solution.py:509
  71.6 0.6 reduce_sum.9
  (1 shorter events, 0.0 us)
Async XLA Ops:
  1.9 20.7 %collective-permute-start.2 = (f32[792,128]{1,0:T(8,128)S(1)}, f32[792,128]{1,0:T(8,128)S(1)}, u32[]{:S(2)}, u32[]{:S(2)}) collective-permute-start(f32[792,128]{1,0:T(8,128)S(1)} %pack.1.full.own), channel_id=1, source_target_pairs={{2,0},{4,2},{6,4},{8,6},{10,8},{12,10},{14,12},{16,14},{18,16},{20... | collective-permute-start | bytes 1216520 | tf_op jit(solution)/shard_map/ppermute | solution.py:450
  9.7 14.9 %collective-permute-start.1 = (f32[792,128]{1,0:T(8,128)S(1)}, f32[792,128]{1,0:T(8,128)S(1)}, u32[]{:S(2)}, u32[]{:S(2)}) collective-permute-start(f32[792,128]{1,0:T(8,128)S(1)} %pack.1.full.own), channel_id=1, source_target_pairs={{0,1},{1,0},{2,3},{3,2},{4,5},{5,4},{6,7},{7,6},{8,9},{9,8},{10,11... | collective-permute-start | bytes 1216520 | tf_op jit(solution)/shard_map/ppermute | solution.py:451
  11.7 14.8 %collective-permute-start = (f32[536,128]{1,0:T(8,128)S(1)}, f32[536,128]{1,0:T(8,128)S(1)}, u32[]{:S(2)}, u32[]{:S(2)}) collective-permute-start(f32[536,128]{1,0:T(8,128)S(1)} %pack_near.1), channel_id=1, source_target_pairs={{0,2},{2,4},{4,6},{6,8},{8,10},{10,12},{12,14},{14,16},{16,18},{18... | collective-permute-start | bytes 823304 | tf_op jit(solution)/shard_map/ppermute | solution.py:452
  22.7 3.9 %collective-permute-start.3 = (f32[792,128]{1,0:T(8,128)S(1)}, f32[792,128]{1,0:T(8,128)S(1)}, u32[]{:S(2)}, u32[]{:S(2)}) collective-permute-start(f32[792,128]{1,0:T(8,128)S(1)} %collective-permute-done.2.far2), channel_id=1, source_target_pairs={{0,1},{1,0},{2,3},{3,2},{4,5},{5,4},{6,7},{7,6},{8,9},{9,8},{10,11... | collective-permute-start | bytes 1216520 | tf_op jit(solution)/shard_map/ppermute | solution.py:479

commit v8 on v7

--- a/solution.py
+++ b/solution.py
@@ -277,17 +277,25 @@
     write_hots(own, D0, False, 0, at_rows, at_lanes, at_segments)
 
 
-def prepare_far_kernel(far1, far2, *refs):
-    at_rows, at_lanes, at_segments, temp2, temp1, kx, ky, kzp, kzm, keep, temp0, load, cond = refs[3:]
+def prepare_chip_kernel(far1, *refs):
+    at_rows, at_lanes, at_segments, temp1, kx, ky, kzp, kzm, keep, temp0, load, cond = refs[3:]
     near, far = validity()
     coefs = (kx, ky, kzp, kzm, keep)
     place(far1, 6, True, None, temp0, cond, load)
+    coefficients(cond, *coefs, 5, 1)
+    advance(temp0, temp1, 5, 6, coefs, load, near, far)
+    write_hots(far1, D0, True, 0, at_rows, at_lanes, at_segments)
+
+
+def prepare_far_kernel(far2, *refs):
+    at_rows, at_lanes, at_segments, temp2, temp1, kx, ky, kzp, kzm, keep, temp0, load, cond = refs[FIELDS - 1 :]
+    near, far = validity()
+    coefs = (kx, ky, kzp, kzm, keep)
     place(far2, 8, False, far, temp0, cond, load)
-    coefficients(cond, *coefs, 5, 2)
-    advance(temp0, temp1, 5, 8, coefs, load, near, far)
+    coefficients(cond, *coefs, 7, 1)
+    advance(temp0, temp1, 7, 8, coefs, load, near, far)
     advance(temp1, temp2, 6, 7, coefs, load, near, far)
-    write_hots(far1, D0, True, 0, at_rows, at_lanes, at_segments)
-    write_hots(far2, D0, False, 1, at_rows, at_lanes, at_segments)
+    write_hots(far2, D0, False, 0, at_rows, at_lanes, at_segments)
 
 
 def prepare_near_kernel(near2, far_segments, at_segments):
@@ -331,7 +339,8 @@
 
 
 def backward_kernel(
-    near2, near1, own_rows, own_lanes, own_segments, far_rows, far_lanes, far_segments, near2_segments,
+    near2, near1, own_rows, own_lanes, own_segments, next_rows, next_lanes, next_segments,
+    far_rows, far_lanes, far_segments, near2_segments,
     sums, temp0, temp1, temp2, temp3, cond, kx, ky, kzp, kzm, keep, grad, seg,
     costate4, costate3, costate2, costate1, acc, weights, near_rows, near_lanes, near_segments,
 ):
@@ -345,9 +354,10 @@
     write_hots(near2, NEAR_D0, False, 0, near_rows, near_lanes, None)
     near_segments[0] = near2_segments[0]
     write_hots(near1, D0, True, 1, near_rows, near_lanes, near_segments)
+    beside = (next_rows, next_lanes, next_segments)
     own, fars = (own_rows, own_lanes, own_segments), (far_rows, far_lanes, far_segments)
     nears = (near_rows, near_lanes, near_segments)
-    places = ((nears, 0, near), (nears, 1, near), (own, 0, 1.0), (fars, 0, 1.0), (fars, 1, far))
+    places = ((nears, 0, near), (nears, 1, near), (own, 0, 1.0), (beside, 0, 1.0), (fars, 0, far))
     for j, ((at_rows, at_lanes, at_segments), n, valid) in enumerate(places):
         source = jnp.dot(stack, at_segments[n], preferred_element_type=f32)
         source = jnp.sum(source, axis=0, keepdims=True) * valid
@@ -449,7 +459,6 @@
     swap = [(s, s ^ 1) for s in range(grid)]
     far2 = lax.ppermute(pack, "grid", to_far)
     far1 = lax.ppermute(pack, "grid", swap)
-    near2 = lax.ppermute(pack_near, "grid", to_near)
 
     def hots(slabs):
         return (
@@ -473,13 +482,16 @@
             name=name,
         )(*operands, *fields)
 
-    results = stage(prepare_own_kernel, (*hots(1), *[field_shape] * 3), "prepare_own", pack)
+    results = stage(prepare_own_kernel, (*hots(1), *[field_shape] * 3), "prepare_own", pack, cost=1000)
     own_hots, fields = results[:3], results[3:]
-    far2, own_hots = lax.optimization_barrier((far2, own_hots))
+    results = stage(
+        prepare_chip_kernel, (*hots(1), *[field_shape] * 6), "prepare_chip", far1, fields=fields, cost=1000
+    )
+    next_hots, fields = results[:3], results[3:]
+    pack_near, next_hots = lax.optimization_barrier((pack_near, next_hots))
+    near2 = lax.ppermute(pack_near, "grid", to_near)
     near1 = lax.ppermute(far2, "grid", swap)
-    results = stage(
-        prepare_far_kernel, (*hots(2), *[field_shape] * 7), "prepare_far", far1, far2, fields=fields
-    )
+    results = stage(prepare_far_kernel, (*hots(1), field_shape), "prepare_far", far2, fields=fields)
     far_hots, fields = results[:3], results[3:]
     near_hots = stage(prepare_near_kernel, hots(1)[2:], "prepare_near", near2, far_hots[2])
     near2, near_hots, far_hots = lax.optimization_barrier((near2, near_hots, far_hots))
@@ -495,7 +507,7 @@
             pltpu.VMEM((tests, 2, share, NZ), f32),
             jax.ShapeDtypeStruct(measured.shape, f32),
         ),
-        in_specs=[vmem] * 20,
+        in_specs=[vmem] * 23,
         out_specs=(vmem, vmem),
         scratch_shapes=[
             *[pltpu.VMEM(field(EXT), f32)] * STEPS,
@@ -505,7 +517,7 @@
         ],
         compiler_params=params,
         name="backward",
-    )(near2, near1, *own_hots, *far_hots, *near_hots, sums, temp0, temp1, temp2, temp3, cond, *coefs)
+    )(near2, near1, *own_hots, *next_hots, *far_hots, *near_hots, sums, temp0, temp1, temp2, temp3, cond, *coefs)
     grad = lax.all_to_all(grad, "tests", split_axis=0, concat_axis=0, tiled=True)
     return jnp.sum(grad, axis=0), seg
 

time: 72.5 us -> 75.2 us (1.037)
  waiting for transfers between devices: 8.68 us -> 11.6 us
    ppermute x1, waiting for transfers between devices: 8.67 us -> 10.8 us  [local(): far2 = lax.ppermute(pack, 'grid', to_far)]
    pallas_call x4 -> x5, Pallas kernels: 4.75 us -> 4.5 us  [stage(): pl.pallas_call(kernel, out_shape=shapes, in_specs=[vmem] * (len(operands)...]
  transfers between devices with their start and end apart: 4 -> 4, of which waited for: 1 -> 2; matrix products, arithmetic and copies ran while one was open for 0% -> 0% of each run, Pallas kernels for 3% -> 3%
where the time goes in v8:
time: 75.2 us; the launch traced here: 74.9 us
  blocking collectives  37.4 us (50%)
  starting transfers between devices  13.5 us (18%)
  waiting for transfers between devices  11.6 us (15%)
  Pallas kernels  11 us (15%)
    all_to_all x1, blocking collectives, local(): lax.all_to_all(grad, 'tests', split_axis=0, concat_axis=0, tiled=True)  25.8 us
    all_to_all x1, blocking collectives, local(): sums = lax.all_to_all(sums, 'grid', split_axis=0, concat_axis=0, tiled=True)  11.6 us
    ppermute x1, waiting for transfers between devices, local(): far2 = lax.ppermute(pack, 'grid', to_far)  10.8 us
    ppermute x1, starting transfers between devices, local(): far2 = lax.ppermute(pack, 'grid', to_far)  7.73 us
    pallas_call x1, Pallas kernels, local(): pl.pallas_call(backward_kernel, out_shape=(pltpu.VMEM((tests, 2, share, N...  5.11 us
    pallas_call x5, Pallas kernels, stage(): pl.pallas_call(kernel, out_shape=shapes, in_specs=[vmem] * (len(operands)...  4.5 us
    ppermute x1, starting transfers between devices, local(): far1 = lax.ppermute(pack, 'grid', swap)  1.92 us
    ppermute x1, starting transfers between devices, local(): near2 = lax.ppermute(pack_near, 'grid', to_near)  1.92 us
  transfers between devices with their start and end apart: 4, of which 2 were waited for; matrix products, arithmetic and copies ran while one was open for 0% of the time, Pallas kernels for 3%

profile of v8, /device:TPU:8, one launch (start us, length us, event | category | flops | bytes accessed | tf_op | source)
XLA Modules:
  0.0 74.9 jit_solution(3180362076820462397)
XLA Ops:
  0.6 1.3 %pack.1.full.own = f32[792,128]{1,0:T(8,128)S(1)} custom-call(f32[2,128,128]{2,1,0:T(8,128)} %log_cond.1, f32[1,2,128,128]{3,2,1,0:T(8,128)} %opening.1, f32[1,2,128,128]{3,2,1,0:T(8,128)} %heat.1, s32[8,256]{1,0:T(8,128)} %bitcast.8, s32[1,256]{1,0:T(1,128)} %bitcast.9, f32[1,4]{1,0:T(1,128)} %measured.1), custom_call_target="tpu_custom_call" | custom-call | tf_op jit(solution)/shard_map/pack/pallas_call | solution.py:434
  1.9 1.9 %collective-permute-start = (f32[792,128]{1,0:T(8,128)S(1)}, f32[792,128]{1,0:T(8,128)S(1)}, u32[]{:S(2)}, u32[]{:S(2)}) collective-permute-start(f32[792,128]{1,0:T(8,128)S(1)} %pack.1.full.own), channel_id=1, source_target_pairs={{0,1},{1,0},{2,3},{3,2},{4,5},{5,4},{6,7},{7,6},{8,9},{9,8},{10,11... | collective-permute-start | bytes 1216520 | tf_op jit(solution)/shard_map/ppermute | solution.py:461
  3.9 7.7 %collective-permute-start.2 = (f32[792,128]{1,0:T(8,128)S(1)}, f32[792,128]{1,0:T(8,128)S(1)}, u32[]{:S(2)}, u32[]{:S(2)}) collective-permute-start(f32[792,128]{1,0:T(8,128)S(1)} %pack.1.full.own), channel_id=1, source_target_pairs={{2,0},{4,2},{6,4},{8,6},{10,8},{12,10},{14,12},{16,14},{18,16},{20... | collective-permute-start | bytes 1216520 | tf_op jit(solution)/shard_map/ppermute | solution.py:460
  11.6 0.3 prepare_own.1
  11.9 0.1 pack_near.1
  12.1 0.0 collective-permute-done.far1
  12.1 0.8 %prepare_chip.1 = (bf16[1,256,2048]{2,1,0:T(8,128)(2,1)S(1)}, bf16[1,128,2048]{2,1,0:T(8,128)(2,1)S(1)}, bf16[1,128,256]{2,1,0:T(8,128)(2,1)S(1)}, f32[10,128,12...) custom-call(f32[792,128]{1,0:T(8,128)S(1)} %collective-permute-done., ...), custom_call_target="tpu_custom_call", output_to_operand_aliasing={{9}: (1, {}), {10}: (2, {}), {11}: (3, {})} | custom-call | flops 1000 | bytes 4000000 | tf_op jit(solution)/shard_map/prepare_chip/pallas_call | solution.py:474
  12.9 1.9 %collective-permute-start.1 = (f32[536,128]{1,0:T(8,128)S(1)}, f32[536,128]{1,0:T(8,128)S(1)}, u32[]{:S(2)}, u32[]{:S(2)}) collective-permute-start(f32[536,128]{1,0:T(8,128)S(1)} %pack_near.1), channel_id=1, source_target_pairs={{0,2},{2,4},{4,6},{6,8},{8,10},{10,12},{12,14},{14,16},{16,18},{18... | collective-permute-start | bytes 823304 | tf_op jit(solution)/shard_map/ppermute | solution.py:492
  14.8 10.8 %collective-permute-done.2.far2 = f32[792,128]{1,0:T(8,128)S(1)} collective-permute-done((f32[792,128]{1,0:T(8,128)S(1)}, f32[792,128]{1,0:T(8,128)S(1)}, u32[]{:S(2)}, u32[]{:S(2)}) %collective-permute-start.2) | collective-permute-done | bytes 405536 | tf_op jit(solution)/shard_map/ppermute | solution.py:460
  25.7 1.9 %collective-permute-start.3 = (f32[792,128]{1,0:T(8,128)S(1)}, f32[792,128]{1,0:T(8,128)S(1)}, u32[]{:S(2)}, u32[]{:S(2)}) collective-permute-start(f32[792,128]{1,0:T(8,128)S(1)} %collective-permute-done.2.far2), channel_id=1, source_target_pairs={{0,1},{1,0},{2,3},{3,2},{4,5},{5,4},{6,7},{7,6},{8,9},{9,8},{10,11... | collective-permute-start | bytes 1216520 | tf_op jit(solution)/shard_map/ppermute | solution.py:493
  27.6 0.9 %prepare_far.1 = (bf16[1,256,2048]{2,1,0:T(8,128)(2,1)S(1)}, bf16[1,128,2048]{2,1,0:T(8,128)(2,1)S(1)}, bf16[1,128,256]{2,1,0:T(8,128)(2,1)S(1)}, f32[10,128,128...) custom-call(f32[792,128]{1,0:T(8,128)S(1)} %collective-permute-done., ...), custom_call_target="tpu_custom_call", output_to_operand_aliasing={{4}: (1, {}), {5}: (2, {}), {6}: (3, {}), {7}: (4, {}), {8}... | custom-call | flops 2000000000 | bytes 4000000 | tf_op jit(solution)/shard_map/prepare_far/pallas_call | solution.py:474
  28.5 0.0 collective-permute-done.1.near2
  28.5 0.7 collective-permute-done.3.near1
  29.3 2.4 %forward.1 = (f32[10,128,128]{2,1,0:T(8,128)S(1)}, f32[10,128,128]{2,1,0:T(8,128)}, f32[32,128]{1,0:T(8,128)S(1)}, f32[10,128,128]{2,1,0:T(8,128)S(1)}, f32[10,1...) custom-call(f32[536,128]{1,0:T(8,128)S(1)} %collective-permute-done., ...), custom_call_target="tpu_custom_call", output_to_operand_aliasing={{3}: (6, {}), {4}: (7, {}), {5}: (8, {}), {6}: (9, {}), {7}... | custom-call | flops 2000000000 | bytes 4000000 | tf_op jit(solution)/shard_map/forward/pallas_call | solution.py:474
  31.7 11.6 %all_to_all.16 = f32[32,1,128]{2,1,0:T(1,128)S(1)} all-to-all(f32[32,1,128]{2,1,0:T(1,128)S(1)} %bitcast.7), channel_id=1, replica_groups=mesh['tests'=16,'grid'=32] {'grid'}, dimensions={0} | all-to-all | bytes 32768 | tf_op jit(solution)/shard_map/all_to_all | solution.py:502
  43.4 5.1 %backward.1 = (f32[16,2,8,128]{3,2,1,0:T(8,128)S(1)}, f32[1,4]{1,0:T(1,128)}) custom-call(f32[536,128]{1,0:T(8,128)S(1)} %collective-permute-done.1.near2, f32[792,128]{1,0:T(8,128)S(1)} %collective-permute-done.3.near1, bf16[1,256,2048]{2,1,0:T(8,128)(2,1)S(1)} %get-tuple-element.75.at_rows.own_rows, ...), custom_call_target="tpu_custom_call" | custom-call | tf_op jit(solution)/shard_map/backward/pallas_call | solution.py:504
  48.5 25.8 %all_to_all.17 = f32[16,2,8,128]{3,2,1,0:T(8,128)S(1)} all-to-all(f32[16,2,8,128]{3,2,1,0:T(8,128)S(1)} %get-tuple-element.106), channel_id=1, replica_groups=mesh['tests'=16,'grid'=32] {'tests'}, dimensions={0} | all-to-all | bytes 262144 | tf_op jit(solution)/shard_map/all_to_all | solution.py:521
  74.3 0.6 reduce_sum.9
  (1 shorter events, 0.0 us)
Async XLA Ops:
  1.9 10.1 %collective-permute-start = (f32[792,128]{1,0:T(8,128)S(1)}, f32[792,128]{1,0:T(8,128)S(1)}, u32[]{:S(2)}, u32[]{:S(2)}) collective-permute-start(f32[792,128]{1,0:T(8,128)S(1)} %pack.1.full.own), channel_id=1, source_target_pairs={{0,1},{1,0},{2,3},{3,2},{4,5},{5,4},{6,7},{7,6},{8,9},{9,8},{10,11... | collective-permute-start | bytes 1216520 | tf_op jit(solution)/shard_map/ppermute | solution.py:461
  3.9 21.8 %collective-permute-start.2 = (f32[792,128]{1,0:T(8,128)S(1)}, f32[792,128]{1,0:T(8,128)S(1)}, u32[]{:S(2)}, u32[]{:S(2)}) collective-permute-start(f32[792,128]{1,0:T(8,128)S(1)} %pack.1.full.own), channel_id=1, source_target_pairs={{2,0},{4,2},{6,4},{8,6},{10,8},{12,10},{14,12},{16,14},{18,16},{20... | collective-permute-start | bytes 1216520 | tf_op jit(solution)/shard_map/ppermute | solution.py:460
  12.9 15.6 %collective-permute-start.1 = (f32[536,128]{1,0:T(8,128)S(1)}, f32[536,128]{1,0:T(8,128)S(1)}, u32[]{:S(2)}, u32[]{:S(2)}) collective-permute-start(f32[536,128]{1,0:T(8,128)S(1)} %pack_near.1), channel_id=1, source_target_pairs={{0,2},{2,4},{4,6},{6,8},{8,10},{10,12},{12,14},{14,16},{16,18},{18... | collective-permute-start | bytes 823304 | tf_op jit(solution)/shard_map/ppermute | solution.py:492
  25.7 3.6 %collective-permute-start.3 = (f32[792,128]{1,0:T(8,128)S(1)}, f32[792,128]{1,0:T(8,128)S(1)}, u32[]{:S(2)}, u32[]{:S(2)}) collective-permute-start(f32[792,128]{1,0:T(8,128)S(1)} %collective-permute-done.2.far2), channel_id=1, source_target_pairs={{0,1},{1,0},{2,3},{3,2},{4,5},{5,4},{6,7},{7,6},{8,9},{9,8},{10,11... | collective-permute-start | bytes 1216520 | tf_op jit(solution)/shard_map/ppermute | solution.py:493

commit v9 on v7

--- a/solution.py
+++ b/solution.py
@@ -357,9 +357,9 @@
             weights[j, 0:NZ, at] = at_lanes[n, :, at] * upper
             weights[j, NZ : 2 * NZ, at] = at_lanes[n, :, at] * lower
         out = lax.dot_general(
-            at_rows[n], weights[j], (((1,), (1,)), ((), ())), preferred_element_type=f32
+            weights[j], at_rows[n], (((1,), (1,)), ((), ())), preferred_element_type=f32
         )
-        out = out[:, :NZ] + out[:, NZ:]
+        out = (out[:NZ] + out[NZ:]).T
         costate4[2 * j] = out[:NY]
         costate4[2 * j + 1] = out[NY:]
 
@@ -449,7 +449,6 @@
     swap = [(s, s ^ 1) for s in range(grid)]
     far2 = lax.ppermute(pack, "grid", to_far)
     far1 = lax.ppermute(pack, "grid", swap)
-    near2 = lax.ppermute(pack_near, "grid", to_near)
 
     def hots(slabs):
         return (
@@ -475,6 +474,8 @@
 
     results = stage(prepare_own_kernel, (*hots(1), *[field_shape] * 3), "prepare_own", pack)
     own_hots, fields = results[:3], results[3:]
+    pack_near, own_hots = lax.optimization_barrier((pack_near, own_hots))
+    near2 = lax.ppermute(pack_near, "grid", to_near)
     far2, own_hots = lax.optimization_barrier((far2, own_hots))
     near1 = lax.ppermute(far2, "grid", swap)
     results = stage(

time: 72.5 us -> 72 us (level)
  no operation moved by 1% of the time
where the time goes in v9:
time: 72 us; the launch traced here: 71.7 us
  blocking collectives  37.2 us (52%)
  starting transfers between devices  13.5 us (19%)
  Pallas kernels  11.2 us (16%)
  waiting for transfers between devices  8.52 us (12%)
  between operations  0.72 us (1%)
    all_to_all x1, blocking collectives, local(): lax.all_to_all(grad, 'tests', split_axis=0, concat_axis=0, tiled=True)  25.5 us
    all_to_all x1, blocking collectives, local(): sums = lax.all_to_all(sums, 'grid', split_axis=0, concat_axis=0, tiled=True)  11.7 us
    ppermute x1, waiting for transfers between devices, local(): far2 = lax.ppermute(pack, 'grid', to_far)  8.51 us
    ppermute x1, starting transfers between devices, local(): far2 = lax.ppermute(pack, 'grid', to_far)  7.73 us
    pallas_call x1, Pallas kernels, local(): pl.pallas_call(backward_kernel, out_shape=(pltpu.VMEM((tests, 2, share, N...  5.03 us
    pallas_call x4, Pallas kernels, stage(): pl.pallas_call(kernel, out_shape=shapes, in_specs=[vmem] * (len(operands)...  4.75 us
    ppermute x1, starting transfers between devices, local(): far1 = lax.ppermute(pack, 'grid', swap)  1.92 us
    ppermute x1, starting transfers between devices, local(): near2 = lax.ppermute(pack_near, 'grid', to_near)  1.92 us
  transfers between devices with their start and end apart: 4, of which 1 were waited for; matrix products, arithmetic and copies ran while one was open for 0% of the time, Pallas kernels for 3%

profile of v9, /device:TPU:8, one launch (start us, length us, event | category | flops | bytes accessed | tf_op | source)
XLA Modules:
  0.0 71.7 jit_solution(11455205833724662153)
XLA Ops:
  0.6 1.3 %pack.1.full.own = f32[792,128]{1,0:T(8,128)S(1)} custom-call(f32[2,128,128]{2,1,0:T(8,128)} %log_cond.1, f32[1,2,128,128]{3,2,1,0:T(8,128)} %opening.1, f32[1,2,128,128]{3,2,1,0:T(8,128)} %heat.1, s32[8,256]{1,0:T(8,128)} %bitcast.8, s32[1,256]{1,0:T(1,128)} %bitcast.9, f32[1,4]{1,0:T(1,128)} %measured.1), custom_call_target="tpu_custom_call" | custom-call | tf_op jit(solution)/shard_map/pack/pallas_call | solution.py:424
  1.9 7.7 %collective-permute-start.2 = (f32[792,128]{1,0:T(8,128)S(1)}, f32[792,128]{1,0:T(8,128)S(1)}, u32[]{:S(2)}, u32[]{:S(2)}) collective-permute-start(f32[792,128]{1,0:T(8,128)S(1)} %pack.1.full.own), channel_id=1, source_target_pairs={{2,0},{4,2},{6,4},{8,6},{10,8},{12,10},{14,12},{16,14},{18,16},{20... | collective-permute-start | bytes 1216520 | tf_op jit(solution)/shard_map/ppermute | solution.py:450
  9.7 1.9 %collective-permute-start.1 = (f32[792,128]{1,0:T(8,128)S(1)}, f32[792,128]{1,0:T(8,128)S(1)}, u32[]{:S(2)}, u32[]{:S(2)}) collective-permute-start(f32[792,128]{1,0:T(8,128)S(1)} %pack.1.full.own), channel_id=1, source_target_pairs={{0,1},{1,0},{2,3},{3,2},{4,5},{5,4},{6,7},{7,6},{8,9},{9,8},{10,11... | collective-permute-start | bytes 1216520 | tf_op jit(solution)/shard_map/ppermute | solution.py:451
  11.6 0.1 pack_near.1
  11.7 0.3 prepare_own.1
  12.1 1.9 %collective-permute-start = (f32[536,128]{1,0:T(8,128)S(1)}, f32[536,128]{1,0:T(8,128)S(1)}, u32[]{:S(2)}, u32[]{:S(2)}) collective-permute-start(f32[536,128]{1,0:T(8,128)S(1)} %pack_near.1), channel_id=1, source_target_pairs={{0,2},{2,4},{4,6},{6,8},{8,10},{10,12},{12,14},{14,16},{16,18},{18... | collective-permute-start | bytes 823304 | tf_op jit(solution)/shard_map/ppermute | solution.py:478
  14.0 8.5 %collective-permute-done.2.far2 = f32[792,128]{1,0:T(8,128)S(1)} collective-permute-done((f32[792,128]{1,0:T(8,128)S(1)}, f32[792,128]{1,0:T(8,128)S(1)}, u32[]{:S(2)}, u32[]{:S(2)}) %collective-permute-start.2) | collective-permute-done | bytes 405536 | tf_op jit(solution)/shard_map/ppermute | solution.py:450
  22.5 1.9 %collective-permute-start.3 = (f32[792,128]{1,0:T(8,128)S(1)}, f32[792,128]{1,0:T(8,128)S(1)}, u32[]{:S(2)}, u32[]{:S(2)}) collective-permute-start(f32[792,128]{1,0:T(8,128)S(1)} %collective-permute-done.2.far2), channel_id=1, source_target_pairs={{0,1},{1,0},{2,3},{3,2},{4,5},{5,4},{6,7},{7,6},{8,9},{9,8},{10,11... | collective-permute-start | bytes 1216520 | tf_op jit(solution)/shard_map/ppermute | solution.py:480
  24.4 0.0 collective-permute-done.1.far1
  24.4 1.9 %prepare_far.1 = (bf16[2,256,2048]{2,1,0:T(8,128)(2,1)S(1)}, bf16[2,128,2048]{2,1,0:T(8,128)(2,1)S(1)}, bf16[2,128,256]{2,1,0:T(8,128)(2,1)S(1)}, f32[10,128,128...) custom-call(f32[792,128]{1,0:T(8,128)S(1)} %collective-permute-done., ...), custom_call_target="tpu_custom_call", output_to_operand_aliasing={{10}: (2, {}), {11}: (3, {}), {12}: (4, {})} | custom-call | flops 2000000000 | bytes 4000000 | tf_op jit(solution)/shard_map/prepare_far/pallas_call | solution.py:464
  26.4 0.0 collective-permute-done.near2
  26.4 0.0 collective-permute-done.3.near1
  26.4 2.5 %forward.1 = (f32[10,128,128]{2,1,0:T(8,128)S(1)}, f32[10,128,128]{2,1,0:T(8,128)}, f32[32,128]{1,0:T(8,128)S(1)}, f32[10,128,128]{2,1,0:T(8,128)S(1)}, f32[10,1...) custom-call(f32[536,128]{1,0:T(8,128)S(1)} %collective-permute-done., ...), custom_call_target="tpu_custom_call", output_to_operand_aliasing={{3}: (6, {}), {4}: (7, {}), {5}: (8, {}), {6}: (9, {}), {7}... | custom-call | flops 2000000000 | bytes 4000000 | tf_op jit(solution)/shard_map/forward/pallas_call | solution.py:464
  28.9 11.7 %all_to_all.16 = f32[32,1,128]{2,1,0:T(1,128)S(1)} all-to-all(f32[32,1,128]{2,1,0:T(1,128)S(1)} %bitcast.7), channel_id=1, replica_groups=mesh['tests'=16,'grid'=32] {'grid'}, dimensions={0} | all-to-all | bytes 32768 | tf_op jit(solution)/shard_map/all_to_all | solution.py:491
  40.6 5.0 %backward.1 = (f32[16,2,8,128]{3,2,1,0:T(8,128)S(1)}, f32[1,4]{1,0:T(1,128)}) custom-call(f32[536,128]{1,0:T(8,128)S(1)} %collective-permute-done.near2, f32[792,128]{1,0:T(8,128)S(1)} %collective-permute-done.3.near1, bf16[1,256,2048]{2,1,0:T(8,128)(2,1)S(1)} %get-tuple-element.62.at_rows.own_rows, ...), custom_call_target="tpu_custom_call" | custom-call | tf_op jit(solution)/shard_map/backward/pallas_call | solution.py:493
  45.6 25.5 %all_to_all.17 = f32[16,2,8,128]{3,2,1,0:T(8,128)S(1)} all-to-all(f32[16,2,8,128]{3,2,1,0:T(8,128)S(1)} %get-tuple-element.90), channel_id=1, replica_groups=mesh['tests'=16,'grid'=32] {'tests'}, dimensions={0} | all-to-all | bytes 262144 | tf_op jit(solution)/shard_map/all_to_all | solution.py:510
  71.1 0.6 reduce_sum.9
  (1 shorter events, 0.0 us)
Async XLA Ops:
  1.9 20.6 %collective-permute-start.2 = (f32[792,128]{1,0:T(8,128)S(1)}, f32[792,128]{1,0:T(8,128)S(1)}, u32[]{:S(2)}, u32[]{:S(2)}) collective-permute-start(f32[792,128]{1,0:T(8,128)S(1)} %pack.1.full.own), channel_id=1, source_target_pairs={{2,0},{4,2},{6,4},{8,6},{10,8},{12,10},{14,12},{16,14},{18,16},{20... | collective-permute-start | bytes 1216520 | tf_op jit(solution)/shard_map/ppermute | solution.py:450
  9.7 14.8 %collective-permute-start.1 = (f32[792,128]{1,0:T(8,128)S(1)}, f32[792,128]{1,0:T(8,128)S(1)}, u32[]{:S(2)}, u32[]{:S(2)}) collective-permute-start(f32[792,128]{1,0:T(8,128)S(1)} %pack.1.full.own), channel_id=1, source_target_pairs={{0,1},{1,0},{2,3},{3,2},{4,5},{5,4},{6,7},{7,6},{8,9},{9,8},{10,11... | collective-permute-start | bytes 1216520 | tf_op jit(solution)/shard_map/ppermute | solution.py:451
  12.1 14.3 %collective-permute-start = (f32[536,128]{1,0:T(8,128)S(1)}, f32[536,128]{1,0:T(8,128)S(1)}, u32[]{:S(2)}, u32[]{:S(2)}) collective-permute-start(f32[536,128]{1,0:T(8,128)S(1)} %pack_near.1), channel_id=1, source_target_pairs={{0,2},{2,4},{4,6},{6,8},{8,10},{10,12},{12,14},{14,16},{16,18},{18... | collective-permute-start | bytes 823304 | tf_op jit(solution)/shard_map/ppermute | solution.py:478
  22.5 3.9 %collective-permute-start.3 = (f32[792,128]{1,0:T(8,128)S(1)}, f32[792,128]{1,0:T(8,128)S(1)}, u32[]{:S(2)}, u32[]{:S(2)}) collective-permute-start(f32[792,128]{1,0:T(8,128)S(1)} %collective-permute-done.2.far2), channel_id=1, source_target_pairs={{0,1},{1,0},{2,3},{3,2},{4,5},{5,4},{6,7},{7,6},{8,9},{9,8},{10,11... | collective-permute-start | bytes 1216520 | tf_op jit(solution)/shard_map/ppermute | solution.py:480

commit v10 on v9

--- a/solution.py
+++ b/solution.py
@@ -286,8 +286,7 @@
     coefficients(cond, *coefs, 5, 2)
     advance(temp0, temp1, 5, 8, coefs, load, near, far)
     advance(temp1, temp2, 6, 7, coefs, load, near, far)
-    write_hots(far1, D0, True, 0, at_rows, at_lanes, at_segments)
-    write_hots(far2, D0, False, 1, at_rows, at_lanes, at_segments)
+    write_hots(far2, D0, False, 0, at_rows, at_lanes, at_segments)
 
 
 def prepare_near_kernel(near2, far_segments, at_segments):
@@ -331,7 +330,7 @@
 
 
 def backward_kernel(
-    near2, near1, own_rows, own_lanes, own_segments, far_rows, far_lanes, far_segments, near2_segments,
+    near2, near1, far1, own_rows, own_lanes, own_segments, far_rows, far_lanes, far_segments, near2_segments,
     sums, temp0, temp1, temp2, temp3, cond, kx, ky, kzp, kzm, keep, grad, seg,
     costate4, costate3, costate2, costate1, acc, weights, near_rows, near_lanes, near_segments,
 ):
@@ -345,9 +344,10 @@
     write_hots(near2, NEAR_D0, False, 0, near_rows, near_lanes, None)
     near_segments[0] = near2_segments[0]
     write_hots(near1, D0, True, 1, near_rows, near_lanes, near_segments)
+    write_hots(far1, D0, True, 2, near_rows, near_lanes, near_segments)
     own, fars = (own_rows, own_lanes, own_segments), (far_rows, far_lanes, far_segments)
     nears = (near_rows, near_lanes, near_segments)
-    places = ((nears, 0, near), (nears, 1, near), (own, 0, 1.0), (fars, 0, 1.0), (fars, 1, far))
+    places = ((nears, 0, near), (nears, 1, near), (own, 0, 1.0), (nears, 2, 1.0), (fars, 0, far))
     for j, ((at_rows, at_lanes, at_segments), n, valid) in enumerate(places):
         source = jnp.dot(stack, at_segments[n], preferred_element_type=f32)
         source = jnp.sum(source, axis=0, keepdims=True) * valid
@@ -479,7 +479,7 @@
     far2, own_hots = lax.optimization_barrier((far2, own_hots))
     near1 = lax.ppermute(far2, "grid", swap)
     results = stage(
-        prepare_far_kernel, (*hots(2), *[field_shape] * 7), "prepare_far", far1, far2, fields=fields
+        prepare_far_kernel, (*hots(1), *[field_shape] * 7), "prepare_far", far1, far2, fields=fields
     )
     far_hots, fields = results[:3], results[3:]
     near_hots = stage(prepare_near_kernel, hots(1)[2:], "prepare_near", near2, far_hots[2])
@@ -496,17 +496,17 @@
             pltpu.VMEM((tests, 2, share, NZ), f32),
             jax.ShapeDtypeStruct(measured.shape, f32),
         ),
-        in_specs=[vmem] * 20,
+        in_specs=[vmem] * 21,
         out_specs=(vmem, vmem),
         scratch_shapes=[
             *[pltpu.VMEM(field(EXT), f32)] * STEPS,
             pltpu.VMEM((NY, NZ), f32),
             pltpu.VMEM((5, CELLS, 2048), bf16),
-            *hots(2),
+            *hots(3),
         ],
         compiler_params=params,
         name="backward",
-    )(near2, near1, *own_hots, *far_hots, *near_hots, sums, temp0, temp1, temp2, temp3, cond, *coefs)
+    )(near2, near1, far1, *own_hots, *far_hots, *near_hots, sums, temp0, temp1, temp2, temp3, cond, *coefs)
     grad = lax.all_to_all(grad, "tests", split_axis=0, concat_axis=0, tiled=True)
     return jnp.sum(grad, axis=0), seg
 

time: 72 us -> 71.7 us (level)
  transfers between devices with their start and end apart: 4 -> 4, of which waited for: 1 -> 2; matrix products, arithmetic and copies ran while one was open for 0% -> 0% of each run, Pallas kernels for 3% -> 2%
where the time goes in v10:
time: 71.7 us; the launch traced here: 71.4 us
  blocking collectives  37.1 us (52%)
  starting transfers between devices  13.5 us (19%)
  Pallas kernels  10.7 us (15%)
  waiting for transfers between devices  8.86 us (12%)
  between operations  0.72 us (1%)
    all_to_all x1, blocking collectives, local(): lax.all_to_all(grad, 'tests', split_axis=0, concat_axis=0, tiled=True)  25.4 us
    all_to_all x1, blocking collectives, local(): sums = lax.all_to_all(sums, 'grid', split_axis=0, concat_axis=0, tiled=True)  11.7 us
    ppermute x1, waiting for transfers between devices, local(): far2 = lax.ppermute(pack, 'grid', to_far)  8.51 us
    ppermute x1, starting transfers between devices, local(): far2 = lax.ppermute(pack, 'grid', to_far)  7.73 us
    pallas_call x1, Pallas kernels, local(): pl.pallas_call(backward_kernel, out_shape=(pltpu.VMEM((tests, 2, share, N...  5.16 us
    pallas_call x4, Pallas kernels, stage(): pl.pallas_call(kernel, out_shape=shapes, in_specs=[vmem] * (len(operands)...  4.08 us
    ppermute x1, starting transfers between devices, local(): far1 = lax.ppermute(pack, 'grid', swap)  1.92 us
    ppermute x1, starting transfers between devices, local(): near2 = lax.ppermute(pack_near, 'grid', to_near)  1.92 us
  transfers between devices with their start and end apart: 4, of which 2 were waited for; matrix products, arithmetic and copies ran while one was open for 0% of the time, Pallas kernels for 2%

profile of v10, /device:TPU:8, one launch (start us, length us, event | category | flops | bytes accessed | tf_op | source)
XLA Modules:
  0.0 71.4 jit_solution(17972541435378049909)
XLA Ops:
  0.6 1.3 %pack.1.full.own = f32[792,128]{1,0:T(8,128)S(1)} custom-call(f32[2,128,128]{2,1,0:T(8,128)} %log_cond.1, f32[1,2,128,128]{3,2,1,0:T(8,128)} %opening.1, f32[1,2,128,128]{3,2,1,0:T(8,128)} %heat.1, s32[8,256]{1,0:T(8,128)} %bitcast.8, s32[1,256]{1,0:T(1,128)} %bitcast.9, f32[1,4]{1,0:T(1,128)} %measured.1), custom_call_target="tpu_custom_call" | custom-call | tf_op jit(solution)/shard_map/pack/pallas_call | solution.py:424
  1.9 7.7 %collective-permute-start.2 = (f32[792,128]{1,0:T(8,128)S(1)}, f32[792,128]{1,0:T(8,128)S(1)}, u32[]{:S(2)}, u32[]{:S(2)}) collective-permute-start(f32[792,128]{1,0:T(8,128)S(1)} %pack.1.full.own), channel_id=1, source_target_pairs={{2,0},{4,2},{6,4},{8,6},{10,8},{12,10},{14,12},{16,14},{18,16},{20... | collective-permute-start | bytes 1216520 | tf_op jit(solution)/shard_map/ppermute | solution.py:450
  9.7 1.9 %collective-permute-start.1 = (f32[792,128]{1,0:T(8,128)S(1)}, f32[792,128]{1,0:T(8,128)S(1)}, u32[]{:S(2)}, u32[]{:S(2)}) collective-permute-start(f32[792,128]{1,0:T(8,128)S(1)} %pack.1.full.own), channel_id=1, source_target_pairs={{0,1},{1,0},{2,3},{3,2},{4,5},{5,4},{6,7},{7,6},{8,9},{9,8},{10,11... | collective-permute-start | bytes 1216520 | tf_op jit(solution)/shard_map/ppermute | solution.py:451
  11.6 0.1 pack_near.1
  11.7 0.3 prepare_own.1
  12.1 1.9 %collective-permute-start = (f32[536,128]{1,0:T(8,128)S(1)}, f32[536,128]{1,0:T(8,128)S(1)}, u32[]{:S(2)}, u32[]{:S(2)}) collective-permute-start(f32[536,128]{1,0:T(8,128)S(1)} %pack_near.1), channel_id=1, source_target_pairs={{0,2},{2,4},{4,6},{6,8},{8,10},{10,12},{12,14},{14,16},{16,18},{18... | collective-permute-start | bytes 823304 | tf_op jit(solution)/shard_map/ppermute | solution.py:478
  14.0 8.5 %collective-permute-done.2.far2 = f32[792,128]{1,0:T(8,128)S(1)} collective-permute-done((f32[792,128]{1,0:T(8,128)S(1)}, f32[792,128]{1,0:T(8,128)S(1)}, u32[]{:S(2)}, u32[]{:S(2)}) %collective-permute-start.2) | collective-permute-done | bytes 405536 | tf_op jit(solution)/shard_map/ppermute | solution.py:450
  22.5 1.9 %collective-permute-start.3 = (f32[792,128]{1,0:T(8,128)S(1)}, f32[792,128]{1,0:T(8,128)S(1)}, u32[]{:S(2)}, u32[]{:S(2)}) collective-permute-start(f32[792,128]{1,0:T(8,128)S(1)} %collective-permute-done.2.far2), channel_id=1, source_target_pairs={{0,1},{1,0},{2,3},{3,2},{4,5},{5,4},{6,7},{7,6},{8,9},{9,8},{10,11... | collective-permute-start | bytes 1216520 | tf_op jit(solution)/shard_map/ppermute | solution.py:480
  24.4 0.0 collective-permute-done.1.far1
  24.4 1.3 %prepare_far.1 = (bf16[1,256,2048]{2,1,0:T(8,128)(2,1)S(1)}, bf16[1,128,2048]{2,1,0:T(8,128)(2,1)S(1)}, bf16[1,128,256]{2,1,0:T(8,128)(2,1)S(1)}, f32[10,128,128...) custom-call(f32[792,128]{1,0:T(8,128)S(1)} %collective-permute-done., ...), custom_call_target="tpu_custom_call", output_to_operand_aliasing={{10}: (2, {}), {11}: (3, {}), {12}: (4, {})} | custom-call | flops 2000000000 | bytes 4000000 | tf_op jit(solution)/shard_map/prepare_far/pallas_call | solution.py:464
  25.7 0.0 collective-permute-done.near2
  25.8 0.3 collective-permute-done.3.near1
  26.1 2.4 %forward.1 = (f32[10,128,128]{2,1,0:T(8,128)S(1)}, f32[10,128,128]{2,1,0:T(8,128)}, f32[32,128]{1,0:T(8,128)S(1)}, f32[10,128,128]{2,1,0:T(8,128)S(1)}, f32[10,1...) custom-call(f32[536,128]{1,0:T(8,128)S(1)} %collective-permute-done., ...), custom_call_target="tpu_custom_call", output_to_operand_aliasing={{3}: (6, {}), {4}: (7, {}), {5}: (8, {}), {6}: (9, {}), {7}... | custom-call | flops 2000000000 | bytes 4000000 | tf_op jit(solution)/shard_map/forward/pallas_call | solution.py:464
  28.6 11.7 %all_to_all.16 = f32[32,1,128]{2,1,0:T(1,128)S(1)} all-to-all(f32[32,1,128]{2,1,0:T(1,128)S(1)} %bitcast.7), channel_id=1, replica_groups=mesh['tests'=16,'grid'=32] {'grid'}, dimensions={0} | all-to-all | bytes 32768 | tf_op jit(solution)/shard_map/all_to_all | solution.py:491
  40.2 5.2 %backward.1 = (f32[16,2,8,128]{3,2,1,0:T(8,128)S(1)}, f32[1,4]{1,0:T(1,128)}) custom-call(f32[536,128]{1,0:T(8,128)S(1)} %collective-permute-done.near2, f32[792,128]{1,0:T(8,128)S(1)} %collective-permute-done.3.near1, f32[792,128]{1,0:T(8,128)S(1)} %collective-permute-done.1.far1, bf16[1,256,2048]{2,1,0:T(8,128)(2,1)S(1)} %get-tuple-element.62.at_rows.own_rows, ...), custom_call_target="tpu_custom_call" | custom-call | tf_op jit(solution)/shard_map/backward/pallas_call | solution.py:493
  45.4 25.4 %all_to_all.17 = f32[16,2,8,128]{3,2,1,0:T(8,128)S(1)} all-to-all(f32[16,2,8,128]{3,2,1,0:T(8,128)S(1)} %get-tuple-element.90), channel_id=1, replica_groups=mesh['tests'=16,'grid'=32] {'tests'}, dimensions={0} | all-to-all | bytes 262144 | tf_op jit(solution)/shard_map/all_to_all | solution.py:510
  70.8 0.6 reduce_sum.9
  (1 shorter events, 0.0 us)
Async XLA Ops:
  1.9 20.6 %collective-permute-start.2 = (f32[792,128]{1,0:T(8,128)S(1)}, f32[792,128]{1,0:T(8,128)S(1)}, u32[]{:S(2)}, u32[]{:S(2)}) collective-permute-start(f32[792,128]{1,0:T(8,128)S(1)} %pack.1.full.own), channel_id=1, source_target_pairs={{2,0},{4,2},{6,4},{8,6},{10,8},{12,10},{14,12},{16,14},{18,16},{20... | collective-permute-start | bytes 1216520 | tf_op jit(solution)/shard_map/ppermute | solution.py:450
  9.7 14.8 %collective-permute-start.1 = (f32[792,128]{1,0:T(8,128)S(1)}, f32[792,128]{1,0:T(8,128)S(1)}, u32[]{:S(2)}, u32[]{:S(2)}) collective-permute-start(f32[792,128]{1,0:T(8,128)S(1)} %pack.1.full.own), channel_id=1, source_target_pairs={{0,1},{1,0},{2,3},{3,2},{4,5},{5,4},{6,7},{7,6},{8,9},{9,8},{10,11... | collective-permute-start | bytes 1216520 | tf_op jit(solution)/shard_map/ppermute | solution.py:451
  12.1 13.7 %collective-permute-start = (f32[536,128]{1,0:T(8,128)S(1)}, f32[536,128]{1,0:T(8,128)S(1)}, u32[]{:S(2)}, u32[]{:S(2)}) collective-permute-start(f32[536,128]{1,0:T(8,128)S(1)} %pack_near.1), channel_id=1, source_target_pairs={{0,2},{2,4},{4,6},{6,8},{8,10},{10,12},{12,14},{14,16},{16,18},{18... | collective-permute-start | bytes 823304 | tf_op jit(solution)/shard_map/ppermute | solution.py:478
  22.5 3.6 %collective-permute-start.3 = (f32[792,128]{1,0:T(8,128)S(1)}, f32[792,128]{1,0:T(8,128)S(1)}, u32[]{:S(2)}, u32[]{:S(2)}) collective-permute-start(f32[792,128]{1,0:T(8,128)S(1)} %collective-permute-done.2.far2), channel_id=1, source_target_pairs={{0,1},{1,0},{2,3},{3,2},{4,5},{5,4},{6,7},{7,6},{8,9},{9,8},{10,11... | collective-permute-start | bytes 1216520 | tf_op jit(solution)/shard_map/ppermute | solution.py:480
